TPU v7x, 32 devices: a whole 2x2x4 slice. The times are simulated.
32 devices in a mesh: clip: 4 (over z), tile: 8 (over y, x, core).
Axes of the slice: x: 2, y: 2, z: 4, core: 2. Of those that a mesh axis runs over, the one named last changes fastest.
Arguments:
- tokens: bfloat16 [256, 16, 16, 1024], P('tile', 'clip'), may hold values from -6 to 6
- mask_bits: int32 [256, 16, 16], P('tile', 'clip'), may hold values from 0 to 1, as said below
- action_ids: int32 [16, 16], P('clip'), may hold values from 0 to 7
- vectors: float32 [8, 1024], replicated, as said below
- action_table: float32 [8, 1024], replicated, may hold values from -4 to 4
- w_space_qkv: bfloat16 [1024, 3072], replicated, may hold values from -0.1875 to 0.1875
- w_space_out: bfloat16 [1024, 1024], replicated, may hold values from -1.5 to 1.5
- w_time_qkv: bfloat16 [1024, 3072], replicated, may hold values from -0.1875 to 0.1875
- w_time_out: bfloat16 [1024, 1024], replicated, may hold values from -0.5 to 0.5
- w_up: bfloat16 [1024, 4096], replicated, may hold values from -0.1875 to 0.1875
- b_up: float32 [4096], replicated, may hold values from -3 to 3
- w_down: bfloat16 [4096, 1024], replicated, may hold values from -0.09375 to 0.09375
- cotangent: bfloat16 [256, 16, 16, 1024], P('tile', 'clip'), may hold values from -6 to 6
Outputs:
- result: bfloat16 [256, 16, 16, 1024], P('tile', 'clip')
- input_grad: bfloat16 [256, 16, 16, 1024], P('tile', 'clip')
- vectors_grad: float32 [8, 1024], replicated
- table_grad: float32 [8, 1024], replicated
- space_qkv_grad: float32 [1024, 3072], P(('clip', 'tile'))
- space_out_grad: float32 [1024, 1024], P(('clip', 'tile'))
- time_qkv_grad: float32 [1024, 3072], P(('clip', 'tile'))
- time_out_grad: float32 [1024, 1024], P(('clip', 'tile'))
- up_grad: float32 [1024, 4096], P(('clip', 'tile'))
- bias_up_grad: float32 [4096], replicated
- down_grad: float32 [4096, 1024], P(('clip', 'tile'))
Inputs may be any that keep to these rules, and one draw needn't show every extreme that they name: `mask_bits`: each clip draws a share between one half and one; each of its tokens is 1 with that probability. `vectors`: gains near one, shifts and biases of a few tenths, the mask embedding of order one.
All inputs are finite; a program needn't handle non-finite values.
Results may differ from a plain program's by a relative error of at most 0.017.
Values may be sent and summed in bfloat16 or wider, within the bound.
No kernel may reach another device: no remote copies, remote signals or barrier semaphores. Data moves between devices by JAX's collectives and lax.ppermute only.
A program may use at most 576 MiB of HBM per device.

v0:
```python
import jax
import jax.numpy as jnp
from jax import lax
from jax.experimental import pallas as pl
from jax.experimental.pallas import tpu as pltpu
from jax.sharding import PartitionSpec as P

HEADS = 16
HEAD_DIM = 64
PAIR = 2 * HEAD_DIM
EPSILON = 1e-05
NEGATIVE = -1e30
MASKED = 2.0**100
SEEN = 2.0**99
LOG2E = 1.4426950408889634
SCALE = HEAD_DIM**-0.5
F32 = jnp.float32
BF16 = jnp.bfloat16
VMEM_LIMIT = 60 * 1024 * 1024

NN = (((1,), (0,)), ((), ()))
NT = (((1,), (1,)), ((), ()))
TN = (((0,), (0,)), ((), ()))


def dot(left, right, form=NN):
    return lax.dot_general(left, right, form, preferred_element_type=F32)


def normalise(values):
    centred = values - jnp.mean(values, -1, keepdims=True)
    spread = lax.rsqrt(jnp.mean(centred * centred, -1, keepdims=True) + EPSILON)
    return centred * spread, spread


def norm_back(unit, spread, gain, upstream):
    scaled = upstream * gain
    return spread * (
        scaled
        - jnp.mean(scaled, -1, keepdims=True)
        - unit * jnp.mean(scaled * unit, -1, keepdims=True)
    )


def half_masks():
    lane = lax.broadcasted_iota(jnp.int32, (1, PAIR), 1)
    low = (lane < HEAD_DIM).astype(F32).astype(BF16)
    high = (lane >= HEAD_DIM).astype(F32).astype(BF16)
    return low, high


def pair_slices(packed, rows, width, pair):
    at = pair * PAIR
    return [packed[rows, part * width + at : part * width + at + PAIR] for part in range(3)]


def pair_slices(packed, rows, width, pair):
    at = pair * PAIR
    return [packed[rows, part * width + at : part * width + at + PAIR] for part in range(3)]


def attend_forward(packed, rows, width, out, total, bias, batch):
    masks = half_masks()
    lane = lax.broadcasted_iota(jnp.int32, (1, PAIR), 1)
    pairs = width // PAIR
    for first in range(0, pairs, batch):
        group = range(first, min(first + batch, pairs))
        loaded = [pair_slices(packed, rows, width, pair) for pair in group]
        scores = [
            dot(keys, queries * masks[side], NT) * (SCALE * LOG2E)
            for queries, keys, _ in loaded
            for side in range(2)
        ]
        if bias is not None:
            scores = [value + bias for value in scores]
        highest = [jnp.max(value, 0, keepdims=True) for value in scores]
        shares = [jnp.exp2(value - top) for value, top in zip(scores, highest)]
        weights = [jnp.sum(value, 0, keepdims=True) for value in shares]
        shares = [(value * (1.0 / weight)).astype(BF16) for value, weight in zip(shares, weights)]
        blended = [dot(value, loaded[i // 2][2], TN) for i, value in enumerate(shares)]
        total[2 * first : 2 * group.stop, rows] = jnp.concatenate(
            [top + jnp.log2(weight) for top, weight in zip(highest, weights)], 0
        )
        for i, pair in enumerate(group):
            out[rows, pair * PAIR : (pair + 1) * PAIR] = jnp.where(
                lane < HEAD_DIM, blended[2 * i], blended[2 * i + 1]
            ).astype(BF16)


def attend_forward_rows(packed, rows, width, out, total, batch):
    masks = half_masks()
    lane = lax.broadcasted_iota(jnp.int32, (1, PAIR), 1)
    pairs = width // PAIR
    for first in range(0, pairs, batch):
        group = range(first, min(first + batch, pairs))
        loaded = [pair_slices(packed, rows, width, pair) for pair in group]
        scores = [
            dot(queries * masks[side], keys, NT) * (SCALE * LOG2E)
            for queries, keys, _ in loaded
            for side in range(2)
        ]
        ones = [jnp.concatenate([v, jnp.ones_like(v)], 1) for _, _, v in loaded]
        highest = [jnp.max(value, 1, keepdims=True) for value in scores]
        shares = [jnp.exp2(value - top).astype(BF16) for value, top in zip(scores, highest)]
        blended = [dot(value, ones[i // 2]) for i, value in enumerate(shares)]
        sums = [b[:, PAIR:] for b in blended]
        blended = [b[:, :PAIR] * (1.0 / w) for b, w in zip(blended, sums)]
        logs = [top + jnp.log2(w) for top, w in zip(highest, sums)]
        for i, pair in enumerate(group):
            lg = jnp.where(lane < HEAD_DIM, logs[2*i], logs[2*i+1]).T
            total[2 * pair : 2 * pair + 1, rows] = lg[0:1]
            total[2 * pair + 1: 2 * pair + 2, rows] = lg[HEAD_DIM:HEAD_DIM+1]
            out[rows, pair * PAIR : (pair + 1) * PAIR] = jnp.where(
                lane < HEAD_DIM, blended[2 * i], blended[2 * i + 1]
            ).astype(BF16)


def attend_back(packed, rows, width, grad_out, total, bias, out, batch):
    masks = half_masks()
    pairs = width // PAIR
    for first in range(0, pairs, batch):
        group = range(first, min(first + batch, pairs))
        loaded = [pair_slices(packed, rows, width, pair) for pair in group]
        upstream = [grad_out[rows, pair * PAIR : (pair + 1) * PAIR] for pair in group]
        heads = [(i, side) for i in range(len(group)) for side in range(2)]
        own_q = [loaded[i][0] * masks[side] for i, side in heads]
        own_k = [loaded[i][1] * masks[side] for i, side in heads]
        own_up = [upstream[i] * masks[side] for i, side in heads]
        scores = [dot(loaded[i][1], own, NT) * (SCALE * LOG2E) for (i, _), own in zip(heads, own_q)]
        grad_shares = [dot(loaded[i][2], own, NT) for (i, _), own in zip(heads, own_up)]
        if bias is not None:
            scores = [value + bias for value in scores]
        sums = total[2 * first : 2 * group.stop, rows]
        shares = [jnp.exp2(value - sums[i : i + 1]) for i, value in enumerate(scores)]
        weighted = [value * grad for value, grad in zip(shares, grad_shares)]
        inner = [jnp.sum(value, 0, keepdims=True) for value in weighted]
        grad_scores = [
            (value - share * total_inner).astype(BF16)
            for value, share, total_inner in zip(weighted, shares, inner)
        ]
        grad_q = [dot(value, own, TN) for value, own in zip(grad_scores, own_k)]
        grad_k = [dot(value, own) for value, own in zip(grad_scores, own_q)]
        grad_v = [dot(value.astype(BF16), own) for value, own in zip(shares, own_up)]
        for i, pair in enumerate(group):
            at = pair * PAIR
            for part, (grad, scale) in enumerate(((grad_q, SCALE), (grad_k, SCALE), (grad_v, 1.0))):
                out[rows, part * width + at : part * width + at + PAIR] = (
                    (grad[2 * i] + grad[2 * i + 1]) * scale
                ).astype(BF16)


def embed(raw, vectors, actions):
    raw = raw.astype(F32)
    masked = raw > SEEN
    return jnp.where(masked, vectors[7:8, :], raw) + actions, masked


def space_forward_kernel(group, pieces, *refs):
    xs, (act, vectors, w_qkv, packed, out, total, *parts) = refs[:pieces], refs[pieces:]
    raw = jnp.concatenate([x[0] for x in xs], 0) if pieces > 1 else xs[0][0]
    count, width = raw.shape
    embedded, _ = embed(raw, vectors, act[0])
    unit, _ = normalise(embedded)
    normed = (unit * vectors[0:1, :] + vectors[1:2, :]).astype(BF16)
    packed[0] = dot(normed, w_qkv[...]).astype(BF16)
    attend_forward_rows(packed.at[0], slice(0, count), width, out.at[0], total.at[0], 4)
    share = count // group
    for j in range(group):
        parts[j][0, 0] = raw[j * share : (j + 1) * share]
        parts[j][0, 1] = out[0, j * share : (j + 1) * share]


def time_forward_kernel(sub, pieces, *refs):
    xs, o1s, refs = refs[:pieces], refs[pieces : 2 * pieces], refs[2 * pieces :]
    (act, perm, bias, vectors, w_space_out, w_qkv, w_out, h1, h2, a2, packed, o2, total) = refs
    x = jnp.concatenate([value[...] for value in xs], 0)
    o1 = jnp.concatenate([value[...] for value in o1s], 0)
    frames, places, width = x.shape
    count = frames * places
    raw = dot(perm[...], x.reshape(count, width))
    blended = dot(perm[...], o1.reshape(count, width)).astype(BF16)
    actions = jnp.broadcast_to(act[...][None], (places, frames, width)).reshape(count, width)
    embedded, _ = embed(raw, vectors, actions)
    after_space = embedded + dot(blended, w_space_out[...])
    h1[...] = after_space
    unit, _ = normalise(after_space)
    normed = (unit * vectors[2:3, :] + vectors[3:4, :]).astype(BF16)
    a2[...] = normed
    packed[...] = dot(normed, w_qkv[...]).astype(BF16)
    for start in range(0, count, sub):
        attend_forward(packed, slice(start, start + sub), width, o2, total, bias[...], 8)
    h2[...] = after_space + dot(o2[...], w_out[...])


def feed_kernel(tile, pieces, per, h2, *refs):
    cots, (vectors, b_up, w_up, w_down), refs = refs[:pieces], refs[pieces : pieces + 4], refs[pieces + 4 :]
    results, (cot, z, dur, a3, r2, sums, bias_grad) = refs[:pieces], refs[pieces:]
    piece = pl.program_id(0) // per
    for j in range(pieces):

        @pl.when(piece == j)
        def _(j=j):
            cot[...] = cots[j][...]

    @pl.when(pl.program_id(0) == 0)
    def _():
        sums[...] = jnp.zeros_like(sums)
        bias_grad[...] = jnp.zeros_like(bias_grad)

    after = h2[...]
    unit, spread = normalise(after)
    gain = vectors[4:5, :]
    normed = (unit * gain + vectors[5:6, :]).astype(BF16)
    a3[...] = normed
    upstream_low = cot[...]
    c = 0.7978845608028654
    total = after + vectors[6:7, :]
    grad_normed = jnp.zeros_like(after)
    for at in range(0, w_up.shape[1], tile):
        cols = slice(at, at + tile)
        hidden = dot(normed, w_up[:, cols]) + b_up[:, cols]
        grad_active = dot(upstream_low, w_down[cols, :], NT)
        square = hidden * hidden
        gate = 0.5 * jnp.tanh(hidden * (c + (c * 0.044715) * square)) + 0.5
        active = hidden * gate
        slope = gate + active * (1.0 - gate) * (2.0 * c + (6.0 * c * 0.044715) * square)
        grad_hidden = grad_active * slope
        bias_grad[:, cols] += jnp.sum(grad_hidden, 0, keepdims=True)
        active = active.astype(BF16)
        grad_hidden = grad_hidden.astype(BF16)
        z[:, cols] = active
        dur[:, cols] = grad_hidden
        total = total + dot(active, w_down[cols, :])
        grad_normed = grad_normed + dot(grad_hidden, w_up[:, cols], NT)
    for j in range(pieces):

        @pl.when(piece == j)
        def _(j=j):
            results[j][...] = total.astype(BF16)

    upstream = upstream_low.astype(F32)
    r2[...] = upstream + norm_back(unit, spread, gain, grad_normed)
    sums[0:1, :] += jnp.sum(grad_normed * unit, 0, keepdims=True)
    sums[1:2, :] += jnp.sum(grad_normed, 0, keepdims=True)
    sums[2:3, :] += jnp.sum(upstream, 0, keepdims=True)


def time_back_kernel(
    sub, r2, h1, packed, total, perm, bias, vectors, w_out, w_qkv, grad_packed, r2_low, sums, *rest
):
    *r1s, grad_out = rest

    @pl.when(pl.program_id(0) == 0)
    def _():
        sums[...] = jnp.zeros_like(sums)

    count, width = r2.shape
    stream = r2[...]
    low = stream.astype(BF16)
    r2_low[...] = low
    grad_out[...] = dot(low, w_out[...], NT).astype(BF16)
    for start in range(0, count, sub):
        attend_back(
            packed, slice(start, start + sub), width, grad_out, total, bias[...], grad_packed, 8
        )
    grad_normed = dot(grad_packed[...], w_qkv[...], NT)
    unit, spread = normalise(h1[...])
    stream = stream + norm_back(unit, spread, vectors[2:3, :], grad_normed)
    sums[0:1, :] += jnp.sum(grad_normed * unit, 0, keepdims=True)
    sums[1:2, :] += jnp.sum(grad_normed, 0, keepdims=True)
    r1 = dot(perm[...], stream.astype(BF16)).astype(BF16).reshape(-1, r1s[0].shape[1], width)
    share = r1s[0].shape[0]
    for j, piece in enumerate(r1s):
        piece[...] = r1[j * share : (j + 1) * share]


def space_back_kernel(pieces, group, order, *refs):
    xs, r1s, refs = refs[:pieces], refs[pieces : pieces + group], refs[pieces + group :]
    (act, hot, earlier, packed, total, vectors, w_out, w_qkv) = refs[:8]
    (grad_packed, a1, r1_all, sums), refs = refs[8:12], refs[12:]
    input_grads, (grad_out,) = refs[:-1], refs[-1:]

    @pl.when(pl.program_id(0) == 0)
    def _():
        sums[...] = earlier[...]

    raw = jnp.concatenate([x[0] for x in xs], 0) if pieces > 1 else xs[0][0]
    r1 = jnp.concatenate([value[0] for value in r1s], 0)
    r1_all[0] = r1
    count, width = raw.shape
    grad_out[...] = dot(r1, w_out[...], NT).astype(BF16)
    attend_back(
        packed.at[0], slice(0, count), width, grad_out, total.at[0], None, grad_packed.at[0], 4
    )
    grad_normed = dot(grad_packed[0], w_qkv[...], NT)
    embedded, masked = embed(raw, vectors, act[0])
    unit, spread = normalise(embedded)
    gain = vectors[0:1, :]
    a1[0] = (unit * gain + vectors[1:2, :]).astype(BF16)
    stream = r1.astype(F32) + norm_back(unit, spread, gain, grad_normed)
    kept = jnp.where(masked, 0.0, stream)
    if len(input_grads) == 1:
        input_grads[0][0] = kept.astype(BF16)
    else:
        share = count // len(order)
        for at, k in enumerate(order):
            input_grads[k // 2][k % 2, 0] = kept[at * share : (at + 1) * share].astype(BF16)
    whole_sum = jnp.sum(stream, 0, keepdims=True)
    sums[0:1, :] += jnp.sum(grad_normed * unit, 0, keepdims=True)
    sums[1:2, :] += jnp.sum(grad_normed, 0, keepdims=True)
    sums[2:3, :] += whole_sum - jnp.sum(kept, 0, keepdims=True)
    sums[8:, :] += hot[0] * whole_sum


def whole(array):
    rank = len(array.shape)
    return pl.BlockSpec(array.shape, lambda *_: (0,) * rank, pipeline_mode=pl.Buffered(1))


def struct(shape, kind):
    return jax.ShapeDtypeStruct(shape, kind)


def call(kernel, grid, operands, outs, scratch=(), flops=0, meta=None):
    in_specs = [
        whole(array) if block is None else pl.BlockSpec(block, index)
        for array, block, index in operands
    ]
    out_specs = [
        pl.BlockSpec(shape, lambda *_, rank=len(shape): (0,) * rank)
        if block is None
        else pl.BlockSpec(block, index)
        for shape, _, block, index in outs
    ]
    moved = sum(a.size * a.dtype.itemsize for a, _, _ in operands)
    return pl.pallas_call(
        kernel,
        grid_spec=pltpu.PrefetchScalarGridSpec(
            num_scalar_prefetch=0 if meta is None else 1,
            grid=grid,
            in_specs=in_specs,
            out_specs=out_specs,
            scratch_shapes=scratch,
        ),
        out_shape=[struct(shape, kind) for shape, kind, _, _ in outs],
        cost_estimate=pl.CostEstimate(flops=flops, bytes_accessed=2 * moved, transcendentals=0),
        compiler_params=pltpu.CompilerParams(vmem_limit_bytes=VMEM_LIMIT),
    )(*(() if meta is None else (meta,)), *[a for a, _, _ in operands])


def collect_kernel(parts, meta, *refs):
    *refs, perm, out, held = refs
    chip = pl.program_id(0)
    for i in range(len(refs) // (2 * parts)):

        @pl.when(chip == i)
        def _(i=i):
            found = [ref[...] for ref in refs[2 * parts * i : 2 * parts * (i + 1)]]
            held[...] = jnp.concatenate(found, 0).reshape(held.shape)

    out[...] = dot(perm[...], held[...]).astype(BF16).reshape(out.shape)


def collect(by_slot, chips, perm, shape, operand):
    p, width = shape[0], shape[-1]
    block = 16
    steps = p // block
    parts = len(by_slot[0])
    span = sum(part.shape[-3] for part, _ in by_slot[0])
    count = len(by_slot)
    operands = []
    for k, pieces in enumerate(by_slot):

        def slot_index(i, h, meta, k=k):
            return 0, jnp.where(i == k // 2, h, jnp.where(i < k // 2, 0, steps - 1)), 0

        operands += [
            operand(piece, (piece[0].shape[-3], block, width), slot_index) for piece in pieces
        ]
    operands.append((perm, None, None))
    outs = [
        (
            (p, count * span, width),
            BF16,
            (block, 2 * span, width),
            lambda i, h, meta: (h, meta[i], 0),
        )
    ]
    return call(
        lambda *refs: collect_kernel(parts, *refs),
        (count // 2, steps),
        operands,
        outs,
        [pltpu.VMEM((block * 2 * span, width), BF16)],
        meta=chips,
    )[0].reshape(shape)


def collect_result_kernel(meta, *refs):
    *pieces, out = refs
    for j, piece in enumerate(pieces):

        @pl.when(pl.program_id(0) == j)
        def _(piece=piece):
            out[...] = piece[...]


def collect_result(pieces, where):
    p, _, frames, width = pieces[0].shape
    return call(
        collect_result_kernel,
        (len(pieces),),
        [(piece, None, None) for piece in pieces],
        [
            (
                (p, len(pieces), frames, width),
                BF16,
                (p, 1, frames, width),
                lambda j, meta: (0, meta[j], 0, 0),
            )
        ],
        meta=where,
    )[0]


def put(outs, slot, value):
    share = outs[0].shape[0]
    outs[slot // share][slot % share] = value


def columns_kernel(meta, *refs, counts, firsts, blocks, split):
    step = pl.program_id(0)
    *refs, held = refs
    local = step % firsts[-1]
    for i, count in enumerate(counts):
        lefts, rights, refs = refs[:count], refs[count : 2 * count], refs[2 * count :]

        @pl.when((local >= firsts[i]) & (local < firsts[i + 1]))
        def _(lefts=lefts, rights=rights):
            total = sum(dot(l[...], r[...], TN) for l, r in zip(lefts, rights))
            held[...] = total.astype(BF16)

    shares = len(split)
    size = held.shape[0] // blocks
    per = firsts[-1] // shares
    for part in range(2 * shares):
        two = part >= shares and split[part - shares]
        own, refs = refs[: 1 + two], refs[1 + two :]

        @pl.when(step // per == part)
        def _(first=(part % shares) * blocks, own=own):
            for slot in range(blocks):
                source = pl.multiple_of(meta[first + slot] * size, size)
                put(own, slot, held[pl.ds(source, size), :])


def columns_grad(pairs, meta, split, tile=512):
    shares = len(split)
    blocks = (meta.shape[0] - 1) // shares
    height = pairs[0][0][0].shape[1]
    size = height // blocks
    tile = min([tile] + [rights[0].shape[1] // 2 for _, rights in pairs])
    steps = [rights[0].shape[1] // 2 // tile for _, rights in pairs]
    firsts = [sum(steps[:i]) for i in range(len(steps) + 1)]
    per = firsts[-1] // shares
    operands, flops = [], 0
    for (lefts, rights), first, count in zip(pairs, firsts, steps):
        operands += [(left, None, None) for left in lefts]
        for right in rights:

            def index(i, meta, first=first, count=count):
                core = meta[shares * blocks]
                half = jnp.where(i < firsts[-1], 1 - core, core)
                return 0, half * count + jnp.clip(i % firsts[-1] - first, 0, count - 1)

            operands.append((right, (right.shape[0], tile), index))
            flops += 2 * right.size * height

    def part_out(part, rows):
        block = (rows, size, tile), lambda i, meta: (0, 0, jnp.clip(i - part * per, 0, per - 1))
        return (rows, size, per * tile), BF16, *block

    outs = [part_out(share, blocks) for share in range(shares)]
    for share, two in enumerate(split):
        outs += [part_out(shares + share, blocks // (1 + two))] * (1 + two)
    kernel = lambda *refs: columns_kernel(
        *refs, counts=[len(lefts) for lefts, _ in pairs], firsts=firsts, blocks=blocks, split=split
    )
    scratch = [pltpu.VMEM((height, tile), BF16)]
    return call(kernel, (2 * firsts[-1],), operands, outs, scratch, flops, meta)


def rows_kernel(meta, *refs, step_blocks, steps, blocks):
    step = pl.program_id(0)
    lefts, right, (sent, *outs) = refs[:step_blocks], refs[step_blocks], refs[step_blocks + 1 :]
    value = dot(jnp.concatenate([left[...] for left in lefts], 1), right[...], TN).astype(BF16)
    value = value.reshape(step_blocks, -1, value.shape[-1])
    middle = value.shape[-1] // 2
    halves = value[:, :, :middle], value[:, :, middle:]
    share = steps // len(outs)
    for core in range(2):

        @pl.when(meta[blocks] == core)
        def _(core=core):
            sent[...] = halves[1 - core]

        for i, out in enumerate(outs):

            @pl.when((meta[blocks] == core) & (step >= i * share) & (step < (i + 1) * share))
            def _(core=core, out=out):
                out[...] = halves[core]


def rows_grad(left, right, meta, split, step_blocks=2):
    blocks = meta.shape[0] - 1
    depth, height = left.shape
    size, columns = height // blocks, right.shape[1] // 2
    steps = blocks // step_blocks
    operands = [
        (left, (depth, size), lambda i, meta, j=j: (0, meta[i * step_blocks + j]))
        for j in range(step_blocks)
    ]
    operands.append((right, None, None))
    parts = 1 + split[0]
    share = steps // parts
    block = (step_blocks, size, columns)
    outs = [((blocks, size, columns), BF16, block, lambda i, meta: (i, 0, 0))]
    outs += [
        (
            (blocks // parts, size, columns),
            BF16,
            block,
            lambda i, meta, first=j * share: (jnp.clip(i - first, 0, share - 1), 0, 0),
        )
        for j in range(parts)
    ]
    kernel = lambda *refs: rows_kernel(
        *refs, step_blocks=step_blocks, steps=steps, blocks=blocks
    )
    return call(kernel, (steps,), operands, outs, flops=4 * depth * height * columns, meta=meta)


def body(
    tokens,
    mask_bits,
    action_ids,
    vectors,
    action_table,
    w_space_qkv,
    w_space_out,
    w_time_qkv,
    w_time_out,
    w_up,
    b_up,
    w_down,
    cotangent,
):
    p, clips, frames, width = tokens.shape
    n, layers = lax.axis_size("tile"), lax.axis_size("clip")
    me, layer = lax.axis_index("tile"), lax.axis_index("clip")
    core = me % 2
    group = n // clips
    own_frames = frames // group
    grid_all = n * p
    places = grid_all // group
    clip, part = me // group, me % group
    hidden = w_up.shape[1]
    rows = places * frames

    def swap(value, k, axis="tile"):
        size = lax.axis_size(axis)
        return lax.ppermute(value, axis, [(i, i ^ k) for i in range(size)])

    def row_block(*shape):
        return shape, lambda i: (i,) + (0,) * (len(shape) - 1)

    blocks = n * layers // 2
    tile_bits = [1 << b for b in range(1, n.bit_length() - 1)]

    def orders(hops):
        slots = [(0, None, 0, None)]
        for hop in hops:
            if hop == "scatter":
                choices = [(0, None, 0, c) for c in range(layers)]
            elif hop == "tiles":
                choices = [(0, t, 0, None) for t in range(n // 2)]
            elif hop == "spread":
                choices = [(0, None, c, None) for c in range(layers)]
            else:
                bit = (hop[1], None, 0, None) if hop[0] == "tile" else (0, None, hop[1], None)
                choices = [(0, None, 0, None), bit]
            slots = [
                (a ^ x, t if u is None else u, b ^ y, c if d is None else d)
                for a, t, b, c in slots
                for x, u, y, d in choices
            ]
        where = [
            (layer ^ b if c is None else c) * (n // 2) + ((me ^ a) // 2 if t is None else t)
            for a, t, b, c in slots
        ]
        return jnp.stack([jnp.asarray(w, jnp.int32) for w in where])

    def halves(value, hop):
        if hop is None or isinstance(hop, str):
            return [value]
        middle = value.shape[0] // 2
        return [value[:middle], value[middle:]]

    def meta_of(chains):
        return jnp.concatenate([orders(hops) for hops in chains] + [core.astype(jnp.int32)[None]])

    def begin(make, chains, meta):
        split = [not isinstance(hops[0], str) for hops in chains]
        made = make(meta, split)
        sent, made, parts = list(made[: len(split)]), made[len(split) :], []
        for two in split:
            parts.append(list(made[: 1 + two]))
            made = made[1 + two :]
        return chains, parts, sent

    def cross(begun):
        chains, parts, sent = begun
        return chains, parts, [swap(value, 1) for value in sent]

    def add(values, kind):
        return sum(value.astype(F32) for value in values).astype(kind)

    def land(crossed):
        chains, all_parts, received = crossed
        landed = []
        for hops, parts, came in zip(chains, all_parts, received):
            if isinstance(hops[0], str):
                landed.append([[(add([parts[0], came], BF16), False)]])
            else:
                _, sent = halves(came, hops[0])
                landed.append([[(parts[0], False), (came, True)], add([parts[1], sent], BF16)])
        return chains, landed, 0

    def merge(state):
        chains, parts, at = state
        kept = jnp.concatenate([own[0][0][0] for own in parts], -1)
        return chains[:1], [[[(kept, False)], jnp.concatenate([own[1] for own in parts], -1)]], at

    def depart(state):
        chains, parts, at = state
        coming = []
        for hops, own in zip(chains, parts):
            hop, value = hops[at], own[0][0][0]
            if hop == "scatter":
                coming.append(lax.psum_scatter(value, "clip", scatter_dimension=0, tiled=True))
            elif hop == "tiles":
                same_core = [list(range(c, n, 2)) for c in range(2)]
                coming.append(
                    lax.psum_scatter(
                        value, "tile", scatter_dimension=0, tiled=True, axis_index_groups=same_core
                    )
                )
            elif hop == "spread":
                share = value.shape[0] // layers
                coming.append(
                    [swap(value[j * share : (j + 1) * share], j, "clip") for j in range(1, layers)]
                )
            else:
                coming.append(swap(own[1], hop[1], hop[0]))
        return state, coming

    def arrive(departed):
        (chains, parts, at), coming = departed
        new_parts = []
        for hops, own, came in zip(chains, parts, coming):
            following = hops[at + 1] if at + 1 < len(hops) else None
            kind = F32 if following is None else BF16
            kept = [v[: v.shape[0] // 2] if first else v for v, first in own[0]]
            if hops[at] == "spread":
                values = [kept[0][: kept[0].shape[0] // layers]] + came
            else:
                values = [came] if isinstance(hops[at], str) else kept + [came]
            summed = [add(piece, kind) for piece in zip(*[halves(v, following) for v in values])]
            new_parts.append([[(summed[0], False)]] + summed[1:])
        return chains, new_parts, at + 1

    def last_swap(state):
        own = jnp.concatenate([own[0][0][0][0].astype(F32) for own in state[1]], 1)
        size = own.shape[0] // 2
        mine = lax.dynamic_slice_in_dim(own, core * size, size, 0)
        other = lax.dynamic_slice_in_dim(own, (1 - core) * size, size, 0)
        return mine, swap(other.astype(BF16), 1)

    def join(mine, other, widths):
        whole_parts, at = [], 0
        for w in widths:
            a, b = mine[:, at : at + w // 2], other[:, at : at + w // 2].astype(F32)
            whole_parts.append(
                jnp.where(core == 0, jnp.concatenate([a, b], 1), jnp.concatenate([b, a], 1))
            )
            at += w // 2
        return whole_parts

    one_way = [("tile", bit) for bit in tile_bits]
    other_way = one_way[::-1]
    clip_bits = [("clip", 1 << b) for b in range(layers.bit_length() - 1)]
    up_chains, down_chains = [one_way + clip_bits], [["scatter"] + one_way]
    time_chains, space_chains = [["scatter"] + other_way], [one_way + clip_bits, other_way + clip_bits]

    order = [k for j in range(group) for k in range(j, n, group)]
    onehot = (action_ids[..., None] == lax.iota(jnp.int32, action_table.shape[0])).astype(F32)
    action_rows = jnp.einsum("cfa,ad->cfd", onehot, action_table, precision=lax.Precision.HIGHEST)
    act_time = lax.dynamic_index_in_dim(action_rows, clip, 0, keepdims=False)
    act_space = lax.dynamic_slice_in_dim(act_time, part * own_frames, own_frames, 0)[:, None, :]

    regular = p % 16 == 0 and 2 * own_frames == 16
    deal_back = None
    if regular:
        at = lax.iota(jnp.int32, 16 * 2 * own_frames)
        place, frame = at % 16, at // 16
        source = place * 2 * own_frames + (frame + core * own_frames) % (2 * own_frames)
        deal_back = (at[:, None] == source[None, :]).astype(BF16)
    marked = jnp.where((mask_bits > 0)[..., None], jnp.asarray(MASKED, BF16), tokens)
    marked = marked.reshape(p, n, own_frames, width)
    chunks = 2
    span = own_frames // chunks
    blocks_of = [lax.dynamic_index_in_dim(marked, me ^ k, 1, keepdims=False) for k in order]
    sources = [
        [value[:, c * span : (c + 1) * span].transpose(1, 0, 2) for value in blocks_of]
        for c in range(chunks)
    ]

    def send_out(parts):
        return [part if k == 0 else swap(part, k) for k, part in zip(order, parts)]

    cot_pieces = [
        lax.dynamic_index_in_dim(cotangent, clip ^ j, 1, keepdims=False).reshape(p * frames, width)
        for j in range(n // group)
    ]
    block = 16
    count = block * frames
    sub = min(count, 128)
    index = lax.iota(jnp.int32, count)
    slot, place = index // block, index % block
    frame_of_slot = ((part ^ (slot // own_frames)) * own_frames) + slot % own_frames
    target = place * frames + frame_of_slot
    perm_back = (target[:, None] == index[None, :]).astype(BF16)
    perm = (index[:, None] == target[None, :]).astype(BF16)
    seq = lax.iota(jnp.int32, sub)
    same = (seq[:, None] // frames) == (seq[None, :] // frames)
    bias = jnp.where(same & (seq[:, None] <= seq[None, :]), 0.0, NEGATIVE).astype(F32)
    own_hot = lax.dynamic_slice_in_dim(
        lax.dynamic_index_in_dim(onehot, clip, 0, keepdims=False), part * own_frames, own_frames, 0
    )[..., None]
    where_clip = clip ^ lax.iota(jnp.int32, clips)
    where_chip = (me // 2) ^ lax.iota(jnp.int32, n // 2)
    tables = dict(
        act_time=act_time,
        act_space=act_space,
        perm=perm,
        perm_back=perm_back,
        bias=bias,
        own_hot=own_hot,
        where_clip=where_clip,
        where_chip=where_chip,
        deal_back=deal_back,
        **{
            name: meta_of(chains)
            for name, chains in (
                ("up", up_chains),
                ("down", down_chains),
                ("time", time_chains),
                ("space", space_chains),
            )
        },
    )
    pieces = []
    for c in range(chunks):
        pieces.append(send_out(sources[c]))
        if c == 0:
            pieces[0], sources, cot_pieces, tables = hold_parts(
                pieces[0], sources, cot_pieces, tables
            )
    cot_pieces = [
        piece if j == 0 else swap(piece, j * group) for j, piece in enumerate(cot_pieces)
    ]
    if p % 16:
        pieces = [[jnp.concatenate(parts, 1)] for parts in pieces]
    kinds = len(pieces[0])
    act_time, act_space, own_hot = (tables[name] for name in ("act_time", "act_space", "own_hot"))
    perm, perm_back, bias = (tables[name] for name in ("perm", "perm_back", "bias"))
    where_clip, where_chip, deal_back = (
        tables[name] for name in ("where_clip", "where_chip", "deal_back")
    )

    head_flops = 2 * HEADS * HEAD_DIM

    def frame_block(*shape):
        return (1,) + shape, lambda i: (i, 0, 0)

    def chunk_block(first, *shape):
        return (1,) + shape, lambda i: (first + i, 0, 0)

    space, both = [], []
    for c in range(chunks):
        packed, o1, total, *parts = call(
            lambda *refs: space_forward_kernel(group, kinds, *refs),
            (span,),
            [(x, *frame_block(*x.shape[1:])) for x in pieces[c]]
            + [
                (act_space, *chunk_block(c * span, 1, width)),
                (vectors, None, None),
                (w_space_qkv, None, None),
            ],
            [
                ((span, grid_all, 3 * width), BF16, *frame_block(grid_all, 3 * width)),
                ((span, grid_all, width), BF16, *frame_block(grid_all, width)),
                ((span, HEADS, grid_all), F32, *frame_block(HEADS, grid_all)),
            ]
            + [
                (
                    (span, 2, places, width),
                    BF16,
                    (1, 2, places, width),
                    lambda i: (i, 0, 0, 0),
                )
            ]
            * group,
            flops=2 * span * grid_all * width * 3 * width
            + 16 * span * grid_all * grid_all * head_flops,
        )
        space.append((packed, o1, total))
        both.append([part if j == 0 else swap(part, j) for j, part in enumerate(parts)])
    both = [both[c][j] for j in range(group) for c in range(chunks)]

    def slot_block(size):
        return (size, block, width), lambda i: (0, i, 0)

    total_block = ((HEADS, count), lambda i: (0, i))
    h1, h2, a2, packed_two, o2, total_two = call(
        lambda *refs: time_forward_kernel(sub, len(both), *refs),
        (places // block,),
        [
            (value, (span, None, block, width), lambda i, which=which: (0, which, i, 0))
            for which in range(2)
            for value in both
        ]
        + [
            (act_time, None, None),
            (perm, None, None),
            (bias, None, None),
            (vectors, None, None),
            (w_space_out, None, None),
            (w_time_qkv, None, None),
            (w_time_out, None, None),
        ],
        [
            ((rows, width), F32, *row_block(count, width)),
            ((rows, width), F32, *row_block(count, width)),
            ((rows, width), BF16, *row_block(count, width)),
            ((rows, 3 * width), BF16, *row_block(count, 3 * width)),
            ((rows, width), BF16, *row_block(count, width)),
            ((HEADS, rows), F32, *total_block),
        ],
        flops=2 * rows * width * 5 * width + 16 * rows * sub * head_flops,
    )

    step = min(p * frames, 256)
    per = p * frames // step

    def piece_block(j):
        return (step, width), lambda i, j=j: (jnp.clip(i - j * per, 0, per - 1), 0)

    *result_pieces, cot, z, dur, a3, r2, sums_three, bias_up = call(
        lambda *refs: feed_kernel(1024, len(cot_pieces), per, *refs),
        (rows // step,),
        [(h2, *row_block(step, width))]
        + [(piece, *piece_block(j)) for j, piece in enumerate(cot_pieces)]
        + [
            (vectors, None, None),
            (b_up[None, :], None, None),
            (w_up, None, None),
            (w_down, None, None),
        ],
        [((p * frames, width), BF16, *piece_block(j)) for j in range(len(cot_pieces))]
        + [
            ((rows, width), BF16, *row_block(step, width)),
            ((rows, hidden), BF16, *row_block(step, hidden)),
            ((rows, hidden), BF16, *row_block(step, hidden)),
            ((rows, width), BF16, *row_block(step, width)),
            ((rows, width), F32, *row_block(step, width)),
            ((8, width), F32, None, None),
            ((1, hidden), F32, None, None),
        ],
        flops=8 * rows * width * hidden,
    )

    result_pieces = [
        (piece if j == 0 else swap(piece, j * group)).reshape(p, 1, frames, width)
        for j, piece in enumerate(result_pieces)
    ]

    def make_down(meta, split):
        if hidden // blocks % 128:
            return columns_grad([([z], [cot])], meta, split, 256)
        return rows_grad(z, cot, meta, split)

    def make_up(meta, split):
        return columns_grad([([a3], [dur])], meta, split)

    up = begin(make_up, up_chains, tables["up"])
    cot, up, result_pieces[:-1] = hold_parts(cot, up, result_pieces[:-1])
    up = cross(up)
    down = begin(make_down, down_chains, tables["down"])
    r2, down, up, result_pieces = hold_parts(r2, down, up, result_pieces)
    up, down = depart(land(up)), cross(down)

    grad_packed_two, r2_low, sums_two, *r1_parts = call(
        lambda *refs: time_back_kernel(sub, *refs),
        (places // block,),
        [
            (r2, *row_block(count, width)),
            (h1, *row_block(count, width)),
            (packed_two, *row_block(count, 3 * width)),
            (total_two, *total_block),
            (perm_back, None, None),
            (bias, None, None),
            (vectors, None, None),
            (w_time_out, None, None),
            (w_time_qkv, None, None),
        ],
        [
            ((rows, 3 * width), BF16, *row_block(count, 3 * width)),
            ((rows, width), BF16, *row_block(count, width)),
            ((8, width), F32, None, None),
        ]
        + [((own_frames, places, width), BF16, *slot_block(own_frames))] * group,
        [pltpu.VMEM((count, width), BF16)],
        flops=2 * rows * width * 4 * width + 40 * rows * sub * head_flops,
    )
    grad_packed_two, up, down = hold_parts(grad_packed_two, up, down)
    up, down = depart(arrive(up)), depart(land(down))
    r1_parts = [r1 if j == 0 else swap(r1, j) for j, r1 in enumerate(r1_parts)]

    def make_time(meta, split):
        return columns_grad([([a2], [grad_packed_two]), ([o2], [r2_low])], meta, split)

    time = begin(make_time, time_chains, tables["time"])

    dealt = 1 if p % 16 else n

    def send_back(parts):
        if dealt == 1:
            parts = [parts[0][:, at * p : (at + 1) * p] for at in range(n)]
            parts = [parts[order.index(k)] for k in range(n)]
            parts = [jnp.stack(parts[2 * j : 2 * j + 2]) for j in range(n // 2)]
        return [part if j == 0 else swap(part, 2 * j) for j, part in enumerate(parts)]

    def pass_on(came):
        crossed = swap(jnp.stack([value[1] for value in came]), 1)
        return [found for j, value in enumerate(came) for found in ((value, 0), (crossed, j))]

    def operand(found, block, index):
        return found[0], (None,) + block, lambda *i: (found[1],) + index(*i)

    def space_back(c, earlier):
        packed, _, total = space[c]
        return call(
            lambda *refs: space_back_kernel(kinds, group, order, *refs),
            (span,),
            [(x, *frame_block(*x.shape[1:])) for x in pieces[c]]
            + [(r1, *chunk_block(c * span, places, width)) for r1 in r1_parts]
            + [
                (act_space, *chunk_block(c * span, 1, width)),
                (own_hot, *chunk_block(c * span, action_table.shape[0], 1)),
                (earlier, None, None),
                (packed, *frame_block(grid_all, 3 * width)),
                (total, *frame_block(HEADS, grid_all)),
                (vectors, None, None),
                (w_space_out, None, None),
                (w_space_qkv, None, None),
            ],
            [
                ((span, grid_all, 3 * width), BF16, *frame_block(grid_all, 3 * width)),
                ((span, grid_all, width), BF16, *frame_block(grid_all, width)),
                ((span, grid_all, width), BF16, *frame_block(grid_all, width)),
                ((8 + action_table.shape[0], width), F32, None, None),
            ]
            + (
                [((span, grid_all, width), BF16, *frame_block(grid_all, width))]
                if dealt == 1
                else [
                    ((2, span, p, width), BF16, (2, 1, p, width), lambda i: (0, i, 0, 0))
                ]
                * (n // 2)
            ),
            [pltpu.VMEM((grid_all, width), BF16)],
            flops=2 * span * grid_all * width * 4 * width
            + 40 * span * grid_all * grid_all * head_flops,
        )

    r1_parts, time, up = hold_parts(r1_parts, time, up)
    up, time = depart(arrive(up)), cross(time)
    early = jnp.concatenate([sums_two, sums_three, bias_up.reshape(-1, width)], 0)
    back = [space_back(0, jnp.zeros((8 + action_table.shape[0], width), F32))]
    back[0], r1_parts, time, up = hold_parts(back[0], r1_parts, time, up)
    input_pieces = [send_back(back[0][4:])]
    up, time = depart(arrive(up)), depart(land(time))
    for c in range(1, chunks):
        back.append(space_back(c, back[-1][3]))
    back, input_pieces, up, down = hold_parts(back, input_pieces, up, down)
    input_pieces[0] = pass_on(input_pieces[0])
    for c in range(1, chunks):
        input_pieces.append(send_back(back[c][4:]))
    up = arrive(up)
    while up[2] < len(up[0][0]):
        up = arrive(depart(up))
    up, down = last_swap(up), depart(arrive(down))
    grads_one, a1s, r1s = list(zip(*back))[:3]

    def flat(values):
        return [value.reshape(-1, value.shape[-1]) for value in values]

    def make_space(meta, split):
        return columns_grad(
            [
                (flat(a1s), flat(grads_one)),
                (flat([o1 for _, o1, _ in space]), flat(r1s)),
            ],
            meta,
            split,
        )

    small = jnp.concatenate([back[-1][3], early], 0)
    small_hops = [("tile", 1 << b) for b in range(n.bit_length() - 1)] + clip_bits

    space_sum = begin(make_space, space_chains, tables["space"])
    where_clip, space_sum, up, down, input_pieces = hold_parts(
        where_clip, space_sum, up, down, input_pieces
    )
    space_sum = cross(space_sum)
    small_came = swap(small, small_hops[0][1], small_hops[0][0])
    down = depart(arrive(down))
    result_out = collect_result(result_pieces, where_clip)
    space_sum, result_out, small_came = hold_parts(space_sum, result_out, small_came)
    space_sum, small = land(space_sum), small + small_came
    input_pieces[1:] = [pass_on(came) for came in input_pieces[1:]]
    time = arrive(time)

    def collect_input(input_pieces, where_chip):
        by_slot = [[pieces_of[k] for pieces_of in input_pieces] for k in range(n)]
        if regular:
            input_grad = collect(by_slot, where_chip, deal_back, tokens.shape, operand)
        else:
            input_grad = jnp.zeros((p, n, own_frames, width), BF16)
            for k, parts in enumerate(by_slot):
                piece = jnp.concatenate([value[at] for value, at in parts], 0)
                input_grad = lax.dynamic_update_slice_in_dim(
                    input_grad, piece.transpose(1, 0, 2)[:, None], me ^ k, 1
                )
            input_grad = input_grad.reshape(tokens.shape)
        return input_grad

    rounds = max(len(small_hops) - 1, len(space_sum[0][0]) + 1, 2 * len(one_way))
    for r in range(rounds):
        departed = small_came = time_moves = None
        if r < len(space_sum[0][0]):
            if r == len(one_way):
                space_sum = merge(space_sum)
            departed = depart(space_sum)
        if r + 1 < len(small_hops):
            small_came = swap(small, small_hops[r + 1][1], small_hops[r + 1][0])
        if r >= len(one_way) and time[2] < len(time[0][0]):
            time_moves = depart(time)
        others = [down, input_pieces] if r == 0 else []
        if r == 1:
            input_grad = collect_input(input_pieces, where_chip)
            others = [input_grad]
        departed, small_came, time_moves, *others = hold_parts(
            departed, small_came, time_moves, *others
        )
        if r == 0:
            down, input_pieces = others
            down = arrive(down)
            while down[2] < len(down[0][0]):
                down = arrive(depart(down))
            down = last_swap(down)
        if r == 1:
            (input_grad,) = others
        if time_moves is not None:
            time = arrive(time_moves)
            if time[2] == len(time[0][0]):
                time_last = last_swap(time)
        if departed is not None:
            space_sum = arrive(departed)
        if small_came is not None:
            small = small + small_came
        if r + 1 == len(space_sum[0][0]):
            space_last = last_swap(space_sum)
    at = 8 + action_table.shape[0]
    sums = small[at:]
    (down_out,) = join(*down, [width])
    (up_out,) = join(*up, [hidden])
    time_qkv, time_out = join(*time_last, [3 * width, width])
    space_qkv, space_out = join(*space_last, [3 * width, width])
    return (
        result_out,
        input_grad,
        jnp.concatenate([small[:2], sums[:2], sums[8:11], small[2:3]], 0),
        small[8:at],
        space_qkv,
        space_out,
        time_qkv,
        time_out,
        up_out,
        sums[16:].reshape(hidden),
        down_out,
    )


def hold_parts(*values):
    leaves, tree = jax.tree.flatten(values)
    arrays = [i for i, leaf in enumerate(leaves) if isinstance(leaf, jax.Array)]
    held = lax.optimization_barrier([leaves[i] for i in arrays])
    for i, leaf in zip(arrays, held):
        leaves[i] = leaf
    return jax.tree.unflatten(tree, leaves)


def solution(mesh):
    spread = P("tile", "clip", None, None)
    rows = P(("clip", "tile"), None)
    return jax.shard_map(
        body,
        mesh=mesh,
        in_specs=(spread, P("tile", "clip", None), P("clip", None)) + (P(),) * 9 + (spread,),
        out_specs=(spread, spread, P(), P(), rows, rows, rows, rows, rows, P(), rows),
        check_vma=False,
    )
```

profile of v0, /device:TPU:0, one launch (start us, length us, event | category | flops | bytes accessed | tf_op | source)
XLA Modules:
  0.0 649.6 jit_solution(18159777626762474299)
XLA Ops:
  8.2 2.5 broadcast_select_fusion
  12.7 2.4 collective-permute-start.5
  15.9 1.7 collective-permute-start.6
  21.3 2.1 collective-permute-start.1
  27.5 4.2 constant_dynamic-slice_fusion.2
  39.2 4.2 collective-permute-done.2.refs_3_
  43.5 3.3 collective-permute-done.refs_1_
  46.8 1.7 collective-permute-start.11
  50.1 1.6 collective-permute-start.7
  53.2 2.2 collective-permute-done.11.refs_5_
  55.4 2.0 collective-permute-start.9
  57.5 20.7 %shard_map.212 = (bf16[4,256,3072]{2,1,0:T(8,128)(2,1)}, bf16[4,256,1024]{2,1,0:T(8,128)(2,1)}, f32[4,16,256]{2,1,0:T(8,128)}, bf16[4,2,128,1024]{3,2,1,0:T(8,128)(2,1)}, bf16[4,2,128,1024]{3,2,1,0:T(8,128)(2,1)}) custom-call(bf16[4,32,1024]{2,1,0:T(8,128)(2,1)} %get-tuple-element.240.refs_0_, bf16[4,32,1024]{2,1,0:T(8,128)(2,1)} %collective-permute-done.refs_1_, ...), custom_call_target="tpu_custom_call" | custom-call | flops 15032385536 | bytes 16908288 | tf_op jit(solution)/shard_map/pallas_call | solution.py:336
  80.2 20.9 %shard_map.213 = (bf16[4,256,3072]{2,1,0:T(8,128)(2,1)}, bf16[4,256,1024]{2,1,0:T(8,128)(2,1)}, f32[4,16,256]{2,1,0:T(8,128)}, bf16[4,2,128,1024]{3,2,1,0:T(8,128)(2,1)}, bf16[4,2,128,1024]{3,2,1,0:T(8,128)(2,1)}) custom-call(bf16[4,32,1024]{2,1,0:T(8,128)(2,1)} %get-tuple-element.250.refs_0_, bf16[4,32,1024]{2,1,0:T(8,128)(2,1)} %collective-permute-done.7.refs_1_, ...), custom_call_target="tpu_custom_call" | custom-call | flops 15032385536 | bytes 16908288 | tf_op jit(solution)/shard_map/pallas_call | solution.py:336
  102.2 2.5 collective-permute-start.18
  105.6 45.7 %shard_map.214 = (f32[2048,1024]{1,0:T(8,128)}, f32[2048,1024]{1,0:T(8,128)}, bf16[2048,1024]{1,0:T(8,128)(2,1)}, bf16[2048,3072]{1,0:T(8,128)(2,1)}, bf16[2048,1024]{1,0:T(8,128)(2,1)}, /*index=5*/f32[16,2048]{1,0:T(8,128)}) custom-call(bf16[4,2,128,1024]{3,2,1,0:T(8,128)(2,1)} %get-tuple-element.249.refs_0_.refs_4_, ...), custom_call_target="tpu_custom_call" | custom-call | flops 30064771072 | bytes 55115776 | tf_op jit(solution)/shard_map/pallas_call | solution.py:336
  151.4 100.1 %shard_map.215 = (bf16[512,1024]{1,0:T(8,128)(2,1)}, bf16[512,1024]{1,0:T(8,128)(2,1)}, bf16[512,1024]{1,0:T(8,128)(2,1)}, bf16[512,1024]{1,0:T(8,128)(2,1)}, bf...) custom-call(f32[2048,1024]{1,0:T(8,128)} %get-tuple-element.264.refs, ...), custom_call_target="tpu_custom_call" | custom-call | flops 68719476736 | bytes 58818560 | tf_op jit(solution)/shard_map/pallas_call | solution.py:336
  252.5 25.4 %shard_map.216 = (bf16[16,64,2048]{2,1,0:T(8,128)(2,1)}, bf16[8,64,2048]{2,1,0:T(8,128)(2,1)}, bf16[8,64,2048]{2,1,0:T(8,128)(2,1)}) custom-call(s32[17]{0:T(128)} %concatenate.63.refs_0_, bf16[2048,1024]{1,0:T(8,128)(2,1)} %get-tuple-element.274.refs_1_, bf16[2048,4096]{1,0:T(8,128)(2,1)} %get-tuple-element.275.refs_2_), custom_call_target="tpu_custom_call" | custom-call | flops 17179869184 | bytes 41943040 | tf_op jit(solution)/shard_map/pallas_call | solution.py:336
  278.1 2.6 collective-permute-start.22
  280.7 24.9 %shard_map.217 = (bf16[16,256,512]{2,1,0:T(8,128)(2,1)}, bf16[16,256,512]{2,1,0:T(8,128)(2,1)}) custom-call(s32[17]{0:T(128)} %concatenate.60.refs_0_, bf16[2048,4096]{1,0:T(8,128)(2,1)} %get-tuple-element.271.refs_1_.refs_2_, bf16[2048,4096]{1,0:T(8,128)(2,1)} %get-tuple-element.271.refs_1_.refs_2_, bf16[2048,1024]{1,0:T(8,128)(2,1)} %get-tuple-element.282.refs_3_), custom_call_target="tpu_custom_call" | custom-call | flops 17179869184 | bytes 75497472 | tf_op jit(solution)/shard_map/pallas_call | solution.py:336
  305.7 4.0 add_convert_fusion.2
  310.5 50.5 %shard_map.218 = (bf16[2048,3072]{1,0:T(8,128)(2,1)}, bf16[2048,1024]{1,0:T(8,128)(2,1)}, f32[8,1024]{1,0:T(8,128)}, bf16[8,128,1024]{2,1,0:T(8,128)(2,1)}, bf16[8,128,1024]{2,1,0:T(8,128)(2,1)}) custom-call(f32[2048,1024]{1,0:T(8,128)} %get-tuple-element.292.refs_0_, f32[2048,1024]{1,0:T(8,128)} %get-tuple-element.293.refs_1_, ...), custom_call_target="tpu_custom_call" | custom-call | flops 38654705664 | bytes 76218368 | tf_op jit(solution)/shard_map/pallas_call | solution.py:336
  362.3 6.9 %add_convert_fusion.1 = bf16[16,256,512]{2,1,0:T(8,128)(2,1)} fusion(bf16[16,256,512]{2,1,0:T(8,128)(2,1)} %collective-permute-done.25, bf16[16,256,512]{2,1,0:T(8,128)(2,1)} %get-tuple-element.354), kind=kLoop, calls=%fused_computation.1 | loop fusion | flops 8388608 | bytes 12582912 | tf_op jit(solution)/shard_map/convert_element_type | solution.py:626
  370.7 4.4 add_convert_fusion.5
  376.6 27.1 %shard_map.219 = (bf16[16,64,2048]{2,1,0:T(8,128)(2,1)}, bf16[16,64,2048]{2,1,0:T(8,128)(2,1)}) custom-call(s32[17]{0:T(128)} %concatenate.62.refs_0_, bf16[2048,1024]{1,0:T(8,128)(2,1)} %get-tuple-element.300.refs_1_, bf16[2048,3072]{1,0:T(8,128)(2,1)} %get-tuple-element.307.refs_2_, bf16[2048,1024]{1,0:T(8,128)(2,1)} %get-tuple-element.308.refs_3_, ...), custom_call_target="tpu_custom_call" | custom-call | flops 17179869184 | bytes 50331648 | tf_op jit(solution)/shard_map/pallas_call | solution.py:336
  405.0 1.6 collective-permute-start.28
  407.2 32.9 %shard_map.220 = (bf16[4,256,3072]{2,1,0:T(8,128)(2,1)}, bf16[4,256,1024]{2,1,0:T(8,128)(2,1)}, bf16[4,256,1024]{2,1,0:T(8,128)(2,1)}, f32[16,1024]{1,0:T(8,128)...) custom-call(bf16[4,32,1024]{2,1,0:T(8,128)(2,1)} %get-tuple-element., ...), custom_call_target="tpu_custom_call" | custom-call | flops 30064771072 | bytes 42336768 | tf_op jit(solution)/shard_map/pallas_call | solution.py:336
  440.1 4.4 collective-permute-done.28
  446.0 2.3 collective-permute-start.31
  448.3 7.7 %add_convert_fusion = bf16[16,64,2048]{2,1,0:T(8,128)(2,1)} fusion(bf16[16,64,2048]{2,1,0:T(8,128)(2,1)} %collective-permute-done.27, bf16[16,64,2048]{2,1,0:T(8,128)(2,1)} %get-tuple-element.449), kind=kLoop, calls=%fused_computation | loop fusion | flops 8388608 | bytes 12582912 | tf_op jit(solution)/shard_map/convert_element_type | solution.py:626
  456.1 32.8 %shard_map.221 = (bf16[4,256,3072]{2,1,0:T(8,128)(2,1)}, bf16[4,256,1024]{2,1,0:T(8,128)(2,1)}, bf16[4,256,1024]{2,1,0:T(8,128)(2,1)}, f32[16,1024]{1,0:T(8,128)...) custom-call(bf16[4,32,1024]{2,1,0:T(8,128)(2,1)} %get-tuple-element., ...), custom_call_target="tpu_custom_call" | custom-call | flops 30064771072 | bytes 42336768 | tf_op jit(solution)/shard_map/pallas_call | solution.py:336
  493.0 1.8 collective-permute-start.36
  494.9 1.5 collective-permute-start.38
  496.5 29.1 %shard_map.222 = (bf16[16,64,1024]{2,1,0:T(8,128)(2,1)}, bf16[16,64,1024]{2,1,0:T(8,128)(2,1)}, bf16[8,64,1024]{2,1,0:T(8,128)(2,1)}, bf16[8,64,1024]{2,1,0:T(8,...) custom-call(s32[33]{0:T(128)} %concatenate.61.refs_0_, bf16[1024,1024]{1,0:T(8,128)(2,1)} %bitcast.144, ...), custom_call_target="tpu_custom_call" | custom-call | flops 17179869184 | bytes 50331648 | tf_op jit(solution)/shard_map/pallas_call | solution.py:336
  525.7 3.3 collective-permute-done.38.refs_14_
  534.3 5.3 shard_map.223
  539.6 2.0 add_convert_fusion.3
  541.7 1.9 collective-permute-start.43
  543.6 1.9 add_convert_fusion.4
  550.2 22.5 %collective-permute-done.45 = bf16[1,256,512]{2,1,0:T(8,128)(2,1)S(1)} collective-permute-done((bf16[1,256,512]{2,1,0:T(8,128)(2,1)S(1)}, bf16[1,256,512]{2,1,0:T(8,128)(2,1)S(1)}, u32[]{:S(2)}, u32[]{:S(2)}) %collective-permute-start.45) | collective-permute-done | bytes 262176 | tf_op jit(solution)/shard_map/ppermute | solution.py:572
  574.1 2.6 add_convert_fusion.7
  577.0 2.6 add_convert_fusion.9
  582.6 9.1 %shard_map.224 = bf16[32,64,1024]{2,1,0:T(8,128)(2,1)} custom-call(s32[4]{0:T(128)} %iota_xor_fusion.meta.refs_0_, bf16[2,4,32,1024]{3,2,1,0:T(8,128)(2,1)} %get-tuple-element.426.refs_1_, bf16[2,4,32,1024]{3,2,1,0:T(8,128)(2,1)} %get-tuple-element.427.refs_2_, bf16[4,4,32,1024]{3,2,1,0:T(8,128)(2,1)} %copy-done.2, bf16[4,4,32,1024]{3,2,1,0:T(8,128)(2,1)} %copy-done.3, ...), custom_call_target="tpu_custom_call" | custom-call | bytes 25427968 | tf_op jit(solution)/shard_map/pallas_call | solution.py:336
  591.7 4.2 collective-permute-done.49
  598.8 3.5 collective-permute-start.50
  606.1 9.7 %collective-permute-done.51 = f32[36,1024]{1,0:T(8,128)S(1)} collective-permute-done((f32[36,1024]{1,0:T(8,128)S(1)}, f32[36,1024]{1,0:T(8,128)S(1)}, u32[]{:S(2)}, u32[]{:S(2)}) %collective-permute-start.51) | collective-permute-done | bytes 147488 | tf_op jit(solution)/shard_map/ppermute | solution.py:572
  616.0 1.8 collective-permute-start.55
  619.9 1.9 collective-permute-start.54
  622.8 13.7 %collective-permute-done.54 = f32[36,1024]{1,0:T(8,128)S(1)} collective-permute-done((f32[36,1024]{1,0:T(8,128)S(1)}, f32[36,1024]{1,0:T(8,128)S(1)}, u32[]{:S(2)}, u32[]{:S(2)}) %collective-permute-start.54) | collective-permute-done | bytes 147488 | tf_op jit(solution)/shard_map/ppermute | solution.py:572
  (268 shorter events, 70.0 us)
Async XLA Ops:
  7.2 481.8 %reduce-scatter.3.cloned.1.call-start = ((), (), s32[]{:S(2)}) async-start(), calls=%async_computation.2 | async-start | bytes 5242880 | tf_op jit(solution)/shard_map/reduce_scatter | solution.py:650
  12.7 20.3 %collective-permute-start.5 = (bf16[4,32,1024]{2,1,0:T(8,128)(2,1)}, bf16[4,32,1024]{2,1,0:T(8,128)(2,1)}, u32[]{:S(2)}, u32[]{:S(2)}) collective-permute-start(bf16[4,32,1024]{2,1,0:T(8,128)(2,1)} %get-tuple-element.504), channel_id=1, source_target_pairs={{0,5},{1,4},{2,7},{3,6},{4,1},{5,0},{6,3},{7,2},{8,13},{9,12},{10,... | collective-permute-start | bytes 786440 | tf_op jit(solution)/shard_map/ppermute | solution.py:572
  15.9 18.6 %collective-permute-start.6 = (bf16[4,32,1024]{2,1,0:T(8,128)(2,1)}, bf16[4,32,1024]{2,1,0:T(8,128)(2,1)}, u32[]{:S(2)}, u32[]{:S(2)}) collective-permute-start(bf16[4,32,1024]{2,1,0:T(8,128)(2,1)} %get-tuple-element.502), channel_id=1, source_target_pairs={{0,7},{1,6},{2,5},{3,4},{4,3},{5,2},{6,1},{7,0},{8,15},{9,14},{10,... | collective-permute-start | bytes 786440 | tf_op jit(solution)/shard_map/ppermute | solution.py:572
  18.9 20.3 %collective-permute-start.3 = (bf16[4,32,1024]{2,1,0:T(8,128)(2,1)}, bf16[4,32,1024]{2,1,0:T(8,128)(2,1)}, u32[]{:S(2)}, u32[]{:S(2)}) collective-permute-start(bf16[4,32,1024]{2,1,0:T(8,128)(2,1)} %get-tuple-element.508), channel_id=1, source_target_pairs={{0,1},{1,0},{2,3},{3,2},{4,5},{5,4},{6,7},{7,6},{8,9},{9,8},{10,11... | collective-permute-start | bytes 786440 | tf_op jit(solution)/shard_map/ppermute | solution.py:572
  19.8 19.4 %collective-permute-start.4 = (bf16[4,32,1024]{2,1,0:T(8,128)(2,1)}, bf16[4,32,1024]{2,1,0:T(8,128)(2,1)}, u32[]{:S(2)}, u32[]{:S(2)}) collective-permute-start(bf16[4,32,1024]{2,1,0:T(8,128)(2,1)} %get-tuple-element.506), channel_id=1, source_target_pairs={{0,3},{1,2},{2,1},{3,0},{4,7},{5,6},{6,5},{7,4},{8,11},{9,10},{10,... | collective-permute-start | bytes 786440 | tf_op jit(solution)/shard_map/ppermute | solution.py:572
  21.3 17.9 %collective-permute-start.1 = (bf16[4,32,1024]{2,1,0:T(8,128)(2,1)}, bf16[4,32,1024]{2,1,0:T(8,128)(2,1)}, u32[]{:S(2)}, u32[]{:S(2)}) collective-permute-start(bf16[4,32,1024]{2,1,0:T(8,128)(2,1)} %get-tuple-element.512), channel_id=1, source_target_pairs={{0,4},{1,5},{2,6},{3,7},{4,0},{5,1},{6,2},{7,3},{8,12},{9,13},{10,... | collective-permute-start | bytes 786440 | tf_op jit(solution)/shard_map/ppermute | solution.py:572
  48.5 29.7 %collective-permute-start.12 = (bf16[4,32,1024]{2,1,0:T(8,128)(2,1)S(1)}, bf16[4,32,1024]{2,1,0:T(8,128)(2,1)S(1)}, u32[]{:S(2)}, u32[]{:S(2)}) collective-permute-start(bf16[4,32,1024]{2,1,0:T(8,128)(2,1)S(1)} %get-tuple-element.256), channel_id=1, source_target_pairs={{0,5},{1,4},{2,7},{3,6},{4,1},{5,0},{6,3},{7,2},{8,13},{9,12},{10,... | collective-permute-start | bytes 786440 | tf_op jit(solution)/shard_map/ppermute | solution.py:572
  49.6 30.5 %collective-permute-start.13 = (bf16[4,32,1024]{2,1,0:T(8,128)(2,1)S(1)}, bf16[4,32,1024]{2,1,0:T(8,128)(2,1)}, u32[]{:S(2)}, u32[]{:S(2)}) collective-permute-start(bf16[4,32,1024]{2,1,0:T(8,128)(2,1)S(1)} %get-tuple-element.257), channel_id=1, source_target_pairs={{0,7},{1,6},{2,5},{3,4},{4,3},{5,2},{6,1},{7,0},{8,15},{9,14},{10,... | collective-permute-start | bytes 786440 | tf_op jit(solution)/shard_map/ppermute | solution.py:572
  50.1 30.0 %collective-permute-start.7 = (bf16[4,32,1024]{2,1,0:T(8,128)(2,1)}, bf16[4,32,1024]{2,1,0:T(8,128)(2,1)}, u32[]{:S(2)}, u32[]{:S(2)}) collective-permute-start(bf16[4,32,1024]{2,1,0:T(8,128)(2,1)} %get-tuple-element.251), channel_id=1, source_target_pairs={{0,2},{1,3},{2,0},{3,1},{4,6},{5,7},{6,4},{7,5},{8,10},{9,11},{10,... | collective-permute-start | bytes 786440 | tf_op jit(solution)/shard_map/ppermute | solution.py:572
  51.7 28.5 %collective-permute-start.8 = (bf16[4,32,1024]{2,1,0:T(8,128)(2,1)}, bf16[4,32,1024]{2,1,0:T(8,128)(2,1)}, u32[]{:S(2)}, u32[]{:S(2)}) collective-permute-start(bf16[4,32,1024]{2,1,0:T(8,128)(2,1)} %get-tuple-element.252), channel_id=1, source_target_pairs={{0,4},{1,5},{2,6},{3,7},{4,0},{5,1},{6,2},{7,3},{8,12},{9,13},{10,... | collective-permute-start | bytes 786440 | tf_op jit(solution)/shard_map/ppermute | solution.py:572
  55.4 24.7 %collective-permute-start.9 = (bf16[4,32,1024]{2,1,0:T(8,128)(2,1)}, bf16[4,32,1024]{2,1,0:T(8,128)(2,1)}, u32[]{:S(2)}, u32[]{:S(2)}) collective-permute-start(bf16[4,32,1024]{2,1,0:T(8,128)(2,1)} %get-tuple-element.253), channel_id=1, source_target_pairs={{0,6},{1,7},{2,4},{3,5},{4,2},{5,3},{6,0},{7,1},{8,14},{9,15},{10,... | collective-permute-start | bytes 786440 | tf_op jit(solution)/shard_map/ppermute | solution.py:572
  78.9 25.8 %collective-permute-start.14 = (bf16[4,2,128,1024]{3,2,1,0:T(8,128)(2,1)}, bf16[4,2,128,1024]{3,2,1,0:T(8,128)(2,1)}, u32[]{:S(2)}, u32[]{:S(2)}) collective-permute-start(bf16[4,2,128,1024]{3,2,1,0:T(8,128)(2,1)} %get-tuple-element.259), channel_id=1, source_target_pairs={{0,1},{1,0},{2,3},{3,2},{4,5},{5,4},{6,7},{7,6},{8,9},{9,8},{10,11... | collective-permute-start | bytes 6291464 | tf_op jit(solution)/shard_map/ppermute | solution.py:572
  101.2 50.2 %collective-permute-start.16 = (bf16[512,1024]{1,0:T(8,128)(2,1)S(1)}, bf16[512,1024]{1,0:T(8,128)(2,1)}, u32[]{:S(2)}, u32[]{:S(2)}) collective-permute-start(bf16[512,1024]{1,0:T(8,128)(2,1)S(1)} %bitcast.137), channel_id=1, source_target_pairs={{0,2},{1,3},{2,0},{3,1},{4,6},{5,7},{6,4},{7,5},{8,10},{9,11},{10,... | collective-permute-start | bytes 3145736 | tf_op jit(solution)/shard_map/ppermute | solution.py:572
  101.7 49.6 %collective-permute-start.17 = (bf16[512,1024]{1,0:T(8,128)(2,1)S(1)}, bf16[512,1024]{1,0:T(8,128)(2,1)}, u32[]{:S(2)}, u32[]{:S(2)}) collective-permute-start(bf16[512,1024]{1,0:T(8,128)(2,1)S(1)} %bitcast.136), channel_id=1, source_target_pairs={{0,4},{1,5},{2,6},{3,7},{4,0},{5,1},{6,2},{7,3},{8,12},{9,13},{10,... | collective-permute-start | bytes 3145736 | tf_op jit(solution)/shard_map/ppermute | solution.py:572
  102.2 49.2 %collective-permute-start.18 = (bf16[512,1024]{1,0:T(8,128)(2,1)S(1)}, bf16[512,1024]{1,0:T(8,128)(2,1)}, u32[]{:S(2)}, u32[]{:S(2)}) collective-permute-start(bf16[512,1024]{1,0:T(8,128)(2,1)S(1)} %bitcast.135), channel_id=1, source_target_pairs={{0,6},{1,7},{2,4},{3,5},{4,2},{5,3},{6,0},{7,1},{8,14},{9,15},{10,... | collective-permute-start | bytes 3145736 | tf_op jit(solution)/shard_map/ppermute | solution.py:572
  251.5 26.5 %collective-permute-start.19 = (bf16[512,1024]{1,0:T(8,128)(2,1)}, bf16[512,1024]{1,0:T(8,128)(2,1)S(1)}, u32[]{:S(2)}, u32[]{:S(2)}) collective-permute-start(bf16[512,1024]{1,0:T(8,128)(2,1)} %get-tuple-element.280), channel_id=1, source_target_pairs={{0,2},{1,3},{2,0},{3,1},{4,6},{5,7},{6,4},{7,5},{8,10},{9,11},{10,... | collective-permute-start | bytes 3145736 | tf_op jit(solution)/shard_map/ppermute | solution.py:572
  252.1 25.9 %collective-permute-start.20 = (bf16[512,1024]{1,0:T(8,128)(2,1)}, bf16[512,1024]{1,0:T(8,128)(2,1)S(1)}, u32[]{:S(2)}, u32[]{:S(2)}) collective-permute-start(bf16[512,1024]{1,0:T(8,128)(2,1)} %get-tuple-element.281), channel_id=1, source_target_pairs={{0,4},{1,5},{2,6},{3,7},{4,0},{5,1},{6,2},{7,3},{8,12},{9,13},{10,... | collective-permute-start | bytes 3145736 | tf_op jit(solution)/shard_map/ppermute | solution.py:572
  278.0 27.6 %collective-permute-start.21 = (bf16[16,64,2048]{2,1,0:T(8,128)(2,1)}, bf16[16,64,2048]{2,1,0:T(8,128)(2,1)}, u32[]{:S(2)}, u32[]{:S(2)}) collective-permute-start(bf16[16,64,2048]{2,1,0:T(8,128)(2,1)} %get-tuple-element.287), channel_id=1, source_target_pairs={{0,1},{1,0},{2,3},{3,2},{4,5},{5,4},{6,7},{7,6},{8,9},{9,8},{10,11... | collective-permute-start | bytes 12582920 | tf_op jit(solution)/shard_map/ppermute | solution.py:572
  278.1 27.5 %collective-permute-start.22 = (bf16[512,1024]{1,0:T(8,128)(2,1)}, bf16[512,1024]{1,0:T(8,128)(2,1)S(1)}, u32[]{:S(2)}, u32[]{:S(2)}) collective-permute-start(bf16[512,1024]{1,0:T(8,128)(2,1)} %get-tuple-element.291), channel_id=1, source_target_pairs={{0,6},{1,7},{2,4},{3,5},{4,2},{5,3},{6,0},{7,1},{8,14},{9,15},{10,... | collective-permute-start | bytes 3145736 | tf_op jit(solution)/shard_map/ppermute | solution.py:572
  305.6 55.4 %collective-permute-start.25 = (bf16[16,256,512]{2,1,0:T(8,128)(2,1)}, bf16[16,256,512]{2,1,0:T(8,128)(2,1)}, u32[]{:S(2)}, u32[]{:S(2)}) collective-permute-start(bf16[16,256,512]{2,1,0:T(8,128)(2,1)} %get-tuple-element.306), channel_id=1, source_target_pairs={{0,1},{1,0},{2,3},{3,2},{4,5},{5,4},{6,7},{7,6},{8,9},{9,8},{10,11... | collective-permute-start | bytes 12582920 | tf_op jit(solution)/shard_map/ppermute | solution.py:572
  309.7 51.2 %collective-permute-start.24 = (bf16[8,64,2048]{2,1,0:T(8,128)(2,1)}, bf16[8,64,2048]{2,1,0:T(8,128)(2,1)S(1)}, u32[]{:S(2)}, u32[]{:S(2)}) collective-permute-start(bf16[8,64,2048]{2,1,0:T(8,128)(2,1)} %add_convert_fusion.2), channel_id=1, source_target_pairs={{0,2},{1,3},{2,0},{3,1},{4,6},{5,7},{6,4},{7,5},{8,10},{9,11},{10,... | collective-permute-start | bytes 6291464 | tf_op jit(solution)/shard_map/ppermute | solution.py:572
  369.2 233.2 %reduce-scatter.5.cloned.1.call-start = ((), (), s32[]{:S(2)}) async-start(), calls=%async_computation.3 | async-start | bytes 5242880 | tf_op jit(solution)/shard_map/reduce_scatter | solution.py:650
  369.4 34.4 %collective-permute-start.23 = (bf16[8,128,1024]{2,1,0:T(8,128)(2,1)}, bf16[8,128,1024]{2,1,0:T(8,128)(2,1)}, u32[]{:S(2)}, u32[]{:S(2)}) collective-permute-start(bf16[8,128,1024]{2,1,0:T(8,128)(2,1)} %get-tuple-element.298), channel_id=1, source_target_pairs={{0,1},{1,0},{2,3},{3,2},{4,5},{5,4},{6,7},{7,6},{8,9},{9,8},{10,11... | collective-permute-start | bytes 6291464 | tf_op jit(solution)/shard_map/ppermute | solution.py:572
  375.1 28.6 %collective-permute-start.26 = (bf16[4,64,2048]{2,1,0:T(8,128)(2,1)}, bf16[4,64,2048]{2,1,0:T(8,128)(2,1)S(1)}, u32[]{:S(2)}, u32[]{:S(2)}) collective-permute-start(bf16[4,64,2048]{2,1,0:T(8,128)(2,1)} %get-tuple-element.465), channel_id=1, source_target_pairs={{0,4},{1,5},{2,6},{3,7},{4,0},{5,1},{6,2},{7,3},{8,12},{9,13},{10,... | collective-permute-start | bytes 3145736 | tf_op jit(solution)/shard_map/ppermute | solution.py:572
  403.8 40.8 %collective-permute-start.27 = (bf16[16,64,2048]{2,1,0:T(8,128)(2,1)}, bf16[16,64,2048]{2,1,0:T(8,128)(2,1)}, u32[]{:S(2)}, u32[]{:S(2)}) collective-permute-start(bf16[16,64,2048]{2,1,0:T(8,128)(2,1)} %get-tuple-element.329), channel_id=1, source_target_pairs={{0,1},{1,0},{2,3},{3,2},{4,5},{5,4},{6,7},{7,6},{8,9},{9,8},{10,11... | collective-permute-start | bytes 12582920 | tf_op jit(solution)/shard_map/ppermute | solution.py:572
  405.0 39.5 %collective-permute-start.28 = (bf16[2,64,2048]{2,1,0:T(8,128)(2,1)S(1)}, bf16[2,64,2048]{2,1,0:T(8,128)(2,1)S(1)}, u32[]{:S(2)}, u32[]{:S(2)}) collective-permute-start(bf16[2,64,2048]{2,1,0:T(8,128)(2,1)S(1)} %get-tuple-element.483), channel_id=1, source_target_pairs={{0,8},{8,0},{16,24},{24,16},{1,9},{9,1},{17,25},{25,17},{2,10},{10... | collective-permute-start | bytes 1572872 | tf_op jit(solution)/shard_map/ppermute | solution.py:572
  444.7 44.2 %collective-permute-start.32 = (bf16[1,64,2048]{2,1,0:T(8,128)(2,1)S(1)}, bf16[1,64,2048]{2,1,0:T(8,128)(2,1)S(1)}, u32[]{:S(2)}, u32[]{:S(2)}) collective-permute-start(bf16[1,64,2048]{2,1,0:T(8,128)(2,1)S(1)} %get-tuple-element.499), channel_id=1, source_target_pairs={{0,16},{8,24},{16,0},{24,8},{1,17},{9,25},{17,1},{25,9},{2,18},{10... | collective-permute-start | bytes 786440 | tf_op jit(solution)/shard_map/ppermute | solution.py:572
  444.8 44.1 %collective-permute-start.29 = (bf16[2,4,32,1024]{3,2,1,0:T(8,128)(2,1)}, bf16[2,4,32,1024]{3,2,1,0:T(8,128)(2,1)S(1)}, u32[]{:S(2)}, u32[]{:S(2)}) collective-permute-start(bf16[2,4,32,1024]{3,2,1,0:T(8,128)(2,1)} %get-tuple-element.336), channel_id=1, source_target_pairs={{0,2},{1,3},{2,0},{3,1},{4,6},{5,7},{6,4},{7,5},{8,10},{9,11},{10,... | collective-permute-start | bytes 1572872 | tf_op jit(solution)/shard_map/ppermute | solution.py:572
  444.8 44.1 %collective-permute-start.30 = (bf16[2,4,32,1024]{3,2,1,0:T(8,128)(2,1)}, bf16[2,4,32,1024]{3,2,1,0:T(8,128)(2,1)S(1)}, u32[]{:S(2)}, u32[]{:S(2)}) collective-permute-start(bf16[2,4,32,1024]{3,2,1,0:T(8,128)(2,1)} %get-tuple-element.337), channel_id=1, source_target_pairs={{0,4},{1,5},{2,6},{3,7},{4,0},{5,1},{6,2},{7,3},{8,12},{9,13},{10,... | collective-permute-start | bytes 1572872 | tf_op jit(solution)/shard_map/ppermute | solution.py:572
  446.0 42.9 %collective-permute-start.31 = (bf16[2,4,32,1024]{3,2,1,0:T(8,128)(2,1)}, bf16[2,4,32,1024]{3,2,1,0:T(8,128)(2,1)S(1)}, u32[]{:S(2)}, u32[]{:S(2)}) collective-permute-start(bf16[2,4,32,1024]{3,2,1,0:T(8,128)(2,1)} %get-tuple-element.338), channel_id=1, source_target_pairs={{0,6},{1,7},{2,4},{3,5},{4,2},{5,3},{6,0},{7,1},{8,14},{9,15},{10,... | collective-permute-start | bytes 1572872 | tf_op jit(solution)/shard_map/ppermute | solution.py:572
  491.1 37.8 %collective-permute-start.35 = (bf16[4,4,32,1024]{3,2,1,0:T(8,128)(2,1)}, bf16[4,4,32,1024]{3,2,1,0:T(8,128)(2,1)S(1)}, u32[]{:S(2)}, u32[]{:S(2)}) collective-permute-start(bf16[4,4,32,1024]{3,2,1,0:T(8,128)(2,1)} %pad_maximum_fusion), channel_id=1, source_target_pairs={{0,1},{1,0},{2,3},{3,2},{4,5},{5,4},{6,7},{7,6},{8,9},{9,8},{10,11... | collective-permute-start | bytes 3145736 | tf_op jit(solution)/shard_map/ppermute | solution.py:572
  492.7 33.0 %collective-permute-start.34 = (bf16[2,256,512]{2,1,0:T(8,128)(2,1)}, bf16[2,256,512]{2,1,0:T(8,128)(2,1)}, u32[]{:S(2)}, u32[]{:S(2)}) collective-permute-start(bf16[2,256,512]{2,1,0:T(8,128)(2,1)} %get-tuple-element.497), channel_id=1, source_target_pairs={{0,2},{1,3},{2,0},{3,1},{4,6},{5,7},{6,4},{7,5},{8,10},{9,11},{10,... | collective-permute-start | bytes 1572872 | tf_op jit(solution)/shard_map/ppermute | solution.py:572
  493.0 32.7 %collective-permute-start.36 = (bf16[2,4,32,1024]{3,2,1,0:T(8,128)(2,1)}, bf16[2,4,32,1024]{3,2,1,0:T(8,128)(2,1)S(1)}, u32[]{:S(2)}, u32[]{:S(2)}) collective-permute-start(bf16[2,4,32,1024]{3,2,1,0:T(8,128)(2,1)} %get-tuple-element.378), channel_id=1, source_target_pairs={{0,2},{1,3},{2,0},{3,1},{4,6},{5,7},{6,4},{7,5},{8,10},{9,11},{10,... | collective-permute-start | bytes 1572872 | tf_op jit(solution)/shard_map/ppermute | solution.py:572
  494.7 31.0 %collective-permute-start.37 = (bf16[2,4,32,1024]{3,2,1,0:T(8,128)(2,1)}, bf16[2,4,32,1024]{3,2,1,0:T(8,128)(2,1)S(1)}, u32[]{:S(2)}, u32[]{:S(2)}) collective-permute-start(bf16[2,4,32,1024]{3,2,1,0:T(8,128)(2,1)} %get-tuple-element.379), channel_id=1, source_target_pairs={{0,4},{1,5},{2,6},{3,7},{4,0},{5,1},{6,2},{7,3},{8,12},{9,13},{10,... | collective-permute-start | bytes 1572872 | tf_op jit(solution)/shard_map/ppermute | solution.py:572
  494.9 34.0 %collective-permute-start.38 = (bf16[2,4,32,1024]{3,2,1,0:T(8,128)(2,1)}, bf16[2,4,32,1024]{3,2,1,0:T(8,128)(2,1)}, u32[]{:S(2)}, u32[]{:S(2)}) collective-permute-start(bf16[2,4,32,1024]{3,2,1,0:T(8,128)(2,1)} %get-tuple-element.380), channel_id=1, source_target_pairs={{0,6},{1,7},{2,4},{3,5},{4,2},{5,3},{6,0},{7,1},{8,14},{9,15},{10,... | collective-permute-start | bytes 1572872 | tf_op jit(solution)/shard_map/ppermute | solution.py:572
  533.8 38.8 %collective-permute-start.46 = (bf16[4,4,32,1024]{3,2,1,0:T(8,128)(2,1)}, bf16[4,4,32,1024]{3,2,1,0:T(8,128)(2,1)S(1)}, u32[]{:S(2)}, u32[]{:S(2)}) collective-permute-start(bf16[4,4,32,1024]{3,2,1,0:T(8,128)(2,1)} %pad_maximum_fusion.1), channel_id=1, source_target_pairs={{0,1},{1,0},{2,3},{3,2},{4,5},{5,4},{6,7},{7,6},{8,9},{9,8},{10,11... | collective-permute-start | bytes 3145736 | tf_op jit(solution)/shard_map/ppermute | solution.py:572
  541.7 32.4 %collective-permute-start.43 = (bf16[8,64,1024]{2,1,0:T(8,128)(2,1)S(1)}, bf16[8,64,1024]{2,1,0:T(8,128)(2,1)S(1)}, u32[]{:S(2)}, u32[]{:S(2)}) collective-permute-start(bf16[8,64,1024]{2,1,0:T(8,128)(2,1)S(1)} %add_convert_fusion.3), channel_id=1, source_target_pairs={{0,4},{1,5},{2,6},{3,7},{4,0},{5,1},{6,2},{7,3},{8,12},{9,13},{10,... | collective-permute-start | bytes 3145736 | tf_op jit(solution)/shard_map/ppermute | solution.py:572
  545.6 28.5 %collective-permute-start.42 = (bf16[8,64,1024]{2,1,0:T(8,128)(2,1)S(1)}, bf16[8,64,1024]{2,1,0:T(8,128)(2,1)S(1)}, u32[]{:S(2)}, u32[]{:S(2)}) collective-permute-start(bf16[8,64,1024]{2,1,0:T(8,128)(2,1)S(1)} %add_convert_fusion.4), channel_id=1, source_target_pairs={{0,2},{1,3},{2,0},{3,1},{4,6},{5,7},{6,4},{7,5},{8,10},{9,11},{10,... | collective-permute-start | bytes 3145736 | tf_op jit(solution)/shard_map/ppermute | solution.py:572
  547.1 25.6 %collective-permute-start.45 = (bf16[1,256,512]{2,1,0:T(8,128)(2,1)S(1)}, bf16[1,256,512]{2,1,0:T(8,128)(2,1)S(1)}, u32[]{:S(2)}, u32[]{:S(2)}) collective-permute-start(bf16[1,256,512]{2,1,0:T(8,128)(2,1)S(1)} %get-tuple-element.495), channel_id=1, source_target_pairs={{0,4},{1,5},{2,6},{3,7},{4,0},{5,1},{6,2},{7,3},{8,12},{9,13},{10,... | collective-permute-start | bytes 786440 | tf_op jit(solution)/shard_map/ppermute | solution.py:572
  549.2 24.8 %collective-permute-start.44 = (f32[36,1024]{1,0:T(8,128)S(1)}, f32[36,1024]{1,0:T(8,128)S(1)}, u32[]{:S(2)}, u32[]{:S(2)}) collective-permute-start(f32[36,1024]{1,0:T(8,128)S(1)} %add.504), channel_id=1, source_target_pairs={{0,2},{1,3},{2,0},{3,1},{4,6},{5,7},{6,4},{7,5},{8,10},{9,11},{10,... | collective-permute-start | bytes 442376 | tf_op jit(solution)/shard_map/ppermute | solution.py:572
  576.7 19.2 %collective-permute-start.48 = (bf16[4,64,1024]{2,1,0:T(8,128)(2,1)}, bf16[4,64,1024]{2,1,0:T(8,128)(2,1)}, u32[]{:S(2)}, u32[]{:S(2)}) collective-permute-start(bf16[4,64,1024]{2,1,0:T(8,128)(2,1)} %get-tuple-element.467), channel_id=1, source_target_pairs={{0,2},{1,3},{2,0},{3,1},{4,6},{5,7},{6,4},{7,5},{8,10},{9,11},{10,... | collective-permute-start | bytes 1572872 | tf_op jit(solution)/shard_map/ppermute | solution.py:572
  579.6 16.3 %collective-permute-start.47 = (bf16[4,64,1024]{2,1,0:T(8,128)(2,1)}, bf16[4,64,1024]{2,1,0:T(8,128)(2,1)S(1)}, u32[]{:S(2)}, u32[]{:S(2)}) collective-permute-start(bf16[4,64,1024]{2,1,0:T(8,128)(2,1)} %get-tuple-element.469), channel_id=1, source_target_pairs={{0,4},{1,5},{2,6},{3,7},{4,0},{5,1},{6,2},{7,3},{8,12},{9,13},{10,... | collective-permute-start | bytes 1572872 | tf_op jit(solution)/shard_map/ppermute | solution.py:572
  580.7 15.2 %collective-permute-start.49 = (f32[36,1024]{1,0:T(8,128)S(1)}, f32[36,1024]{1,0:T(8,128)S(1)}, u32[]{:S(2)}, u32[]{:S(2)}) collective-permute-start(f32[36,1024]{1,0:T(8,128)S(1)} %add.515), channel_id=1, source_target_pairs={{0,4},{1,5},{2,6},{3,7},{4,0},{5,1},{6,2},{7,3},{8,12},{9,13},{10,... | collective-permute-start | bytes 442376 | tf_op jit(solution)/shard_map/ppermute | solution.py:572
  598.8 17.0 %collective-permute-start.50 = (bf16[2,64,2048]{2,1,0:T(8,128)(2,1)}, bf16[2,64,2048]{2,1,0:T(8,128)(2,1)S(1)}, u32[]{:S(2)}, u32[]{:S(2)}) collective-permute-start(bf16[2,64,2048]{2,1,0:T(8,128)(2,1)} %pad_maximum_fusion.3), channel_id=1, source_target_pairs={{0,8},{8,0},{16,24},{24,16},{1,9},{9,1},{17,25},{25,17},{2,10},{10... | collective-permute-start | bytes 1572872 | tf_op jit(solution)/shard_map/ppermute | solution.py:572
  605.0 16.9 %collective-permute-start.58 = (bf16[128,512]{1,0:T(8,128)(2,1)S(1)}, bf16[128,512]{1,0:T(8,128)(2,1)S(1)}, u32[]{:S(2)}, u32[]{:S(2)}) collective-permute-start(bf16[128,512]{1,0:T(8,128)(2,1)S(1)} %fusion.6), channel_id=1, source_target_pairs={{0,1},{1,0},{2,3},{3,2},{4,5},{5,4},{6,7},{7,6},{8,9},{9,8},{10,11... | collective-permute-start | bytes 393224 | tf_op jit(solution)/shard_map/ppermute | solution.py:572
  616.0 20.5 %collective-permute-start.55 = (bf16[1,64,2048]{2,1,0:T(8,128)(2,1)S(1)}, bf16[1,64,2048]{2,1,0:T(8,128)(2,1)S(1)}, u32[]{:S(2)}, u32[]{:S(2)}) collective-permute-start(bf16[1,64,2048]{2,1,0:T(8,128)(2,1)S(1)} %get-tuple-element.485), channel_id=1, source_target_pairs={{0,2},{1,3},{2,0},{3,1},{4,6},{5,7},{6,4},{7,5},{8,10},{9,11},{10,... | collective-permute-start | bytes 786440 | tf_op jit(solution)/shard_map/ppermute | solution.py:572
  617.9 18.6 %collective-permute-start.53 = (bf16[1,64,2048]{2,1,0:T(8,128)(2,1)S(1)}, bf16[1,64,2048]{2,1,0:T(8,128)(2,1)S(1)}, u32[]{:S(2)}, u32[]{:S(2)}) collective-permute-start(bf16[1,64,2048]{2,1,0:T(8,128)(2,1)S(1)} %get-tuple-element.487), channel_id=1, source_target_pairs={{0,16},{8,24},{16,0},{24,8},{1,17},{9,25},{17,1},{25,9},{2,18},{10... | collective-permute-start | bytes 786440 | tf_op jit(solution)/shard_map/ppermute | solution.py:572
  619.9 16.6 %collective-permute-start.54 = (f32[36,1024]{1,0:T(8,128)S(1)}, f32[36,1024]{1,0:T(8,128)S(1)}, u32[]{:S(2)}, u32[]{:S(2)}) collective-permute-start(f32[36,1024]{1,0:T(8,128)S(1)} %add.522), channel_id=1, source_target_pairs={{0,16},{8,24},{16,0},{24,8},{1,17},{9,25},{17,1},{25,9},{2,18},{10... | collective-permute-start | bytes 442376 | tf_op jit(solution)/shard_map/ppermute | solution.py:572
  (47 other events, 644.2 us)
Sparse Core Ops, SparseCore 0:
  369.3 93.5 reduce-scatter.2
  465.3 77.4 reduce-scatter.4
where the time goes:
time: 657 us; the launch traced here: 650 us
  Pallas kernels  424 us (65%)
  waiting for transfers between devices  70 us (11%)
  starting transfers between devices  55.5 us (8%)
  other arithmetic  53.8 us (8%)
  local copies, waits for them, and re-layouts  29.9 us (5%)
  between operations  15.6 us (2%)
    pallas_call x13, Pallas kernels, call(): pl.pallas_call(kernel, grid_spec=pltpu.PrefetchScalarGridSpec(num_scalar_...  424 us
    ppermute x59, waiting for transfers between devices, swap(): return lax.ppermute(value, axis, [(i, i ^ k) for i in range(size)])  69.9 us
    ppermute x59, starting transfers between devices, swap(): return lax.ppermute(value, axis, [(i, i ^ k) for i in range(size)])  55.2 us
    convert_element_type x15, other arithmetic, add(): return sum((value.astype(F32) for value in values)).astype(kind)  35.5 us
  transfers between devices with their start and end apart: 61, of which 11 were waited for; matrix products, arithmetic and copies ran while one was open for 10% of the time, Pallas kernels for 50%

commit v1 on v0

--- a/solution.py
+++ b/solution.py
@@ -321,7 +321,26 @@
     return jax.ShapeDtypeStruct(shape, kind)
 
 
-def call(kernel, grid, operands, outs, scratch=(), flops=0, meta=None):
+def call(kernel, grid, operands, outs, scratch=(), flops=0, meta=None, sums=()):
+    if sums:
+        own, reads, makes, lead = kernel, len(operands), len(outs), meta is not None
+        operands, outs = list(operands), list(outs)
+        for arrays in sums:
+            length = min(array.shape[0] for array in arrays)
+            block = (length // grid[0],) + arrays[0].shape[1:]
+            index = lambda i, *_, rank=arrays[0].ndim: (i,) + (0,) * (rank - 1)
+            operands += [(array, block, index) for array in arrays]
+            outs.append(((length,) + arrays[0].shape[1:], BF16, block, index))
+        ends = lead + len(operands), lead + len(operands) + len(outs)
+
+        def kernel(*refs):
+            made = refs[ends[0] : ends[1]]
+            own(*refs[: lead + reads], *made[:makes], *refs[ends[1] :])
+            terms = refs[lead + reads : ends[0]]
+            for arrays, out in zip(sums, made[makes:]):
+                out[...] = sum(term[...].astype(F32) for term in terms[: len(arrays)]).astype(BF16)
+                terms = terms[len(arrays) :]
+
     in_specs = [
         whole(array) if block is None else pl.BlockSpec(block, index)
         for array, block, index in operands
@@ -454,7 +473,7 @@
                 put(own, slot, held[pl.ds(source, size), :])
 
 
-def columns_grad(pairs, meta, split, tile=512):
+def columns_grad(pairs, meta, split, tile=512, sums=()):
     shares = len(split)
     blocks = (meta.shape[0] - 1) // shares
     height = pairs[0][0][0].shape[1]
@@ -487,7 +506,7 @@
         *refs, counts=[len(lefts) for lefts, _ in pairs], firsts=firsts, blocks=blocks, split=split
     )
     scratch = [pltpu.VMEM((height, tile), BF16)]
-    return call(kernel, (2 * firsts[-1],), operands, outs, scratch, flops, meta)
+    return call(kernel, (2 * firsts[-1],), operands, outs, scratch, flops, meta, sums)
 
 
 def rows_kernel(meta, *refs, step_blocks, steps, blocks):
@@ -636,10 +655,20 @@
                 landed.append([[(parts[0], False), (came, True)], add([parts[1], sent], BF16)])
         return chains, landed, 0
 
+    def addends(departed):
+        (chains, parts, at), coming = departed
+        return [value for value, _ in parts[0][0]] + coming
+
+    def arrived(departed, total):
+        chains, parts, at = departed[0]
+        hops = chains[0]
+        pieces = halves(total, hops[at + 1] if at + 1 < len(hops) else None)
+        return chains, [[[(total, len(pieces) == 2)]] + pieces[1:]], at + 1
+
     def merge(state):
         chains, parts, at = state
         kept = jnp.concatenate([own[0][0][0] for own in parts], -1)
-        return chains[:1], [[[(kept, False)], jnp.concatenate([own[1] for own in parts], -1)]], at
+        return chains[:1], [[[(kept, False)]]], at
 
     def depart(state):
         chains, parts, at = state
@@ -700,7 +729,8 @@
     other_way = one_way[::-1]
     clip_bits = [("clip", 1 << b) for b in range(layers.bit_length() - 1)]
     up_chains, down_chains = [one_way + clip_bits], [["scatter"] + one_way]
-    time_chains, space_chains = [["scatter"] + other_way], [one_way + clip_bits, other_way + clip_bits]
+    time_chains = [["scatter"] + other_way]
+    space_chains = [one_way + ["spread"], other_way + ["spread"]]
 
     order = [k for j in range(group) for k in range(j, n, group)]
     onehot = (action_ids[..., None] == lax.iota(jnp.int32, action_table.shape[0])).astype(F32)
@@ -934,13 +964,19 @@
         flops=2 * rows * width * 4 * width + 40 * rows * sub * head_flops,
     )
     grad_packed_two, up, down = hold_parts(grad_packed_two, up, down)
-    up, down = depart(arrive(up)), depart(land(down))
     r1_parts = [r1 if j == 0 else swap(r1, j) for j, r1 in enumerate(r1_parts)]
+    extra = []
 
     def make_time(meta, split):
-        return columns_grad([([a2], [grad_packed_two]), ([o2], [r2_low])], meta, split)
+        pairs = [([a2], [grad_packed_two]), ([o2], [r2_low])]
+        beside = [[down[1][0][0], down[2][0]], addends(up)]
+        *made, down_total, up_total = columns_grad(pairs, meta, split, sums=beside)
+        extra.extend((down_total, up_total))
+        return made
 
     time = begin(make_time, time_chains, tables["time"])
+    down = down[0], [[[(extra[0], False)]]], 0
+    up = arrived(up, extra[1])
 
     dealt = 1 if p % 16 else n
 
@@ -958,7 +994,7 @@
     def operand(found, block, index):
         return found[0], (None,) + block, lambda *i: (found[1],) + index(*i)
 
-    def space_back(c, earlier):
+    def space_back(c, earlier, sums=()):
         packed, _, total = space[c]
         return call(
             lambda *refs: space_back_kernel(kinds, group, order, *refs),
@@ -992,25 +1028,27 @@
             [pltpu.VMEM((grid_all, width), BF16)],
             flops=2 * span * grid_all * width * 4 * width
             + 40 * span * grid_all * grid_all * head_flops,
+            sums=sums,
         )
 
-    r1_parts, time, up = hold_parts(r1_parts, time, up)
-    up, time = depart(arrive(up)), cross(time)
+    r1_parts, time, up, down = hold_parts(r1_parts, time, up, down)
+    up, down, time = depart(up), depart(down), cross(time)
     early = jnp.concatenate([sums_two, sums_three, bias_up.reshape(-1, width)], 0)
     back = [space_back(0, jnp.zeros((8 + action_table.shape[0], width), F32))]
     back[0], r1_parts, time, up = hold_parts(back[0], r1_parts, time, up)
     input_pieces = [send_back(back[0][4:])]
-    up, time = depart(arrive(up)), depart(land(time))
+    up = depart(arrive(up))
     for c in range(1, chunks):
-        back.append(space_back(c, back[-1][3]))
-    back, input_pieces, up, down = hold_parts(back, input_pieces, up, down)
+        beside = [[time[1][0][0], time[2][0]]] if c == 1 else []
+        back.append(space_back(c, back[-1][3], beside))
+        if c == 1:
+            *back[c], time_total = back[c]
+    time = time[0], [[[(time_total, False)]]], 0
+    back, input_pieces, up, time = hold_parts(back, input_pieces, up, time)
     input_pieces[0] = pass_on(input_pieces[0])
     for c in range(1, chunks):
         input_pieces.append(send_back(back[c][4:]))
-    up = arrive(up)
-    while up[2] < len(up[0][0]):
-        up = arrive(depart(up))
-    up, down = last_swap(up), depart(arrive(down))
+    up, time = depart(arrive(up)), depart(time)
     grads_one, a1s, r1s = list(zip(*back))[:3]
 
     def flat(values):
@@ -1035,7 +1073,10 @@
     )
     space_sum = cross(space_sum)
     small_came = swap(small, small_hops[0][1], small_hops[0][0])
-    down = depart(arrive(down))
+    up = arrive(up)
+    while up[2] < len(up[0][0]):
+        up = arrive(depart(up))
+    up, down = last_swap(up), depart(arrive(down))
     result_out = collect_result(result_pieces, where_clip)
     space_sum, result_out, small_came = hold_parts(space_sum, result_out, small_came)
     space_sum, small = land(space_sum), small + small_came
@@ -1056,9 +1097,9 @@
             input_grad = input_grad.reshape(tokens.shape)
         return input_grad
 
-    rounds = max(len(small_hops) - 1, len(space_sum[0][0]) + 1, 2 * len(one_way))
+    rounds = max(len(small_hops) - 1, len(space_sum[0][0]) + 1, 2 * len(one_way) + 1)
     for r in range(rounds):
-        departed = small_came = time_moves = None
+        departed = small_came = time_moves = down_moves = None
         if r < len(space_sum[0][0]):
             if r == len(one_way):
                 space_sum = merge(space_sum)
@@ -1067,25 +1108,28 @@
             small_came = swap(small, small_hops[r + 1][1], small_hops[r + 1][0])
         if r >= len(one_way) and time[2] < len(time[0][0]):
             time_moves = depart(time)
-        others = [down, input_pieces] if r == 0 else []
+        if r > len(one_way) and down[2] < len(down[0][0]):
+            down_moves = depart(down)
+        others = [down, input_pieces, up] if r == 0 else []
         if r == 1:
             input_grad = collect_input(input_pieces, where_chip)
             others = [input_grad]
-        departed, small_came, time_moves, *others = hold_parts(
-            departed, small_came, time_moves, *others
+        departed, small_came, time_moves, down_moves, *others = hold_parts(
+            departed, small_came, time_moves, down_moves, *others
         )
         if r == 0:
-            down, input_pieces = others
+            down, input_pieces, up = others
             down = arrive(down)
-            while down[2] < len(down[0][0]):
-                down = arrive(depart(down))
-            down = last_swap(down)
         if r == 1:
             (input_grad,) = others
         if time_moves is not None:
             time = arrive(time_moves)
             if time[2] == len(time[0][0]):
                 time_last = last_swap(time)
+        if down_moves is not None:
+            down = arrive(down_moves)
+            if down[2] == len(down[0][0]):
+                down_last = last_swap(down)
         if departed is not None:
             space_sum = arrive(departed)
         if small_came is not None:
@@ -1094,7 +1138,7 @@
             space_last = last_swap(space_sum)
     at = 8 + action_table.shape[0]
     sums = small[at:]
-    (down_out,) = join(*down, [width])
+    (down_out,) = join(*down_last, [width])
     (up_out,) = join(*up, [hidden])
     time_qkv, time_out = join(*time_last, [3 * width, width])
     space_qkv, space_out = join(*space_last, [3 * width, width])

time: 657 us -> 644 us (0.980)
  other arithmetic: 53.8 us -> 36.4 us
  waiting for transfers between devices: 70 us -> 60.6 us
  Pallas kernels: 424 us -> 432 us
    convert_element_type x15 -> x11, other arithmetic: 35.5 us -> 20.7 us  [add(): return sum((value.astype(F32) for value in values)).astype(kind)]
    ppermute x59 -> x60, waiting for transfers between devices: 69.9 us -> 60.5 us  [swap(): return lax.ppermute(value, axis, [(i, i ^ k) for i in range(size)])]
    pallas_call x13, Pallas kernels: 424 us -> 432 us  [call(): pl.pallas_call(kernel, grid_spec=pltpu.PrefetchScalarGridSpec(num_scalar_...]
    ppermute x59 -> x60, starting transfers between devices: 55.2 us -> 59 us  [swap(): return lax.ppermute(value, axis, [(i, i ^ k) for i in range(size)])]
  transfers between devices with their start and end apart: 61 -> 62, of which waited for: 11 -> 9; matrix products, arithmetic and copies ran while one was open for 10% -> 9% of each run, Pallas kernels for 50% -> 52%
where the time goes in v1:
time: 644 us; the launch traced here: 636 us
  Pallas kernels  432 us (67%)
  waiting for transfers between devices  60.6 us (9%)
  starting transfers between devices  59.1 us (9%)
  other arithmetic  36.4 us (6%)
  local copies, waits for them, and re-layouts  32 us (5%)
  between operations  15.6 us (2%)
    pallas_call x13, Pallas kernels, call(): pl.pallas_call(kernel, grid_spec=pltpu.PrefetchScalarGridSpec(num_scalar_...  432 us
    ppermute x60, waiting for transfers between devices, swap(): return lax.ppermute(value, axis, [(i, i ^ k) for i in range(size)])  60.5 us
    ppermute x60, starting transfers between devices, swap(): return lax.ppermute(value, axis, [(i, i ^ k) for i in range(size)])  59 us
    convert_element_type x11, other arithmetic, add(): return sum((value.astype(F32) for value in values)).astype(kind)  20.7 us
  transfers between devices with their start and end apart: 62, of which 9 were waited for; matrix products, arithmetic and copies ran while one was open for 9% of the time, Pallas kernels for 52%

profile of v1, /device:TPU:0, one launch (start us, length us, event | category | flops | bytes accessed | tf_op | source)
XLA Modules:
  0.0 635.8 jit_solution(18442264040600789491)
XLA Ops:
  8.2 2.5 broadcast_select_fusion
  12.7 2.4 collective-permute-start.5
  15.9 1.7 collective-permute-start.6
  21.3 2.1 collective-permute-start.1
  27.4 4.2 constant_dynamic-slice_fusion.2
  33.0 1.4 collective-permute-start.2
  39.3 4.2 collective-permute-done.2.refs_3_
  43.4 3.3 collective-permute-done.refs_1_
  46.7 1.7 collective-permute-start.11
  50.1 1.6 collective-permute-start.7
  51.6 1.5 collective-permute-start.8
  53.2 2.2 collective-permute-done.11.refs_5_
  56.1 2.0 collective-permute-start.9
  58.2 20.7 %shard_map.212 = (bf16[4,256,3072]{2,1,0:T(8,128)(2,1)}, bf16[4,256,1024]{2,1,0:T(8,128)(2,1)}, f32[4,16,256]{2,1,0:T(8,128)}, bf16[4,2,128,1024]{3,2,1,0:T(8,128)(2,1)}, bf16[4,2,128,1024]{3,2,1,0:T(8,128)(2,1)}) custom-call(bf16[4,32,1024]{2,1,0:T(8,128)(2,1)} %get-tuple-element.247.refs_0_, bf16[4,32,1024]{2,1,0:T(8,128)(2,1)} %collective-permute-done.refs_1_, ...), custom_call_target="tpu_custom_call" | custom-call | flops 15032385536 | bytes 16908288 | tf_op jit(solution)/shard_map/pallas_call | solution.py:355
  80.9 20.9 %shard_map.213 = (bf16[4,256,3072]{2,1,0:T(8,128)(2,1)}, bf16[4,256,1024]{2,1,0:T(8,128)(2,1)}, f32[4,16,256]{2,1,0:T(8,128)}, bf16[4,2,128,1024]{3,2,1,0:T(8,128)(2,1)}, bf16[4,2,128,1024]{3,2,1,0:T(8,128)(2,1)}) custom-call(bf16[4,32,1024]{2,1,0:T(8,128)(2,1)} %get-tuple-element.257.refs_0_, bf16[4,32,1024]{2,1,0:T(8,128)(2,1)} %collective-permute-done.7.refs_1_, ...), custom_call_target="tpu_custom_call" | custom-call | flops 15032385536 | bytes 16908288 | tf_op jit(solution)/shard_map/pallas_call | solution.py:355
  102.9 2.5 collective-permute-start.18
  106.3 45.7 %shard_map.214 = (f32[2048,1024]{1,0:T(8,128)}, f32[2048,1024]{1,0:T(8,128)}, bf16[2048,1024]{1,0:T(8,128)(2,1)}, bf16[2048,3072]{1,0:T(8,128)(2,1)}, bf16[2048,1024]{1,0:T(8,128)(2,1)}, /*index=5*/f32[16,2048]{1,0:T(8,128)}) custom-call(bf16[4,2,128,1024]{3,2,1,0:T(8,128)(2,1)} %get-tuple-element.256.refs_0_.refs_4_, ...), custom_call_target="tpu_custom_call" | custom-call | flops 30064771072 | bytes 55115776 | tf_op jit(solution)/shard_map/pallas_call | solution.py:355
  152.1 100.1 %shard_map.215 = (bf16[512,1024]{1,0:T(8,128)(2,1)}, bf16[512,1024]{1,0:T(8,128)(2,1)}, bf16[512,1024]{1,0:T(8,128)(2,1)}, bf16[512,1024]{1,0:T(8,128)(2,1)}, bf...) custom-call(f32[2048,1024]{1,0:T(8,128)} %get-tuple-element.271.refs, ...), custom_call_target="tpu_custom_call" | custom-call | flops 68719476736 | bytes 58818560 | tf_op jit(solution)/shard_map/pallas_call | solution.py:355
  253.2 25.4 %shard_map.216 = (bf16[16,64,2048]{2,1,0:T(8,128)(2,1)}, bf16[8,64,2048]{2,1,0:T(8,128)(2,1)}, bf16[8,64,2048]{2,1,0:T(8,128)(2,1)}) custom-call(s32[17]{0:T(128)} %concatenate.60.refs_0_, bf16[2048,1024]{1,0:T(8,128)(2,1)} %get-tuple-element.281.refs_1_, bf16[2048,4096]{1,0:T(8,128)(2,1)} %get-tuple-element.282.refs_2_), custom_call_target="tpu_custom_call" | custom-call | flops 17179869184 | bytes 41943040 | tf_op jit(solution)/shard_map/pallas_call | solution.py:355
  278.8 2.6 collective-permute-start.22
  281.4 24.9 %shard_map.217 = (bf16[16,256,512]{2,1,0:T(8,128)(2,1)}, bf16[16,256,512]{2,1,0:T(8,128)(2,1)}) custom-call(s32[17]{0:T(128)} %concatenate.57.refs_0_, bf16[2048,4096]{1,0:T(8,128)(2,1)} %get-tuple-element.278.refs_1_.refs_2_, bf16[2048,4096]{1,0:T(8,128)(2,1)} %get-tuple-element.278.refs_1_.refs_2_, bf16[2048,1024]{1,0:T(8,128)(2,1)} %get-tuple-element.289.refs_3_), custom_call_target="tpu_custom_call" | custom-call | flops 17179869184 | bytes 75497472 | tf_op jit(solution)/shard_map/pallas_call | solution.py:355
  306.4 4.0 add_convert_fusion
  311.2 50.5 %shard_map.218 = (bf16[2048,3072]{1,0:T(8,128)(2,1)}, bf16[2048,1024]{1,0:T(8,128)(2,1)}, f32[8,1024]{1,0:T(8,128)}, bf16[8,128,1024]{2,1,0:T(8,128)(2,1)}, bf16[8,128,1024]{2,1,0:T(8,128)(2,1)}) custom-call(f32[2048,1024]{1,0:T(8,128)} %get-tuple-element.299.refs_0_, f32[2048,1024]{1,0:T(8,128)} %get-tuple-element.300.refs_1_, ...), custom_call_target="tpu_custom_call" | custom-call | flops 38654705664 | bytes 76218368 | tf_op jit(solution)/shard_map/pallas_call | solution.py:355
  363.2 30.4 %shard_map.219 = (bf16[16,64,2048]{2,1,0:T(8,128)(2,1)}, bf16[16,64,2048]{2,1,0:T(8,128)(2,1)}, bf16[16,256,512]{2,1,0:T(8,128)(2,1)}, bf16[8,64,2048]{2,1,0:T(8,128)(2,1)}) custom-call(s32[17]{0:T(128)} %concatenate.59.refs_0_, bf16[2048,1024]{1,0:T(8,128)(2,1)} %get-tuple-element.307.refs_1_, bf16[2048,3072]{1,0:T(8,128)(2,1)} %get-tuple-element.314.refs_2_, ...), custom_call_target="tpu_custom_call" | custom-call | flops 17179869184 | bytes 83886080 | tf_op jit(solution)/shard_map/pallas_call | solution.py:355
  393.6 2.4 slice.264
  397.3 1.5 collective-permute-start.27
  399.5 33.6 %shard_map.220 = (bf16[4,256,3072]{2,1,0:T(8,128)(2,1)}, bf16[4,256,1024]{2,1,0:T(8,128)(2,1)}, bf16[4,256,1024]{2,1,0:T(8,128)(2,1)}, f32[16,1024]{1,0:T(8,128)...) custom-call(bf16[4,32,1024]{2,1,0:T(8,128)(2,1)} %get-tuple-element., ...), custom_call_target="tpu_custom_call" | custom-call | flops 30064771072 | bytes 42336768 | tf_op jit(solution)/shard_map/pallas_call | solution.py:355
  434.3 1.6 collective-permute-start.31
  436.8 2.5 collective-permute-start.30
  439.3 36.1 %shard_map.221 = (bf16[4,256,3072]{2,1,0:T(8,128)(2,1)}, bf16[4,256,1024]{2,1,0:T(8,128)(2,1)}, bf16[4,256,1024]{2,1,0:T(8,128)(2,1)}, f32[16,1024]{1,0:T(8,128)...) custom-call(bf16[4,32,1024]{2,1,0:T(8,128)(2,1)} %get-tuple-element., ...), custom_call_target="tpu_custom_call" | custom-call | flops 30064771072 | bytes 59113984 | tf_op jit(solution)/shard_map/pallas_call | solution.py:355
  478.2 2.8 collective-permute-start.32
  481.9 2.5 collective-permute-start.36
  484.5 29.2 %shard_map.222 = (bf16[16,64,1024]{2,1,0:T(8,128)(2,1)}, bf16[16,64,1024]{2,1,0:T(8,128)(2,1)}, bf16[8,64,1024]{2,1,0:T(8,128)(2,1)}, bf16[8,64,1024]{2,1,0:T(8,...) custom-call(s32[33]{0:T(128)} %concatenate.58.refs_0_, bf16[1024,1024]{1,0:T(8,128)(2,1)} %bitcast.144, ...), custom_call_target="tpu_custom_call" | custom-call | flops 17179869184 | bytes 50331648 | tf_op jit(solution)/shard_map/pallas_call | solution.py:355
  520.4 5.3 shard_map.223
  525.8 3.0 add_convert_fusion.1
  529.5 3.0 add_convert_fusion.2
  536.1 24.7 %collective-permute-done.42 = f32[36,1024]{1,0:T(8,128)S(1)} collective-permute-done((f32[36,1024]{1,0:T(8,128)S(1)}, f32[36,1024]{1,0:T(8,128)S(1)}, u32[]{:S(2)}, u32[]{:S(2)}) %collective-permute-start.42) | collective-permute-done | bytes 147488 | tf_op jit(solution)/shard_map/ppermute | solution.py:591
  560.8 3.3 add_convert_fusion.5
  564.1 1.4 collective-permute-start.47
  565.5 3.3 add_convert_fusion.7
  568.9 1.4 collective-permute-start.46
  571.9 9.1 %shard_map.224 = bf16[32,64,1024]{2,1,0:T(8,128)(2,1)} custom-call(s32[4]{0:T(128)} %iota_xor_fusion.meta.refs_0_, bf16[2,4,32,1024]{3,2,1,0:T(8,128)(2,1)} %get-tuple-element.439.refs_1_, bf16[2,4,32,1024]{3,2,1,0:T(8,128)(2,1)} %get-tuple-element.440.refs_2_, bf16[4,4,32,1024]{3,2,1,0:T(8,128)(2,1)} %copy-done.2, bf16[4,4,32,1024]{3,2,1,0:T(8,128)(2,1)} %copy-done.3, ...), custom_call_target="tpu_custom_call" | custom-call | bytes 25427968 | tf_op jit(solution)/shard_map/pallas_call | solution.py:355
  580.9 3.9 collective-permute-done.48
  588.1 1.4 collective-permute-start.53
  590.6 3.5 collective-permute-start.51
  595.5 14.2 %collective-permute-done.52 = f32[36,1024]{1,0:T(8,128)S(1)} collective-permute-done((f32[36,1024]{1,0:T(8,128)S(1)}, f32[36,1024]{1,0:T(8,128)S(1)}, u32[]{:S(2)}, u32[]{:S(2)}) %collective-permute-start.52) | collective-permute-done | bytes 147488 | tf_op jit(solution)/shard_map/ppermute | solution.py:591
  611.8 3.3 collective-permute-start.54
  616.6 6.6 %collective-permute-done.54 = f32[36,1024]{1,0:T(8,128)S(1)} collective-permute-done((f32[36,1024]{1,0:T(8,128)S(1)}, f32[36,1024]{1,0:T(8,128)S(1)}, u32[]{:S(2)}, u32[]{:S(2)}) %collective-permute-start.54) | collective-permute-done | bytes 147488 | tf_op jit(solution)/shard_map/ppermute | solution.py:591
  (283 shorter events, 61.9 us)
Async XLA Ops:
  7.2 507.2 %reduce-scatter.3.cloned.1.call-start = ((), (), s32[]{:S(2)}) async-start(), calls=%async_computation.2 | async-start | bytes 5242880 | tf_op jit(solution)/shard_map/reduce_scatter | solution.py:679
  12.7 20.3 %collective-permute-start.5 = (bf16[4,32,1024]{2,1,0:T(8,128)(2,1)}, bf16[4,32,1024]{2,1,0:T(8,128)(2,1)}, u32[]{:S(2)}, u32[]{:S(2)}) collective-permute-start(bf16[4,32,1024]{2,1,0:T(8,128)(2,1)} %get-tuple-element.513), channel_id=1, source_target_pairs={{0,5},{1,4},{2,7},{3,6},{4,1},{5,0},{6,3},{7,2},{8,13},{9,12},{10,... | collective-permute-start | bytes 786440 | tf_op jit(solution)/shard_map/ppermute | solution.py:591
  15.9 18.6 %collective-permute-start.6 = (bf16[4,32,1024]{2,1,0:T(8,128)(2,1)}, bf16[4,32,1024]{2,1,0:T(8,128)(2,1)}, u32[]{:S(2)}, u32[]{:S(2)}) collective-permute-start(bf16[4,32,1024]{2,1,0:T(8,128)(2,1)} %get-tuple-element.511), channel_id=1, source_target_pairs={{0,7},{1,6},{2,5},{3,4},{4,3},{5,2},{6,1},{7,0},{8,15},{9,14},{10,... | collective-permute-start | bytes 786440 | tf_op jit(solution)/shard_map/ppermute | solution.py:591
  19.0 20.3 %collective-permute-start.3 = (bf16[4,32,1024]{2,1,0:T(8,128)(2,1)}, bf16[4,32,1024]{2,1,0:T(8,128)(2,1)}, u32[]{:S(2)}, u32[]{:S(2)}) collective-permute-start(bf16[4,32,1024]{2,1,0:T(8,128)(2,1)} %get-tuple-element.517), channel_id=1, source_target_pairs={{0,1},{1,0},{2,3},{3,2},{4,5},{5,4},{6,7},{7,6},{8,9},{9,8},{10,11... | collective-permute-start | bytes 786440 | tf_op jit(solution)/shard_map/ppermute | solution.py:591
  19.9 19.4 %collective-permute-start.4 = (bf16[4,32,1024]{2,1,0:T(8,128)(2,1)}, bf16[4,32,1024]{2,1,0:T(8,128)(2,1)}, u32[]{:S(2)}, u32[]{:S(2)}) collective-permute-start(bf16[4,32,1024]{2,1,0:T(8,128)(2,1)} %get-tuple-element.515), channel_id=1, source_target_pairs={{0,3},{1,2},{2,1},{3,0},{4,7},{5,6},{6,5},{7,4},{8,11},{9,10},{10,... | collective-permute-start | bytes 786440 | tf_op jit(solution)/shard_map/ppermute | solution.py:591
  21.3 18.0 %collective-permute-start.1 = (bf16[4,32,1024]{2,1,0:T(8,128)(2,1)}, bf16[4,32,1024]{2,1,0:T(8,128)(2,1)}, u32[]{:S(2)}, u32[]{:S(2)}) collective-permute-start(bf16[4,32,1024]{2,1,0:T(8,128)(2,1)} %get-tuple-element.521), channel_id=1, source_target_pairs={{0,4},{1,5},{2,6},{3,7},{4,0},{5,1},{6,2},{7,3},{8,12},{9,13},{10,... | collective-permute-start | bytes 786440 | tf_op jit(solution)/shard_map/ppermute | solution.py:591
  48.4 30.4 %collective-permute-start.12 = (bf16[4,32,1024]{2,1,0:T(8,128)(2,1)S(1)}, bf16[4,32,1024]{2,1,0:T(8,128)(2,1)S(1)}, u32[]{:S(2)}, u32[]{:S(2)}) collective-permute-start(bf16[4,32,1024]{2,1,0:T(8,128)(2,1)S(1)} %get-tuple-element.263), channel_id=1, source_target_pairs={{0,5},{1,4},{2,7},{3,6},{4,1},{5,0},{6,3},{7,2},{8,13},{9,12},{10,... | collective-permute-start | bytes 786440 | tf_op jit(solution)/shard_map/ppermute | solution.py:591
  49.6 31.3 %collective-permute-start.13 = (bf16[4,32,1024]{2,1,0:T(8,128)(2,1)S(1)}, bf16[4,32,1024]{2,1,0:T(8,128)(2,1)}, u32[]{:S(2)}, u32[]{:S(2)}) collective-permute-start(bf16[4,32,1024]{2,1,0:T(8,128)(2,1)S(1)} %get-tuple-element.264), channel_id=1, source_target_pairs={{0,7},{1,6},{2,5},{3,4},{4,3},{5,2},{6,1},{7,0},{8,15},{9,14},{10,... | collective-permute-start | bytes 786440 | tf_op jit(solution)/shard_map/ppermute | solution.py:591
  50.1 30.8 %collective-permute-start.7 = (bf16[4,32,1024]{2,1,0:T(8,128)(2,1)}, bf16[4,32,1024]{2,1,0:T(8,128)(2,1)}, u32[]{:S(2)}, u32[]{:S(2)}) collective-permute-start(bf16[4,32,1024]{2,1,0:T(8,128)(2,1)} %get-tuple-element.258), channel_id=1, source_target_pairs={{0,2},{1,3},{2,0},{3,1},{4,6},{5,7},{6,4},{7,5},{8,10},{9,11},{10,... | collective-permute-start | bytes 786440 | tf_op jit(solution)/shard_map/ppermute | solution.py:591
  51.6 29.2 %collective-permute-start.8 = (bf16[4,32,1024]{2,1,0:T(8,128)(2,1)S(1)}, bf16[4,32,1024]{2,1,0:T(8,128)(2,1)}, u32[]{:S(2)}, u32[]{:S(2)}) collective-permute-start(bf16[4,32,1024]{2,1,0:T(8,128)(2,1)S(1)} %get-tuple-element.259), channel_id=1, source_target_pairs={{0,4},{1,5},{2,6},{3,7},{4,0},{5,1},{6,2},{7,3},{8,12},{9,13},{10,... | collective-permute-start | bytes 786440 | tf_op jit(solution)/shard_map/ppermute | solution.py:591
  56.1 24.7 %collective-permute-start.9 = (bf16[4,32,1024]{2,1,0:T(8,128)(2,1)}, bf16[4,32,1024]{2,1,0:T(8,128)(2,1)}, u32[]{:S(2)}, u32[]{:S(2)}) collective-permute-start(bf16[4,32,1024]{2,1,0:T(8,128)(2,1)} %get-tuple-element.260), channel_id=1, source_target_pairs={{0,6},{1,7},{2,4},{3,5},{4,2},{5,3},{6,0},{7,1},{8,14},{9,15},{10,... | collective-permute-start | bytes 786440 | tf_op jit(solution)/shard_map/ppermute | solution.py:591
  79.6 25.8 %collective-permute-start.14 = (bf16[4,2,128,1024]{3,2,1,0:T(8,128)(2,1)}, bf16[4,2,128,1024]{3,2,1,0:T(8,128)(2,1)}, u32[]{:S(2)}, u32[]{:S(2)}) collective-permute-start(bf16[4,2,128,1024]{3,2,1,0:T(8,128)(2,1)} %get-tuple-element.266), channel_id=1, source_target_pairs={{0,1},{1,0},{2,3},{3,2},{4,5},{5,4},{6,7},{7,6},{8,9},{9,8},{10,11... | collective-permute-start | bytes 6291464 | tf_op jit(solution)/shard_map/ppermute | solution.py:591
  101.9 50.2 %collective-permute-start.16 = (bf16[512,1024]{1,0:T(8,128)(2,1)S(1)}, bf16[512,1024]{1,0:T(8,128)(2,1)}, u32[]{:S(2)}, u32[]{:S(2)}) collective-permute-start(bf16[512,1024]{1,0:T(8,128)(2,1)S(1)} %bitcast.136), channel_id=1, source_target_pairs={{0,2},{1,3},{2,0},{3,1},{4,6},{5,7},{6,4},{7,5},{8,10},{9,11},{10,... | collective-permute-start | bytes 3145736 | tf_op jit(solution)/shard_map/ppermute | solution.py:591
  102.4 49.6 %collective-permute-start.17 = (bf16[512,1024]{1,0:T(8,128)(2,1)S(1)}, bf16[512,1024]{1,0:T(8,128)(2,1)}, u32[]{:S(2)}, u32[]{:S(2)}) collective-permute-start(bf16[512,1024]{1,0:T(8,128)(2,1)S(1)} %bitcast.135), channel_id=1, source_target_pairs={{0,4},{1,5},{2,6},{3,7},{4,0},{5,1},{6,2},{7,3},{8,12},{9,13},{10,... | collective-permute-start | bytes 3145736 | tf_op jit(solution)/shard_map/ppermute | solution.py:591
  102.9 49.2 %collective-permute-start.18 = (bf16[512,1024]{1,0:T(8,128)(2,1)S(1)}, bf16[512,1024]{1,0:T(8,128)(2,1)}, u32[]{:S(2)}, u32[]{:S(2)}) collective-permute-start(bf16[512,1024]{1,0:T(8,128)(2,1)S(1)} %bitcast.134), channel_id=1, source_target_pairs={{0,6},{1,7},{2,4},{3,5},{4,2},{5,3},{6,0},{7,1},{8,14},{9,15},{10,... | collective-permute-start | bytes 3145736 | tf_op jit(solution)/shard_map/ppermute | solution.py:591
  252.2 26.5 %collective-permute-start.19 = (bf16[512,1024]{1,0:T(8,128)(2,1)}, bf16[512,1024]{1,0:T(8,128)(2,1)S(1)}, u32[]{:S(2)}, u32[]{:S(2)}) collective-permute-start(bf16[512,1024]{1,0:T(8,128)(2,1)} %get-tuple-element.287), channel_id=1, source_target_pairs={{0,2},{1,3},{2,0},{3,1},{4,6},{5,7},{6,4},{7,5},{8,10},{9,11},{10,... | collective-permute-start | bytes 3145736 | tf_op jit(solution)/shard_map/ppermute | solution.py:591
  252.8 25.9 %collective-permute-start.20 = (bf16[512,1024]{1,0:T(8,128)(2,1)}, bf16[512,1024]{1,0:T(8,128)(2,1)S(1)}, u32[]{:S(2)}, u32[]{:S(2)}) collective-permute-start(bf16[512,1024]{1,0:T(8,128)(2,1)} %get-tuple-element.288), channel_id=1, source_target_pairs={{0,4},{1,5},{2,6},{3,7},{4,0},{5,1},{6,2},{7,3},{8,12},{9,13},{10,... | collective-permute-start | bytes 3145736 | tf_op jit(solution)/shard_map/ppermute | solution.py:591
  278.7 27.6 %collective-permute-start.21 = (bf16[16,64,2048]{2,1,0:T(8,128)(2,1)}, bf16[16,64,2048]{2,1,0:T(8,128)(2,1)}, u32[]{:S(2)}, u32[]{:S(2)}) collective-permute-start(bf16[16,64,2048]{2,1,0:T(8,128)(2,1)} %get-tuple-element.294), channel_id=1, source_target_pairs={{0,1},{1,0},{2,3},{3,2},{4,5},{5,4},{6,7},{7,6},{8,9},{9,8},{10,11... | collective-permute-start | bytes 12582920 | tf_op jit(solution)/shard_map/ppermute | solution.py:591
  278.8 27.5 %collective-permute-start.22 = (bf16[512,1024]{1,0:T(8,128)(2,1)}, bf16[512,1024]{1,0:T(8,128)(2,1)S(1)}, u32[]{:S(2)}, u32[]{:S(2)}) collective-permute-start(bf16[512,1024]{1,0:T(8,128)(2,1)} %get-tuple-element.298), channel_id=1, source_target_pairs={{0,6},{1,7},{2,4},{3,5},{4,2},{5,3},{6,0},{7,1},{8,14},{9,15},{10,... | collective-permute-start | bytes 3145736 | tf_op jit(solution)/shard_map/ppermute | solution.py:591
  306.3 55.5 %collective-permute-start.25 = (bf16[16,256,512]{2,1,0:T(8,128)(2,1)}, bf16[16,256,512]{2,1,0:T(8,128)(2,1)}, u32[]{:S(2)}, u32[]{:S(2)}) collective-permute-start(bf16[16,256,512]{2,1,0:T(8,128)(2,1)} %get-tuple-element.313), channel_id=1, source_target_pairs={{0,1},{1,0},{2,3},{3,2},{4,5},{5,4},{6,7},{7,6},{8,9},{9,8},{10,11... | collective-permute-start | bytes 12582920 | tf_op jit(solution)/shard_map/ppermute | solution.py:591
  310.5 51.3 %collective-permute-start.24 = (bf16[8,64,2048]{2,1,0:T(8,128)(2,1)}, bf16[8,64,2048]{2,1,0:T(8,128)(2,1)S(1)}, u32[]{:S(2)}, u32[]{:S(2)}) collective-permute-start(bf16[8,64,2048]{2,1,0:T(8,128)(2,1)} %add_convert_fusion), channel_id=1, source_target_pairs={{0,2},{1,3},{2,0},{3,1},{4,6},{5,7},{6,4},{7,5},{8,10},{9,11},{10,... | collective-permute-start | bytes 6291464 | tf_op jit(solution)/shard_map/ppermute | solution.py:591
  361.7 34.2 %collective-permute-start.23 = (bf16[8,128,1024]{2,1,0:T(8,128)(2,1)}, bf16[8,128,1024]{2,1,0:T(8,128)(2,1)}, u32[]{:S(2)}, u32[]{:S(2)}) collective-permute-start(bf16[8,128,1024]{2,1,0:T(8,128)(2,1)} %get-tuple-element.305), channel_id=1, source_target_pairs={{0,1},{1,0},{2,3},{3,2},{4,5},{5,4},{6,7},{7,6},{8,9},{9,8},{10,11... | collective-permute-start | bytes 6291464 | tf_op jit(solution)/shard_map/ppermute | solution.py:591
  396.0 190.8 %reduce-scatter.5.cloned.1.call-start = ((), (), s32[]{:S(2)}) async-start(), calls=%async_computation.3 | async-start | bytes 5242880 | tf_op jit(solution)/shard_map/reduce_scatter | solution.py:679
  396.0 37.0 %collective-permute-start.26 = (bf16[16,64,2048]{2,1,0:T(8,128)(2,1)}, bf16[16,64,2048]{2,1,0:T(8,128)(2,1)}, u32[]{:S(2)}, u32[]{:S(2)}) collective-permute-start(bf16[16,64,2048]{2,1,0:T(8,128)(2,1)} %get-tuple-element.340), channel_id=1, source_target_pairs={{0,1},{1,0},{2,3},{3,2},{4,5},{5,4},{6,7},{7,6},{8,9},{9,8},{10,11... | collective-permute-start | bytes 12582920 | tf_op jit(solution)/shard_map/ppermute | solution.py:591
  397.3 35.8 %collective-permute-start.27 = (bf16[4,64,2048]{2,1,0:T(8,128)(2,1)}, bf16[4,64,2048]{2,1,0:T(8,128)(2,1)S(1)}, u32[]{:S(2)}, u32[]{:S(2)}) collective-permute-start(bf16[4,64,2048]{2,1,0:T(8,128)(2,1)} %slice.264), channel_id=1, source_target_pairs={{0,4},{1,5},{2,6},{3,7},{4,0},{5,1},{6,2},{7,3},{8,12},{9,13},{10,... | collective-permute-start | bytes 3145736 | tf_op jit(solution)/shard_map/ppermute | solution.py:591
  434.3 41.2 %collective-permute-start.31 = (bf16[2,64,2048]{2,1,0:T(8,128)(2,1)}, bf16[2,64,2048]{2,1,0:T(8,128)(2,1)S(1)}, u32[]{:S(2)}, u32[]{:S(2)}) collective-permute-start(bf16[2,64,2048]{2,1,0:T(8,128)(2,1)} %get-tuple-element.495), channel_id=1, source_target_pairs={{0,8},{8,0},{16,24},{24,16},{1,9},{9,1},{17,25},{25,17},{2,10},{10... | collective-permute-start | bytes 1572872 | tf_op jit(solution)/shard_map/ppermute | solution.py:591
  435.8 39.7 %collective-permute-start.28 = (bf16[2,4,32,1024]{3,2,1,0:T(8,128)(2,1)}, bf16[2,4,32,1024]{3,2,1,0:T(8,128)(2,1)S(1)}, u32[]{:S(2)}, u32[]{:S(2)}) collective-permute-start(bf16[2,4,32,1024]{3,2,1,0:T(8,128)(2,1)} %get-tuple-element.347), channel_id=1, source_target_pairs={{0,2},{1,3},{2,0},{3,1},{4,6},{5,7},{6,4},{7,5},{8,10},{9,11},{10,... | collective-permute-start | bytes 1572872 | tf_op jit(solution)/shard_map/ppermute | solution.py:591
  435.8 39.7 %collective-permute-start.29 = (bf16[2,4,32,1024]{3,2,1,0:T(8,128)(2,1)}, bf16[2,4,32,1024]{3,2,1,0:T(8,128)(2,1)S(1)}, u32[]{:S(2)}, u32[]{:S(2)}) collective-permute-start(bf16[2,4,32,1024]{3,2,1,0:T(8,128)(2,1)} %get-tuple-element.348), channel_id=1, source_target_pairs={{0,4},{1,5},{2,6},{3,7},{4,0},{5,1},{6,2},{7,3},{8,12},{9,13},{10,... | collective-permute-start | bytes 1572872 | tf_op jit(solution)/shard_map/ppermute | solution.py:591
  436.8 38.7 %collective-permute-start.30 = (bf16[2,4,32,1024]{3,2,1,0:T(8,128)(2,1)}, bf16[2,4,32,1024]{3,2,1,0:T(8,128)(2,1)S(1)}, u32[]{:S(2)}, u32[]{:S(2)}) collective-permute-start(bf16[2,4,32,1024]{3,2,1,0:T(8,128)(2,1)} %get-tuple-element.349), channel_id=1, source_target_pairs={{0,6},{1,7},{2,4},{3,5},{4,2},{5,3},{6,0},{7,1},{8,14},{9,15},{10,... | collective-permute-start | bytes 1572872 | tf_op jit(solution)/shard_map/ppermute | solution.py:591
  478.1 36.3 %collective-permute-start.33 = (bf16[4,4,32,1024]{3,2,1,0:T(8,128)(2,1)}, bf16[4,4,32,1024]{3,2,1,0:T(8,128)(2,1)S(1)}, u32[]{:S(2)}, u32[]{:S(2)}) collective-permute-start(bf16[4,4,32,1024]{3,2,1,0:T(8,128)(2,1)} %pad_maximum_fusion.1), channel_id=1, source_target_pairs={{0,1},{1,0},{2,3},{3,2},{4,5},{5,4},{6,7},{7,6},{8,9},{9,8},{10,11... | collective-permute-start | bytes 3145736 | tf_op jit(solution)/shard_map/ppermute | solution.py:591
  478.2 35.4 %collective-permute-start.32 = (bf16[1,64,2048]{2,1,0:T(8,128)(2,1)S(1)}, bf16[1,64,2048]{2,1,0:T(8,128)(2,1)S(1)}, u32[]{:S(2)}, u32[]{:S(2)}) collective-permute-start(bf16[1,64,2048]{2,1,0:T(8,128)(2,1)S(1)} %get-tuple-element.508), channel_id=1, source_target_pairs={{0,16},{8,24},{16,0},{24,8},{1,17},{9,25},{17,1},{25,9},{2,18},{10... | collective-permute-start | bytes 786440 | tf_op jit(solution)/shard_map/ppermute | solution.py:591
  481.0 32.7 %collective-permute-start.34 = (bf16[2,4,32,1024]{3,2,1,0:T(8,128)(2,1)}, bf16[2,4,32,1024]{3,2,1,0:T(8,128)(2,1)S(1)}, u32[]{:S(2)}, u32[]{:S(2)}) collective-permute-start(bf16[2,4,32,1024]{3,2,1,0:T(8,128)(2,1)} %get-tuple-element.390), channel_id=1, source_target_pairs={{0,2},{1,3},{2,0},{3,1},{4,6},{5,7},{6,4},{7,5},{8,10},{9,11},{10,... | collective-permute-start | bytes 1572872 | tf_op jit(solution)/shard_map/ppermute | solution.py:591
  481.0 32.7 %collective-permute-start.35 = (bf16[2,4,32,1024]{3,2,1,0:T(8,128)(2,1)}, bf16[2,4,32,1024]{3,2,1,0:T(8,128)(2,1)S(1)}, u32[]{:S(2)}, u32[]{:S(2)}) collective-permute-start(bf16[2,4,32,1024]{3,2,1,0:T(8,128)(2,1)} %get-tuple-element.391), channel_id=1, source_target_pairs={{0,4},{1,5},{2,6},{3,7},{4,0},{5,1},{6,2},{7,3},{8,12},{9,13},{10,... | collective-permute-start | bytes 1572872 | tf_op jit(solution)/shard_map/ppermute | solution.py:591
  481.9 31.8 %collective-permute-start.36 = (bf16[2,4,32,1024]{3,2,1,0:T(8,128)(2,1)}, bf16[2,4,32,1024]{3,2,1,0:T(8,128)(2,1)S(1)}, u32[]{:S(2)}, u32[]{:S(2)}) collective-permute-start(bf16[2,4,32,1024]{3,2,1,0:T(8,128)(2,1)} %get-tuple-element.392), channel_id=1, source_target_pairs={{0,6},{1,7},{2,4},{3,5},{4,2},{5,3},{6,0},{7,1},{8,14},{9,15},{10,... | collective-permute-start | bytes 1572872 | tf_op jit(solution)/shard_map/ppermute | solution.py:591
  518.5 17.6 %collective-permute-start.44 = (bf16[4,4,32,1024]{3,2,1,0:T(8,128)(2,1)}, bf16[4,4,32,1024]{3,2,1,0:T(8,128)(2,1)S(1)}, u32[]{:S(2)}, u32[]{:S(2)}) collective-permute-start(bf16[4,4,32,1024]{3,2,1,0:T(8,128)(2,1)} %pad_maximum_fusion.2), channel_id=1, source_target_pairs={{0,1},{1,0},{2,3},{3,2},{4,5},{5,4},{6,7},{7,6},{8,9},{9,8},{10,11... | collective-permute-start | bytes 3145736 | tf_op jit(solution)/shard_map/ppermute | solution.py:591
  519.8 16.3 %collective-permute-start.43 = (bf16[2,256,512]{2,1,0:T(8,128)(2,1)}, bf16[2,256,512]{2,1,0:T(8,128)(2,1)}, u32[]{:S(2)}, u32[]{:S(2)}) collective-permute-start(bf16[2,256,512]{2,1,0:T(8,128)(2,1)} %get-tuple-element.506), channel_id=1, source_target_pairs={{0,2},{1,3},{2,0},{3,1},{4,6},{5,7},{6,4},{7,5},{8,10},{9,11},{10,... | collective-permute-start | bytes 1572872 | tf_op jit(solution)/shard_map/ppermute | solution.py:591
  528.8 32.0 %collective-permute-start.41 = (bf16[8,64,1024]{2,1,0:T(8,128)(2,1)}, bf16[8,64,1024]{2,1,0:T(8,128)(2,1)}, u32[]{:S(2)}, u32[]{:S(2)}) collective-permute-start(bf16[8,64,1024]{2,1,0:T(8,128)(2,1)} %add_convert_fusion.1), channel_id=1, source_target_pairs={{0,4},{1,5},{2,6},{3,7},{4,0},{5,1},{6,2},{7,3},{8,12},{9,13},{10,... | collective-permute-start | bytes 3145736 | tf_op jit(solution)/shard_map/ppermute | solution.py:591
  532.5 28.3 %collective-permute-start.40 = (bf16[8,64,1024]{2,1,0:T(8,128)(2,1)}, bf16[8,64,1024]{2,1,0:T(8,128)(2,1)}, u32[]{:S(2)}, u32[]{:S(2)}) collective-permute-start(bf16[8,64,1024]{2,1,0:T(8,128)(2,1)} %add_convert_fusion.2), channel_id=1, source_target_pairs={{0,2},{1,3},{2,0},{3,1},{4,6},{5,7},{6,4},{7,5},{8,10},{9,11},{10,... | collective-permute-start | bytes 3145736 | tf_op jit(solution)/shard_map/ppermute | solution.py:591
  535.3 25.5 %collective-permute-start.42 = (f32[36,1024]{1,0:T(8,128)S(1)}, f32[36,1024]{1,0:T(8,128)S(1)}, u32[]{:S(2)}, u32[]{:S(2)}) collective-permute-start(f32[36,1024]{1,0:T(8,128)S(1)} %add.472), channel_id=1, source_target_pairs={{0,2},{1,3},{2,0},{3,1},{4,6},{5,7},{6,4},{7,5},{8,10},{9,11},{10,... | collective-permute-start | bytes 442376 | tf_op jit(solution)/shard_map/ppermute | solution.py:591
  564.1 20.7 %collective-permute-start.47 = (bf16[4,64,1024]{2,1,0:T(8,128)(2,1)}, bf16[4,64,1024]{2,1,0:T(8,128)(2,1)}, u32[]{:S(2)}, u32[]{:S(2)}) collective-permute-start(bf16[4,64,1024]{2,1,0:T(8,128)(2,1)} %get-tuple-element.479), channel_id=1, source_target_pairs={{0,2},{1,3},{2,0},{3,1},{4,6},{5,7},{6,4},{7,5},{8,10},{9,11},{10,... | collective-permute-start | bytes 1572872 | tf_op jit(solution)/shard_map/ppermute | solution.py:591
  568.9 16.0 %collective-permute-start.46 = (bf16[4,64,1024]{2,1,0:T(8,128)(2,1)}, bf16[4,64,1024]{2,1,0:T(8,128)(2,1)S(1)}, u32[]{:S(2)}, u32[]{:S(2)}) collective-permute-start(bf16[4,64,1024]{2,1,0:T(8,128)(2,1)} %get-tuple-element.481), channel_id=1, source_target_pairs={{0,4},{1,5},{2,6},{3,7},{4,0},{5,1},{6,2},{7,3},{8,12},{9,13},{10,... | collective-permute-start | bytes 1572872 | tf_op jit(solution)/shard_map/ppermute | solution.py:591
  570.3 14.6 %collective-permute-start.48 = (f32[36,1024]{1,0:T(8,128)S(1)}, f32[36,1024]{1,0:T(8,128)S(1)}, u32[]{:S(2)}, u32[]{:S(2)}) collective-permute-start(f32[36,1024]{1,0:T(8,128)S(1)} %add.484), channel_id=1, source_target_pairs={{0,4},{1,5},{2,6},{3,7},{4,0},{5,1},{6,2},{7,3},{8,12},{9,13},{10,... | collective-permute-start | bytes 442376 | tf_op jit(solution)/shard_map/ppermute | solution.py:591
  588.1 22.0 %collective-permute-start.53 = (bf16[2,64,2048]{2,1,0:T(8,128)(2,1)S(1)}, bf16[2,64,2048]{2,1,0:T(8,128)(2,1)S(1)}, u32[]{:S(2)}, u32[]{:S(2)}) collective-permute-start(bf16[2,64,2048]{2,1,0:T(8,128)(2,1)S(1)} %get-tuple-element.501), channel_id=1, source_target_pairs={{0,4},{1,5},{2,6},{3,7},{4,0},{5,1},{6,2},{7,3},{8,12},{9,13},{10,... | collective-permute-start | bytes 1572872 | tf_op jit(solution)/shard_map/ppermute | solution.py:591
  589.6 20.5 %collective-permute-start.49 = (bf16[1,64,2048]{2,1,0:T(8,128)(2,1)S(1)}, bf16[1,64,2048]{2,1,0:T(8,128)(2,1)S(1)}, u32[]{:S(2)}, u32[]{:S(2)}) collective-permute-start(bf16[1,64,2048]{2,1,0:T(8,128)(2,1)S(1)} %get-tuple-element.504), channel_id=1, source_target_pairs={{0,8},{8,0},{16,24},{24,16},{1,9},{9,1},{17,25},{25,17},{2,10},{10... | collective-permute-start | bytes 786440 | tf_op jit(solution)/shard_map/ppermute | solution.py:591
  590.6 19.6 %collective-permute-start.50 = (bf16[1,64,2048]{2,1,0:T(8,128)(2,1)S(1)}, bf16[1,64,2048]{2,1,0:T(8,128)(2,1)S(1)}, u32[]{:S(2)}, u32[]{:S(2)}) collective-permute-start(bf16[1,64,2048]{2,1,0:T(8,128)(2,1)S(1)} %get-tuple-element.505), channel_id=1, source_target_pairs={{0,16},{8,24},{16,0},{24,8},{1,17},{9,25},{17,1},{25,9},{2,18},{10... | collective-permute-start | bytes 786440 | tf_op jit(solution)/shard_map/ppermute | solution.py:591
  590.6 19.6 %collective-permute-start.51 = (bf16[1,64,2048]{2,1,0:T(8,128)(2,1)S(1)}, bf16[1,64,2048]{2,1,0:T(8,128)(2,1)S(1)}, u32[]{:S(2)}, u32[]{:S(2)}) collective-permute-start(bf16[1,64,2048]{2,1,0:T(8,128)(2,1)S(1)} %get-tuple-element.503), channel_id=1, source_target_pairs={{0,24},{8,16},{16,8},{24,0},{1,25},{9,17},{17,9},{25,1},{2,26},{10... | collective-permute-start | bytes 786440 | tf_op jit(solution)/shard_map/ppermute | solution.py:591
  595.3 14.3 %collective-permute-start.52 = (f32[36,1024]{1,0:T(8,128)S(1)}, f32[36,1024]{1,0:T(8,128)S(1)}, u32[]{:S(2)}, u32[]{:S(2)}) collective-permute-start(f32[36,1024]{1,0:T(8,128)S(1)} %add.485), channel_id=1, source_target_pairs={{0,8},{8,0},{16,24},{24,16},{1,9},{9,1},{17,25},{25,17},{2,10},{10... | collective-permute-start | bytes 442376 | tf_op jit(solution)/shard_map/ppermute | solution.py:591
  610.6 12.6 %collective-permute-start.55 = (bf16[1,64,2048]{2,1,0:T(8,128)(2,1)S(1)}, bf16[1,64,2048]{2,1,0:T(8,128)(2,1)S(1)}, u32[]{:S(2)}, u32[]{:S(2)}) collective-permute-start(bf16[1,64,2048]{2,1,0:T(8,128)(2,1)S(1)} %get-tuple-element.499), channel_id=1, source_target_pairs={{0,2},{1,3},{2,0},{3,1},{4,6},{5,7},{6,4},{7,5},{8,10},{9,11},{10,... | collective-permute-start | bytes 786440 | tf_op jit(solution)/shard_map/ppermute | solution.py:591
  (56 other events, 605.1 us)
Sparse Core Ops, SparseCore 0:
  396.1 88.9 reduce-scatter.2
  487.5 81.4 reduce-scatter.4

commit v2 on v1

--- a/solution.py
+++ b/solution.py
@@ -642,6 +642,8 @@
         return chains, parts, [swap(value, 1) for value in sent]
 
     def add(values, kind):
+        if len(values) == 2 and all(value.dtype == kind for value in values):
+            return values[0] + values[1]
         return sum(value.astype(F32) for value in values).astype(kind)
 
     def land(crossed):
@@ -799,13 +801,20 @@
             )
         },
     )
-    pieces = []
-    for c in range(chunks):
-        pieces.append(send_out(sources[c]))
-        if c == 0:
-            pieces[0], sources, cot_pieces, tables = hold_parts(
-                pieces[0], sources, cot_pieces, tables
-            )
+    ahead = [at for at, k in enumerate(order) if k in (1, n - 1)]
+    started = [swap(sources[1][at], order[at]) for at in ahead]
+    pieces = [send_out(sources[0])]
+    pieces[0], sources, cot_pieces, tables, started = hold_parts(
+        pieces[0], sources, cot_pieces, tables, started
+    )
+    for c in range(1, chunks):
+        came = dict(zip(ahead, started)) if c == 1 else {}
+        pieces.append(
+            [
+                came[at] if at in came else part if k == 0 else swap(part, k)
+                for at, (k, part) in enumerate(zip(order, sources[c]))
+            ]
+        )
     cot_pieces = [
         piece if j == 0 else swap(piece, j * group) for j, piece in enumerate(cot_pieces)
     ]

time: 644 us -> 639 us (level)
    convert_element_type x11 -> x2, other arithmetic: 20.7 us -> 6.69 us  [add(): return sum((value.astype(F32) for value in values)).astype(kind)]
    add x0 -> x9, other arithmetic: none -> 12.2 us  [add(): return values[0] + values[1]]
  transfers between devices with their start and end apart: 62 -> 62, of which waited for: 9 -> 8; matrix products, arithmetic and copies ran while one was open for 9% -> 8% of each run, Pallas kernels for 52% -> 53%
where the time goes in v2:
time: 639 us; the launch traced here: 631 us
  Pallas kernels  432 us (68%)
  waiting for transfers between devices  59.7 us (9%)
  starting transfers between devices  57.7 us (9%)
  other arithmetic  34.5 us (5%)
  local copies, waits for them, and re-layouts  31 us (5%)
  between operations  15.7 us (2%)
    pallas_call x13, Pallas kernels, call(): pl.pallas_call(kernel, grid_spec=pltpu.PrefetchScalarGridSpec(num_scalar_...  432 us
    ppermute x60, waiting for transfers between devices, swap(): return lax.ppermute(value, axis, [(i, i ^ k) for i in range(size)])  59.6 us
    ppermute x60, starting transfers between devices, swap(): return lax.ppermute(value, axis, [(i, i ^ k) for i in range(size)])  57.7 us
  transfers between devices with their start and end apart: 62, of which 8 were waited for; matrix products, arithmetic and copies ran while one was open for 8% of the time, Pallas kernels for 53%

profile of v2, /device:TPU:0, one launch (start us, length us, event | category | flops | bytes accessed | tf_op | source)
XLA Modules:
  0.0 630.9 jit_solution(932161566230034784)
XLA Ops:
  8.2 2.5 broadcast_select_fusion
  12.7 2.4 collective-permute-start.5
  16.0 1.7 collective-permute-start.6
  27.9 4.2 constant_dynamic-slice_fusion.2
  34.1 1.9 collective-permute-start.1
  35.9 1.4 collective-permute-start.2
  42.2 6.5 %collective-permute-done.1.refs_2_ = bf16[4,32,1024]{2,1,0:T(8,128)(2,1)} collective-permute-done((bf16[4,32,1024]{2,1,0:T(8,128)(2,1)}, bf16[4,32,1024]{2,1,0:T(8,128)(2,1)}, u32[]{:S(2)}, u32[]{:S(2)}) %collective-permute-start.1) | collective-permute-done | bytes 262176 | tf_op jit(solution)/shard_map/ppermute | solution.py:591
  48.7 1.3 collective-permute-done.refs_1_
  50.0 1.7 collective-permute-start.10
  51.7 1.4 collective-permute-start.11
  53.1 1.8 collective-permute-start.13
  54.9 1.5 collective-permute-start.9
  56.4 20.7 %shard_map.212 = (bf16[4,256,3072]{2,1,0:T(8,128)(2,1)}, bf16[4,256,1024]{2,1,0:T(8,128)(2,1)}, f32[4,16,256]{2,1,0:T(8,128)}, bf16[4,2,128,1024]{3,2,1,0:T(8,128)(2,1)}, bf16[4,2,128,1024]{3,2,1,0:T(8,128)(2,1)}) custom-call(bf16[4,32,1024]{2,1,0:T(8,128)(2,1)} %get-tuple-element.247.refs_0_, bf16[4,32,1024]{2,1,0:T(8,128)(2,1)} %collective-permute-done.refs_1_, ...), custom_call_target="tpu_custom_call" | custom-call | flops 15032385536 | bytes 16908288 | tf_op jit(solution)/shard_map/pallas_call | solution.py:355
  77.8 20.9 %shard_map.213 = (bf16[4,256,3072]{2,1,0:T(8,128)(2,1)}, bf16[4,256,1024]{2,1,0:T(8,128)(2,1)}, f32[4,16,256]{2,1,0:T(8,128)}, bf16[4,2,128,1024]{3,2,1,0:T(8,128)(2,1)}, bf16[4,2,128,1024]{3,2,1,0:T(8,128)(2,1)}) custom-call(bf16[4,32,1024]{2,1,0:T(8,128)(2,1)} %get-tuple-element.257.refs_0_, bf16[4,32,1024]{2,1,0:T(8,128)(2,1)} %collective-permute-done.9.refs_1_, ...), custom_call_target="tpu_custom_call" | custom-call | flops 15032385536 | bytes 16908288 | tf_op jit(solution)/shard_map/pallas_call | solution.py:355
  99.7 2.6 collective-permute-start.18
  103.2 45.7 %shard_map.214 = (f32[2048,1024]{1,0:T(8,128)}, f32[2048,1024]{1,0:T(8,128)}, bf16[2048,1024]{1,0:T(8,128)(2,1)}, bf16[2048,3072]{1,0:T(8,128)(2,1)}, bf16[2048,1024]{1,0:T(8,128)(2,1)}, /*index=5*/f32[16,2048]{1,0:T(8,128)}) custom-call(bf16[4,2,128,1024]{3,2,1,0:T(8,128)(2,1)} %get-tuple-element.256.refs_0_.refs_4_, ...), custom_call_target="tpu_custom_call" | custom-call | flops 30064771072 | bytes 55115776 | tf_op jit(solution)/shard_map/pallas_call | solution.py:355
  149.0 100.1 %shard_map.215 = (bf16[512,1024]{1,0:T(8,128)(2,1)}, bf16[512,1024]{1,0:T(8,128)(2,1)}, bf16[512,1024]{1,0:T(8,128)(2,1)}, bf16[512,1024]{1,0:T(8,128)(2,1)}, bf...) custom-call(f32[2048,1024]{1,0:T(8,128)} %get-tuple-element.271.refs, ...), custom_call_target="tpu_custom_call" | custom-call | flops 68719476736 | bytes 58818560 | tf_op jit(solution)/shard_map/pallas_call | solution.py:355
  250.1 25.4 %shard_map.216 = (bf16[16,64,2048]{2,1,0:T(8,128)(2,1)}, bf16[8,64,2048]{2,1,0:T(8,128)(2,1)}, bf16[8,64,2048]{2,1,0:T(8,128)(2,1)}) custom-call(s32[17]{0:T(128)} %concatenate.60.refs_0_, bf16[2048,1024]{1,0:T(8,128)(2,1)} %get-tuple-element.281.refs_1_, bf16[2048,4096]{1,0:T(8,128)(2,1)} %get-tuple-element.282.refs_2_), custom_call_target="tpu_custom_call" | custom-call | flops 17179869184 | bytes 41943040 | tf_op jit(solution)/shard_map/pallas_call | solution.py:355
  275.6 2.7 collective-permute-start.22
  278.3 24.9 %shard_map.217 = (bf16[16,256,512]{2,1,0:T(8,128)(2,1)}, bf16[16,256,512]{2,1,0:T(8,128)(2,1)}) custom-call(s32[17]{0:T(128)} %concatenate.57.refs_0_, bf16[2048,4096]{1,0:T(8,128)(2,1)} %get-tuple-element.278.refs_1_.refs_2_, bf16[2048,4096]{1,0:T(8,128)(2,1)} %get-tuple-element.278.refs_1_.refs_2_, bf16[2048,1024]{1,0:T(8,128)(2,1)} %get-tuple-element.289.refs_3_), custom_call_target="tpu_custom_call" | custom-call | flops 17179869184 | bytes 75497472 | tf_op jit(solution)/shard_map/pallas_call | solution.py:355
  303.4 3.4 slice_add_fusion
  307.4 50.5 %shard_map.218 = (bf16[2048,3072]{1,0:T(8,128)(2,1)}, bf16[2048,1024]{1,0:T(8,128)(2,1)}, f32[8,1024]{1,0:T(8,128)}, bf16[8,128,1024]{2,1,0:T(8,128)(2,1)}, bf16[8,128,1024]{2,1,0:T(8,128)(2,1)}) custom-call(f32[2048,1024]{1,0:T(8,128)} %get-tuple-element.299.refs_0_, f32[2048,1024]{1,0:T(8,128)} %get-tuple-element.300.refs_1_, ...), custom_call_target="tpu_custom_call" | custom-call | flops 38654705664 | bytes 76218368 | tf_op jit(solution)/shard_map/pallas_call | solution.py:355
  358.0 1.4 copy-done.38
  359.4 30.4 %shard_map.219 = (bf16[16,64,2048]{2,1,0:T(8,128)(2,1)}, bf16[16,64,2048]{2,1,0:T(8,128)(2,1)}, bf16[16,256,512]{2,1,0:T(8,128)(2,1)}, bf16[8,64,2048]{2,1,0:T(8,128)(2,1)}) custom-call(s32[17]{0:T(128)} %concatenate.59.refs_0_, bf16[2048,1024]{1,0:T(8,128)(2,1)} %get-tuple-element.307.refs_1_, bf16[2048,3072]{1,0:T(8,128)(2,1)} %get-tuple-element.314.refs_2_, ...), custom_call_target="tpu_custom_call" | custom-call | flops 17179869184 | bytes 83886080 | tf_op jit(solution)/shard_map/pallas_call | solution.py:355
  389.7 2.4 slice.264
  393.5 1.6 collective-permute-start.27
  395.7 33.6 %shard_map.220 = (bf16[4,256,3072]{2,1,0:T(8,128)(2,1)}, bf16[4,256,1024]{2,1,0:T(8,128)(2,1)}, bf16[4,256,1024]{2,1,0:T(8,128)(2,1)}, f32[16,1024]{1,0:T(8,128)...) custom-call(bf16[4,32,1024]{2,1,0:T(8,128)(2,1)} %get-tuple-element., ...), custom_call_target="tpu_custom_call" | custom-call | flops 30064771072 | bytes 42336768 | tf_op jit(solution)/shard_map/pallas_call | solution.py:355
  430.2 1.6 collective-permute-start.31
  432.8 2.5 collective-permute-start.30
  435.3 36.1 %shard_map.221 = (bf16[4,256,3072]{2,1,0:T(8,128)(2,1)}, bf16[4,256,1024]{2,1,0:T(8,128)(2,1)}, bf16[4,256,1024]{2,1,0:T(8,128)(2,1)}, f32[16,1024]{1,0:T(8,128)...) custom-call(bf16[4,32,1024]{2,1,0:T(8,128)(2,1)} %get-tuple-element., ...), custom_call_target="tpu_custom_call" | custom-call | flops 30064771072 | bytes 59113984 | tf_op jit(solution)/shard_map/pallas_call | solution.py:355
  474.1 2.7 collective-permute-start.32
  477.8 2.5 collective-permute-start.36
  480.3 29.3 %shard_map.222 = (bf16[16,64,1024]{2,1,0:T(8,128)(2,1)}, bf16[16,64,1024]{2,1,0:T(8,128)(2,1)}, bf16[8,64,1024]{2,1,0:T(8,128)(2,1)}, bf16[8,64,1024]{2,1,0:T(8,...) custom-call(s32[33]{0:T(128)} %concatenate.58.refs_0_, bf16[1024,1024]{1,0:T(8,128)(2,1)} %bitcast.144, ...), custom_call_target="tpu_custom_call" | custom-call | flops 17179869184 | bytes 50331648 | tf_op jit(solution)/shard_map/pallas_call | solution.py:355
  515.8 5.3 shard_map.223
  521.2 2.7 slice_add_fusion.1
  524.7 2.6 slice_add_fusion.2
  530.9 25.0 %collective-permute-done.42 = f32[36,1024]{1,0:T(8,128)S(1)} collective-permute-done((f32[36,1024]{1,0:T(8,128)S(1)}, f32[36,1024]{1,0:T(8,128)S(1)}, u32[]{:S(2)}, u32[]{:S(2)}) %collective-permute-start.42) | collective-permute-done | bytes 147488 | tf_op jit(solution)/shard_map/ppermute | solution.py:591
  555.9 3.3 add_convert_fusion
  560.5 3.4 add_convert_fusion.2
  563.8 1.7 collective-permute-start.46
  566.8 9.1 %shard_map.224 = bf16[32,64,1024]{2,1,0:T(8,128)(2,1)} custom-call(s32[4]{0:T(128)} %iota_xor_fusion.meta.refs_0_, bf16[2,4,32,1024]{3,2,1,0:T(8,128)(2,1)} %get-tuple-element.439.refs_1_, bf16[2,4,32,1024]{3,2,1,0:T(8,128)(2,1)} %get-tuple-element.440.refs_2_, bf16[4,4,32,1024]{3,2,1,0:T(8,128)(2,1)} %copy-done.2, bf16[4,4,32,1024]{3,2,1,0:T(8,128)(2,1)} %copy-done.3, ...), custom_call_target="tpu_custom_call" | custom-call | bytes 25427968 | tf_op jit(solution)/shard_map/pallas_call | solution.py:355
  575.9 4.3 collective-permute-done.48
  582.1 1.3 fusion.20
  583.5 1.5 collective-permute-start.53
  585.7 3.7 collective-permute-start.51
  590.8 14.6 %collective-permute-done.52 = f32[36,1024]{1,0:T(8,128)S(1)} collective-permute-done((f32[36,1024]{1,0:T(8,128)S(1)}, f32[36,1024]{1,0:T(8,128)S(1)}, u32[]{:S(2)}, u32[]{:S(2)}) %collective-permute-start.52) | collective-permute-done | bytes 147488 | tf_op jit(solution)/shard_map/ppermute | solution.py:591
  607.5 2.8 collective-permute-start.54
  611.8 6.6 %collective-permute-done.54 = f32[36,1024]{1,0:T(8,128)S(1)} collective-permute-done((f32[36,1024]{1,0:T(8,128)S(1)}, f32[36,1024]{1,0:T(8,128)S(1)}, u32[]{:S(2)}, u32[]{:S(2)}) %collective-permute-start.54) | collective-permute-done | bytes 147488 | tf_op jit(solution)/shard_map/ppermute | solution.py:591
  (279 shorter events, 58.2 us)
Async XLA Ops:
  7.2 503.2 %reduce-scatter.3.cloned.1.call-start = ((), (), s32[]{:S(2)}) async-start(), calls=%async_computation.2 | async-start | bytes 5242880 | tf_op jit(solution)/shard_map/reduce_scatter | solution.py:681
  12.7 20.9 %collective-permute-start.5 = (bf16[4,32,1024]{2,1,0:T(8,128)(2,1)}, bf16[4,32,1024]{2,1,0:T(8,128)(2,1)}, u32[]{:S(2)}, u32[]{:S(2)}) collective-permute-start(bf16[4,32,1024]{2,1,0:T(8,128)(2,1)} %get-tuple-element.513), channel_id=1, source_target_pairs={{0,5},{1,4},{2,7},{3,6},{4,1},{5,0},{6,3},{7,2},{8,13},{9,12},{10,... | collective-permute-start | bytes 786440 | tf_op jit(solution)/shard_map/ppermute | solution.py:591
  16.0 18.1 %collective-permute-start.6 = (bf16[4,32,1024]{2,1,0:T(8,128)(2,1)}, bf16[4,32,1024]{2,1,0:T(8,128)(2,1)}, u32[]{:S(2)}, u32[]{:S(2)}) collective-permute-start(bf16[4,32,1024]{2,1,0:T(8,128)(2,1)} %get-tuple-element.511), channel_id=1, source_target_pairs={{0,7},{1,6},{2,5},{3,4},{4,3},{5,2},{6,1},{7,0},{8,15},{9,14},{10,... | collective-permute-start | bytes 786440 | tf_op jit(solution)/shard_map/ppermute | solution.py:591
  17.7 18.3 %collective-permute-start.8 = (bf16[4,32,1024]{2,1,0:T(8,128)(2,1)}, bf16[4,32,1024]{2,1,0:T(8,128)(2,1)}, u32[]{:S(2)}, u32[]{:S(2)}) collective-permute-start(bf16[4,32,1024]{2,1,0:T(8,128)(2,1)} %get-tuple-element.510), channel_id=1, source_target_pairs={{0,7},{1,6},{2,5},{3,4},{4,3},{5,2},{6,1},{7,0},{8,15},{9,14},{10,... | collective-permute-start | bytes 786440 | tf_op jit(solution)/shard_map/ppermute | solution.py:591
  19.9 17.4 %collective-permute-start.3 = (bf16[4,32,1024]{2,1,0:T(8,128)(2,1)}, bf16[4,32,1024]{2,1,0:T(8,128)(2,1)}, u32[]{:S(2)}, u32[]{:S(2)}) collective-permute-start(bf16[4,32,1024]{2,1,0:T(8,128)(2,1)} %get-tuple-element.517), channel_id=1, source_target_pairs={{0,1},{1,0},{2,3},{3,2},{4,5},{5,4},{6,7},{7,6},{8,9},{9,8},{10,11... | collective-permute-start | bytes 786440 | tf_op jit(solution)/shard_map/ppermute | solution.py:591
  21.4 20.8 %collective-permute-start.4 = (bf16[4,32,1024]{2,1,0:T(8,128)(2,1)}, bf16[4,32,1024]{2,1,0:T(8,128)(2,1)}, u32[]{:S(2)}, u32[]{:S(2)}) collective-permute-start(bf16[4,32,1024]{2,1,0:T(8,128)(2,1)} %get-tuple-element.515), channel_id=1, source_target_pairs={{0,3},{1,2},{2,1},{3,0},{4,7},{5,6},{6,5},{7,4},{8,11},{9,10},{10,... | collective-permute-start | bytes 786440 | tf_op jit(solution)/shard_map/ppermute | solution.py:591
  34.1 14.7 %collective-permute-start.1 = (bf16[4,32,1024]{2,1,0:T(8,128)(2,1)}, bf16[4,32,1024]{2,1,0:T(8,128)(2,1)}, u32[]{:S(2)}, u32[]{:S(2)}) collective-permute-start(bf16[4,32,1024]{2,1,0:T(8,128)(2,1)} %get-tuple-element.521), channel_id=1, source_target_pairs={{0,4},{1,5},{2,6},{3,7},{4,0},{5,1},{6,2},{7,3},{8,12},{9,13},{10,... | collective-permute-start | bytes 786440 | tf_op jit(solution)/shard_map/ppermute | solution.py:591
  50.0 27.1 %collective-permute-start.10 = (bf16[4,32,1024]{2,1,0:T(8,128)(2,1)}, bf16[4,32,1024]{2,1,0:T(8,128)(2,1)S(1)}, u32[]{:S(2)}, u32[]{:S(2)}) collective-permute-start(bf16[4,32,1024]{2,1,0:T(8,128)(2,1)} %get-tuple-element.259), channel_id=1, source_target_pairs={{0,4},{1,5},{2,6},{3,7},{4,0},{5,1},{6,2},{7,3},{8,12},{9,13},{10,... | collective-permute-start | bytes 786440 | tf_op jit(solution)/shard_map/ppermute | solution.py:591
  51.7 25.5 %collective-permute-start.11 = (bf16[4,32,1024]{2,1,0:T(8,128)(2,1)}, bf16[4,32,1024]{2,1,0:T(8,128)(2,1)}, u32[]{:S(2)}, u32[]{:S(2)}) collective-permute-start(bf16[4,32,1024]{2,1,0:T(8,128)(2,1)} %get-tuple-element.260), channel_id=1, source_target_pairs={{0,6},{1,7},{2,4},{3,5},{4,2},{5,3},{6,0},{7,1},{8,14},{9,15},{10,... | collective-permute-start | bytes 786440 | tf_op jit(solution)/shard_map/ppermute | solution.py:591
  53.1 24.1 %collective-permute-start.12 = (bf16[4,32,1024]{2,1,0:T(8,128)(2,1)S(1)}, bf16[4,32,1024]{2,1,0:T(8,128)(2,1)}, u32[]{:S(2)}, u32[]{:S(2)}) collective-permute-start(bf16[4,32,1024]{2,1,0:T(8,128)(2,1)S(1)} %get-tuple-element.262), channel_id=1, source_target_pairs={{0,3},{1,2},{2,1},{3,0},{4,7},{5,6},{6,5},{7,4},{8,11},{9,10},{10,... | collective-permute-start | bytes 786440 | tf_op jit(solution)/shard_map/ppermute | solution.py:591
  53.1 24.1 %collective-permute-start.13 = (bf16[4,32,1024]{2,1,0:T(8,128)(2,1)S(1)}, bf16[4,32,1024]{2,1,0:T(8,128)(2,1)}, u32[]{:S(2)}, u32[]{:S(2)}) collective-permute-start(bf16[4,32,1024]{2,1,0:T(8,128)(2,1)S(1)} %get-tuple-element.263), channel_id=1, source_target_pairs={{0,5},{1,4},{2,7},{3,6},{4,1},{5,0},{6,3},{7,2},{8,13},{9,12},{10,... | collective-permute-start | bytes 786440 | tf_op jit(solution)/shard_map/ppermute | solution.py:591
  54.9 22.3 %collective-permute-start.9 = (bf16[4,32,1024]{2,1,0:T(8,128)(2,1)}, bf16[4,32,1024]{2,1,0:T(8,128)(2,1)}, u32[]{:S(2)}, u32[]{:S(2)}) collective-permute-start(bf16[4,32,1024]{2,1,0:T(8,128)(2,1)} %get-tuple-element.258), channel_id=1, source_target_pairs={{0,2},{1,3},{2,0},{3,1},{4,6},{5,7},{6,4},{7,5},{8,10},{9,11},{10,... | collective-permute-start | bytes 786440 | tf_op jit(solution)/shard_map/ppermute | solution.py:591
  77.1 25.2 %collective-permute-start.14 = (bf16[4,2,128,1024]{3,2,1,0:T(8,128)(2,1)}, bf16[4,2,128,1024]{3,2,1,0:T(8,128)(2,1)}, u32[]{:S(2)}, u32[]{:S(2)}) collective-permute-start(bf16[4,2,128,1024]{3,2,1,0:T(8,128)(2,1)} %get-tuple-element.266), channel_id=1, source_target_pairs={{0,1},{1,0},{2,3},{3,2},{4,5},{5,4},{6,7},{7,6},{8,9},{9,8},{10,11... | collective-permute-start | bytes 6291464 | tf_op jit(solution)/shard_map/ppermute | solution.py:591
  98.8 50.2 %collective-permute-start.16 = (bf16[512,1024]{1,0:T(8,128)(2,1)S(1)}, bf16[512,1024]{1,0:T(8,128)(2,1)}, u32[]{:S(2)}, u32[]{:S(2)}) collective-permute-start(bf16[512,1024]{1,0:T(8,128)(2,1)S(1)} %bitcast.136), channel_id=1, source_target_pairs={{0,2},{1,3},{2,0},{3,1},{4,6},{5,7},{6,4},{7,5},{8,10},{9,11},{10,... | collective-permute-start | bytes 3145736 | tf_op jit(solution)/shard_map/ppermute | solution.py:591
  99.4 49.6 %collective-permute-start.17 = (bf16[512,1024]{1,0:T(8,128)(2,1)S(1)}, bf16[512,1024]{1,0:T(8,128)(2,1)}, u32[]{:S(2)}, u32[]{:S(2)}) collective-permute-start(bf16[512,1024]{1,0:T(8,128)(2,1)S(1)} %bitcast.135), channel_id=1, source_target_pairs={{0,4},{1,5},{2,6},{3,7},{4,0},{5,1},{6,2},{7,3},{8,12},{9,13},{10,... | collective-permute-start | bytes 3145736 | tf_op jit(solution)/shard_map/ppermute | solution.py:591
  99.7 49.3 %collective-permute-start.18 = (bf16[512,1024]{1,0:T(8,128)(2,1)S(1)}, bf16[512,1024]{1,0:T(8,128)(2,1)}, u32[]{:S(2)}, u32[]{:S(2)}) collective-permute-start(bf16[512,1024]{1,0:T(8,128)(2,1)S(1)} %bitcast.134), channel_id=1, source_target_pairs={{0,6},{1,7},{2,4},{3,5},{4,2},{5,3},{6,0},{7,1},{8,14},{9,15},{10,... | collective-permute-start | bytes 3145736 | tf_op jit(solution)/shard_map/ppermute | solution.py:591
  249.1 26.4 %collective-permute-start.19 = (bf16[512,1024]{1,0:T(8,128)(2,1)}, bf16[512,1024]{1,0:T(8,128)(2,1)S(1)}, u32[]{:S(2)}, u32[]{:S(2)}) collective-permute-start(bf16[512,1024]{1,0:T(8,128)(2,1)} %get-tuple-element.287), channel_id=1, source_target_pairs={{0,2},{1,3},{2,0},{3,1},{4,6},{5,7},{6,4},{7,5},{8,10},{9,11},{10,... | collective-permute-start | bytes 3145736 | tf_op jit(solution)/shard_map/ppermute | solution.py:591
  249.7 25.8 %collective-permute-start.20 = (bf16[512,1024]{1,0:T(8,128)(2,1)}, bf16[512,1024]{1,0:T(8,128)(2,1)S(1)}, u32[]{:S(2)}, u32[]{:S(2)}) collective-permute-start(bf16[512,1024]{1,0:T(8,128)(2,1)} %get-tuple-element.288), channel_id=1, source_target_pairs={{0,4},{1,5},{2,6},{3,7},{4,0},{5,1},{6,2},{7,3},{8,12},{9,13},{10,... | collective-permute-start | bytes 3145736 | tf_op jit(solution)/shard_map/ppermute | solution.py:591
  275.5 27.7 %collective-permute-start.21 = (bf16[16,64,2048]{2,1,0:T(8,128)(2,1)}, bf16[16,64,2048]{2,1,0:T(8,128)(2,1)}, u32[]{:S(2)}, u32[]{:S(2)}) collective-permute-start(bf16[16,64,2048]{2,1,0:T(8,128)(2,1)} %get-tuple-element.294), channel_id=1, source_target_pairs={{0,1},{1,0},{2,3},{3,2},{4,5},{5,4},{6,7},{7,6},{8,9},{9,8},{10,11... | collective-permute-start | bytes 12582920 | tf_op jit(solution)/shard_map/ppermute | solution.py:591
  275.6 27.6 %collective-permute-start.22 = (bf16[512,1024]{1,0:T(8,128)(2,1)}, bf16[512,1024]{1,0:T(8,128)(2,1)S(1)}, u32[]{:S(2)}, u32[]{:S(2)}) collective-permute-start(bf16[512,1024]{1,0:T(8,128)(2,1)} %get-tuple-element.298), channel_id=1, source_target_pairs={{0,6},{1,7},{2,4},{3,5},{4,2},{5,3},{6,0},{7,1},{8,14},{9,15},{10,... | collective-permute-start | bytes 3145736 | tf_op jit(solution)/shard_map/ppermute | solution.py:591
  303.2 54.8 %collective-permute-start.25 = (bf16[16,256,512]{2,1,0:T(8,128)(2,1)}, bf16[16,256,512]{2,1,0:T(8,128)(2,1)}, u32[]{:S(2)}, u32[]{:S(2)}) collective-permute-start(bf16[16,256,512]{2,1,0:T(8,128)(2,1)} %get-tuple-element.313), channel_id=1, source_target_pairs={{0,1},{1,0},{2,3},{3,2},{4,5},{5,4},{6,7},{7,6},{8,9},{9,8},{10,11... | collective-permute-start | bytes 12582920 | tf_op jit(solution)/shard_map/ppermute | solution.py:591
  306.7 51.3 %collective-permute-start.24 = (bf16[8,64,2048]{2,1,0:T(8,128)(2,1)}, bf16[8,64,2048]{2,1,0:T(8,128)(2,1)S(1)}, u32[]{:S(2)}, u32[]{:S(2)}) collective-permute-start(bf16[8,64,2048]{2,1,0:T(8,128)(2,1)} %slice_add_fusion), channel_id=1, source_target_pairs={{0,2},{1,3},{2,0},{3,1},{4,6},{5,7},{6,4},{7,5},{8,10},{9,11},{10,... | collective-permute-start | bytes 6291464 | tf_op jit(solution)/shard_map/ppermute | solution.py:591
  357.9 34.2 %collective-permute-start.23 = (bf16[8,128,1024]{2,1,0:T(8,128)(2,1)}, bf16[8,128,1024]{2,1,0:T(8,128)(2,1)}, u32[]{:S(2)}, u32[]{:S(2)}) collective-permute-start(bf16[8,128,1024]{2,1,0:T(8,128)(2,1)} %get-tuple-element.305), channel_id=1, source_target_pairs={{0,1},{1,0},{2,3},{3,2},{4,5},{5,4},{6,7},{7,6},{8,9},{9,8},{10,11... | collective-permute-start | bytes 6291464 | tf_op jit(solution)/shard_map/ppermute | solution.py:591
  392.1 190.0 %reduce-scatter.5.cloned.1.call-start = ((), (), s32[]{:S(2)}) async-start(), calls=%async_computation.3 | async-start | bytes 5242880 | tf_op jit(solution)/shard_map/reduce_scatter | solution.py:681
  392.2 37.1 %collective-permute-start.26 = (bf16[16,64,2048]{2,1,0:T(8,128)(2,1)}, bf16[16,64,2048]{2,1,0:T(8,128)(2,1)}, u32[]{:S(2)}, u32[]{:S(2)}) collective-permute-start(bf16[16,64,2048]{2,1,0:T(8,128)(2,1)} %get-tuple-element.340), channel_id=1, source_target_pairs={{0,1},{1,0},{2,3},{3,2},{4,5},{5,4},{6,7},{7,6},{8,9},{9,8},{10,11... | collective-permute-start | bytes 12582920 | tf_op jit(solution)/shard_map/ppermute | solution.py:591
  393.5 35.8 %collective-permute-start.27 = (bf16[4,64,2048]{2,1,0:T(8,128)(2,1)}, bf16[4,64,2048]{2,1,0:T(8,128)(2,1)S(1)}, u32[]{:S(2)}, u32[]{:S(2)}) collective-permute-start(bf16[4,64,2048]{2,1,0:T(8,128)(2,1)} %slice.264), channel_id=1, source_target_pairs={{0,4},{1,5},{2,6},{3,7},{4,0},{5,1},{6,2},{7,3},{8,12},{9,13},{10,... | collective-permute-start | bytes 3145736 | tf_op jit(solution)/shard_map/ppermute | solution.py:591
  430.2 41.2 %collective-permute-start.31 = (bf16[2,64,2048]{2,1,0:T(8,128)(2,1)}, bf16[2,64,2048]{2,1,0:T(8,128)(2,1)S(1)}, u32[]{:S(2)}, u32[]{:S(2)}) collective-permute-start(bf16[2,64,2048]{2,1,0:T(8,128)(2,1)} %get-tuple-element.495), channel_id=1, source_target_pairs={{0,8},{8,0},{16,24},{24,16},{1,9},{9,1},{17,25},{25,17},{2,10},{10... | collective-permute-start | bytes 1572872 | tf_op jit(solution)/shard_map/ppermute | solution.py:591
  431.8 39.7 %collective-permute-start.28 = (bf16[2,4,32,1024]{3,2,1,0:T(8,128)(2,1)}, bf16[2,4,32,1024]{3,2,1,0:T(8,128)(2,1)S(1)}, u32[]{:S(2)}, u32[]{:S(2)}) collective-permute-start(bf16[2,4,32,1024]{3,2,1,0:T(8,128)(2,1)} %get-tuple-element.347), channel_id=1, source_target_pairs={{0,2},{1,3},{2,0},{3,1},{4,6},{5,7},{6,4},{7,5},{8,10},{9,11},{10,... | collective-permute-start | bytes 1572872 | tf_op jit(solution)/shard_map/ppermute | solution.py:591
  431.8 39.7 %collective-permute-start.29 = (bf16[2,4,32,1024]{3,2,1,0:T(8,128)(2,1)}, bf16[2,4,32,1024]{3,2,1,0:T(8,128)(2,1)S(1)}, u32[]{:S(2)}, u32[]{:S(2)}) collective-permute-start(bf16[2,4,32,1024]{3,2,1,0:T(8,128)(2,1)} %get-tuple-element.348), channel_id=1, source_target_pairs={{0,4},{1,5},{2,6},{3,7},{4,0},{5,1},{6,2},{7,3},{8,12},{9,13},{10,... | collective-permute-start | bytes 1572872 | tf_op jit(solution)/shard_map/ppermute | solution.py:591
  432.8 38.7 %collective-permute-start.30 = (bf16[2,4,32,1024]{3,2,1,0:T(8,128)(2,1)}, bf16[2,4,32,1024]{3,2,1,0:T(8,128)(2,1)S(1)}, u32[]{:S(2)}, u32[]{:S(2)}) collective-permute-start(bf16[2,4,32,1024]{3,2,1,0:T(8,128)(2,1)} %get-tuple-element.349), channel_id=1, source_target_pairs={{0,6},{1,7},{2,4},{3,5},{4,2},{5,3},{6,0},{7,1},{8,14},{9,15},{10,... | collective-permute-start | bytes 1572872 | tf_op jit(solution)/shard_map/ppermute | solution.py:591
  474.0 36.4 %collective-permute-start.33 = (bf16[4,4,32,1024]{3,2,1,0:T(8,128)(2,1)}, bf16[4,4,32,1024]{3,2,1,0:T(8,128)(2,1)S(1)}, u32[]{:S(2)}, u32[]{:S(2)}) collective-permute-start(bf16[4,4,32,1024]{3,2,1,0:T(8,128)(2,1)} %pad_maximum_fusion.1), channel_id=1, source_target_pairs={{0,1},{1,0},{2,3},{3,2},{4,5},{5,4},{6,7},{7,6},{8,9},{9,8},{10,11... | collective-permute-start | bytes 3145736 | tf_op jit(solution)/shard_map/ppermute | solution.py:591
  474.1 35.6 %collective-permute-start.32 = (bf16[1,64,2048]{2,1,0:T(8,128)(2,1)S(1)}, bf16[1,64,2048]{2,1,0:T(8,128)(2,1)S(1)}, u32[]{:S(2)}, u32[]{:S(2)}) collective-permute-start(bf16[1,64,2048]{2,1,0:T(8,128)(2,1)S(1)} %get-tuple-element.508), channel_id=1, source_target_pairs={{0,16},{8,24},{16,0},{24,8},{1,17},{9,25},{17,1},{25,9},{2,18},{10... | collective-permute-start | bytes 786440 | tf_op jit(solution)/shard_map/ppermute | solution.py:591
  476.8 32.9 %collective-permute-start.34 = (bf16[2,4,32,1024]{3,2,1,0:T(8,128)(2,1)}, bf16[2,4,32,1024]{3,2,1,0:T(8,128)(2,1)S(1)}, u32[]{:S(2)}, u32[]{:S(2)}) collective-permute-start(bf16[2,4,32,1024]{3,2,1,0:T(8,128)(2,1)} %get-tuple-element.390), channel_id=1, source_target_pairs={{0,2},{1,3},{2,0},{3,1},{4,6},{5,7},{6,4},{7,5},{8,10},{9,11},{10,... | collective-permute-start | bytes 1572872 | tf_op jit(solution)/shard_map/ppermute | solution.py:591
  476.8 32.9 %collective-permute-start.35 = (bf16[2,4,32,1024]{3,2,1,0:T(8,128)(2,1)}, bf16[2,4,32,1024]{3,2,1,0:T(8,128)(2,1)S(1)}, u32[]{:S(2)}, u32[]{:S(2)}) collective-permute-start(bf16[2,4,32,1024]{3,2,1,0:T(8,128)(2,1)} %get-tuple-element.391), channel_id=1, source_target_pairs={{0,4},{1,5},{2,6},{3,7},{4,0},{5,1},{6,2},{7,3},{8,12},{9,13},{10,... | collective-permute-start | bytes 1572872 | tf_op jit(solution)/shard_map/ppermute | solution.py:591
  477.8 31.9 %collective-permute-start.36 = (bf16[2,4,32,1024]{3,2,1,0:T(8,128)(2,1)}, bf16[2,4,32,1024]{3,2,1,0:T(8,128)(2,1)S(1)}, u32[]{:S(2)}, u32[]{:S(2)}) collective-permute-start(bf16[2,4,32,1024]{3,2,1,0:T(8,128)(2,1)} %get-tuple-element.392), channel_id=1, source_target_pairs={{0,6},{1,7},{2,4},{3,5},{4,2},{5,3},{6,0},{7,1},{8,14},{9,15},{10,... | collective-permute-start | bytes 1572872 | tf_op jit(solution)/shard_map/ppermute | solution.py:591
  514.5 16.4 %collective-permute-start.44 = (bf16[4,4,32,1024]{3,2,1,0:T(8,128)(2,1)}, bf16[4,4,32,1024]{3,2,1,0:T(8,128)(2,1)S(1)}, u32[]{:S(2)}, u32[]{:S(2)}) collective-permute-start(bf16[4,4,32,1024]{3,2,1,0:T(8,128)(2,1)} %pad_maximum_fusion.2), channel_id=1, source_target_pairs={{0,1},{1,0},{2,3},{3,2},{4,5},{5,4},{6,7},{7,6},{8,9},{9,8},{10,11... | collective-permute-start | bytes 3145736 | tf_op jit(solution)/shard_map/ppermute | solution.py:591
  515.8 15.1 %collective-permute-start.43 = (bf16[2,256,512]{2,1,0:T(8,128)(2,1)}, bf16[2,256,512]{2,1,0:T(8,128)(2,1)}, u32[]{:S(2)}, u32[]{:S(2)}) collective-permute-start(bf16[2,256,512]{2,1,0:T(8,128)(2,1)} %get-tuple-element.506), channel_id=1, source_target_pairs={{0,2},{1,3},{2,0},{3,1},{4,6},{5,7},{6,4},{7,5},{8,10},{9,11},{10,... | collective-permute-start | bytes 1572872 | tf_op jit(solution)/shard_map/ppermute | solution.py:591
  523.8 32.1 %collective-permute-start.41 = (bf16[8,64,1024]{2,1,0:T(8,128)(2,1)}, bf16[8,64,1024]{2,1,0:T(8,128)(2,1)}, u32[]{:S(2)}, u32[]{:S(2)}) collective-permute-start(bf16[8,64,1024]{2,1,0:T(8,128)(2,1)} %slice_add_fusion.1), channel_id=1, source_target_pairs={{0,4},{1,5},{2,6},{3,7},{4,0},{5,1},{6,2},{7,3},{8,12},{9,13},{10,... | collective-permute-start | bytes 3145736 | tf_op jit(solution)/shard_map/ppermute | solution.py:591
  527.3 28.6 %collective-permute-start.40 = (bf16[8,64,1024]{2,1,0:T(8,128)(2,1)}, bf16[8,64,1024]{2,1,0:T(8,128)(2,1)}, u32[]{:S(2)}, u32[]{:S(2)}) collective-permute-start(bf16[8,64,1024]{2,1,0:T(8,128)(2,1)} %slice_add_fusion.2), channel_id=1, source_target_pairs={{0,2},{1,3},{2,0},{3,1},{4,6},{5,7},{6,4},{7,5},{8,10},{9,11},{10,... | collective-permute-start | bytes 3145736 | tf_op jit(solution)/shard_map/ppermute | solution.py:591
  530.0 25.9 %collective-permute-start.42 = (f32[36,1024]{1,0:T(8,128)S(1)}, f32[36,1024]{1,0:T(8,128)S(1)}, u32[]{:S(2)}, u32[]{:S(2)}) collective-permute-start(f32[36,1024]{1,0:T(8,128)S(1)} %add.472), channel_id=1, source_target_pairs={{0,2},{1,3},{2,0},{3,1},{4,6},{5,7},{6,4},{7,5},{8,10},{9,11},{10,... | collective-permute-start | bytes 442376 | tf_op jit(solution)/shard_map/ppermute | solution.py:591
  559.3 20.9 %collective-permute-start.47 = (bf16[4,64,1024]{2,1,0:T(8,128)(2,1)}, bf16[4,64,1024]{2,1,0:T(8,128)(2,1)}, u32[]{:S(2)}, u32[]{:S(2)}) collective-permute-start(bf16[4,64,1024]{2,1,0:T(8,128)(2,1)} %get-tuple-element.479), channel_id=1, source_target_pairs={{0,2},{1,3},{2,0},{3,1},{4,6},{5,7},{6,4},{7,5},{8,10},{9,11},{10,... | collective-permute-start | bytes 1572872 | tf_op jit(solution)/shard_map/ppermute | solution.py:591
  563.8 16.4 %collective-permute-start.46 = (bf16[4,64,1024]{2,1,0:T(8,128)(2,1)}, bf16[4,64,1024]{2,1,0:T(8,128)(2,1)S(1)}, u32[]{:S(2)}, u32[]{:S(2)}) collective-permute-start(bf16[4,64,1024]{2,1,0:T(8,128)(2,1)} %get-tuple-element.481), channel_id=1, source_target_pairs={{0,4},{1,5},{2,6},{3,7},{4,0},{5,1},{6,2},{7,3},{8,12},{9,13},{10,... | collective-permute-start | bytes 1572872 | tf_op jit(solution)/shard_map/ppermute | solution.py:591
  565.6 14.6 %collective-permute-start.48 = (f32[36,1024]{1,0:T(8,128)S(1)}, f32[36,1024]{1,0:T(8,128)S(1)}, u32[]{:S(2)}, u32[]{:S(2)}) collective-permute-start(f32[36,1024]{1,0:T(8,128)S(1)} %add.484), channel_id=1, source_target_pairs={{0,4},{1,5},{2,6},{3,7},{4,0},{5,1},{6,2},{7,3},{8,12},{9,13},{10,... | collective-permute-start | bytes 442376 | tf_op jit(solution)/shard_map/ppermute | solution.py:591
  583.5 22.8 %collective-permute-start.53 = (bf16[2,64,2048]{2,1,0:T(8,128)(2,1)S(1)}, bf16[2,64,2048]{2,1,0:T(8,128)(2,1)S(1)}, u32[]{:S(2)}, u32[]{:S(2)}) collective-permute-start(bf16[2,64,2048]{2,1,0:T(8,128)(2,1)S(1)} %get-tuple-element.501), channel_id=1, source_target_pairs={{0,4},{1,5},{2,6},{3,7},{4,0},{5,1},{6,2},{7,3},{8,12},{9,13},{10,... | collective-permute-start | bytes 1572872 | tf_op jit(solution)/shard_map/ppermute | solution.py:591
  585.0 21.2 %collective-permute-start.49 = (bf16[1,64,2048]{2,1,0:T(8,128)(2,1)S(1)}, bf16[1,64,2048]{2,1,0:T(8,128)(2,1)S(1)}, u32[]{:S(2)}, u32[]{:S(2)}) collective-permute-start(bf16[1,64,2048]{2,1,0:T(8,128)(2,1)S(1)} %get-tuple-element.504), channel_id=1, source_target_pairs={{0,8},{8,0},{16,24},{24,16},{1,9},{9,1},{17,25},{25,17},{2,10},{10... | collective-permute-start | bytes 786440 | tf_op jit(solution)/shard_map/ppermute | solution.py:591
  585.7 20.5 %collective-permute-start.50 = (bf16[1,64,2048]{2,1,0:T(8,128)(2,1)S(1)}, bf16[1,64,2048]{2,1,0:T(8,128)(2,1)S(1)}, u32[]{:S(2)}, u32[]{:S(2)}) collective-permute-start(bf16[1,64,2048]{2,1,0:T(8,128)(2,1)S(1)} %get-tuple-element.505), channel_id=1, source_target_pairs={{0,16},{8,24},{16,0},{24,8},{1,17},{9,25},{17,1},{25,9},{2,18},{10... | collective-permute-start | bytes 786440 | tf_op jit(solution)/shard_map/ppermute | solution.py:591
  585.7 20.5 %collective-permute-start.51 = (bf16[1,64,2048]{2,1,0:T(8,128)(2,1)S(1)}, bf16[1,64,2048]{2,1,0:T(8,128)(2,1)S(1)}, u32[]{:S(2)}, u32[]{:S(2)}) collective-permute-start(bf16[1,64,2048]{2,1,0:T(8,128)(2,1)S(1)} %get-tuple-element.503), channel_id=1, source_target_pairs={{0,24},{8,16},{16,8},{24,0},{1,25},{9,17},{17,9},{25,1},{2,26},{10... | collective-permute-start | bytes 786440 | tf_op jit(solution)/shard_map/ppermute | solution.py:591
  590.6 14.7 %collective-permute-start.52 = (f32[36,1024]{1,0:T(8,128)S(1)}, f32[36,1024]{1,0:T(8,128)S(1)}, u32[]{:S(2)}, u32[]{:S(2)}) collective-permute-start(f32[36,1024]{1,0:T(8,128)S(1)} %add.485), channel_id=1, source_target_pairs={{0,8},{8,0},{16,24},{24,16},{1,9},{9,1},{17,25},{25,17},{2,10},{10... | collective-permute-start | bytes 442376 | tf_op jit(solution)/shard_map/ppermute | solution.py:591
  (54 other events, 608.3 us)
Sparse Core Ops, SparseCore 0:
  392.2 88.9 reduce-scatter.2
  483.6 81.9 reduce-scatter.4

commit v3 on v2

--- a/solution.py
+++ b/solution.py
@@ -801,25 +801,43 @@
             )
         },
     )
-    ahead = [at for at, k in enumerate(order) if k in (1, n - 1)]
-    started = [swap(sources[1][at], order[at]) for at in ahead]
+    whole_at = [at for at, k in enumerate(order) if k in (0, 1, n - 1)]
+    sources = [
+        [blocks_of[at].transpose(1, 0, 2) if at in whole_at else part for at, part in enumerate(parts)]
+        for parts in sources
+    ]
     pieces = [send_out(sources[0])]
-    pieces[0], sources, cot_pieces, tables, started = hold_parts(
-        pieces[0], sources, cot_pieces, tables, started
-    )
+    pieces[0], sources, cot_pieces, tables = hold_parts(pieces[0], sources, cot_pieces, tables)
     for c in range(1, chunks):
-        came = dict(zip(ahead, started)) if c == 1 else {}
         pieces.append(
             [
-                came[at] if at in came else part if k == 0 else swap(part, k)
-                for at, (k, part) in enumerate(zip(order, sources[c]))
+                pieces[0][at] if at in whole_at else swap(part, order[at])
+                for at, part in enumerate(sources[c])
             ]
         )
     cot_pieces = [
         piece if j == 0 else swap(piece, j * group) for j, piece in enumerate(cot_pieces)
     ]
     if p % 16:
-        pieces = [[jnp.concatenate(parts, 1)] for parts in pieces]
+        pieces = [
+            [
+                jnp.concatenate(
+                    [
+                        part[c * span : (c + 1) * span] if at in whole_at else part
+                        for at, part in enumerate(parts)
+                    ],
+                    1,
+                )
+            ]
+            for c, parts in enumerate(pieces)
+        ]
+
+    def piece_blocks(c):
+        return [
+            (x, (1,) + x.shape[1:], lambda i, first=c * span * (x.shape[0] > span): (first + i, 0, 0))
+            for x in pieces[c]
+        ]
+
     kinds = len(pieces[0])
     act_time, act_space, own_hot = (tables[name] for name in ("act_time", "act_space", "own_hot"))
     perm, perm_back, bias = (tables[name] for name in ("perm", "perm_back", "bias"))
@@ -840,7 +858,7 @@
         packed, o1, total, *parts = call(
             lambda *refs: space_forward_kernel(group, kinds, *refs),
             (span,),
-            [(x, *frame_block(*x.shape[1:])) for x in pieces[c]]
+            piece_blocks(c)
             + [
                 (act_space, *chunk_block(c * span, 1, width)),
                 (vectors, None, None),
@@ -1008,7 +1026,7 @@
         return call(
             lambda *refs: space_back_kernel(kinds, group, order, *refs),
             (span,),
-            [(x, *frame_block(*x.shape[1:])) for x in pieces[c]]
+            piece_blocks(c)
             + [(r1, *chunk_block(c * span, places, width)) for r1 in r1_parts]
             + [
                 (act_space, *chunk_block(c * span, 1, width)),

time: 639 us -> 637 us (level)
    ppermute x60 -> x58, starting transfers between devices: 57.7 us -> 52.9 us  [swap(): return lax.ppermute(value, axis, [(i, i ^ k) for i in range(size)])]
    ppermute x60 -> x58, waiting for transfers between devices: 59.6 us -> 61.1 us  [swap(): return lax.ppermute(value, axis, [(i, i ^ k) for i in range(size)])]
  transfers between devices with their start and end apart: 62 -> 60, of which waited for: 8 -> 10; matrix products, arithmetic and copies ran while one was open for 8% -> 8% of each run, Pallas kernels for 53% -> 53%
where the time goes in v3:
time: 637 us; the launch traced here: 629 us
  Pallas kernels  432 us (68%)
  waiting for transfers between devices  61.2 us (10%)
  starting transfers between devices  53 us (8%)
  other arithmetic  34.7 us (5%)
  local copies, waits for them, and re-layouts  32 us (5%)
  between operations  15.7 us (2%)
    pallas_call x13, Pallas kernels, call(): pl.pallas_call(kernel, grid_spec=pltpu.PrefetchScalarGridSpec(num_scalar_...  432 us
    ppermute x58, waiting for transfers between devices, swap(): return lax.ppermute(value, axis, [(i, i ^ k) for i in range(size)])  61.1 us
    ppermute x58, starting transfers between devices, swap(): return lax.ppermute(value, axis, [(i, i ^ k) for i in range(size)])  52.9 us
  transfers between devices with their start and end apart: 60, of which 10 were waited for; matrix products, arithmetic and copies ran while one was open for 8% of the time, Pallas kernels for 53%

profile of v3, /device:TPU:0, one launch (start us, length us, event | category | flops | bytes accessed | tf_op | source)
XLA Modules:
  0.0 629.0 jit_solution(15251939474397517478)
XLA Ops:
  8.2 2.5 broadcast_select_fusion
  12.8 2.4 collective-permute-start.4
  16.0 1.8 collective-permute-start.5
  21.9 1.6 collective-permute-start.6
  27.9 4.2 constant_dynamic-slice_fusion.2
  32.1 1.5 collective-permute-start.2
  39.5 8.0 %collective-permute-done.1.refs_2_ = bf16[4,32,1024]{2,1,0:T(8,128)(2,1)} collective-permute-done((bf16[4,32,1024]{2,1,0:T(8,128)(2,1)}, bf16[4,32,1024]{2,1,0:T(8,128)(2,1)}, u32[]{:S(2)}, u32[]{:S(2)}) %collective-permute-start.1) | collective-permute-done | bytes 262176 | tf_op jit(solution)/shard_map/ppermute | solution.py:591
  49.4 1.6 collective-permute-start.7
  51.0 1.5 collective-permute-start.8
  52.9 20.7 %shard_map.212 = (bf16[4,256,3072]{2,1,0:T(8,128)(2,1)}, bf16[4,256,1024]{2,1,0:T(8,128)(2,1)}, f32[4,16,256]{2,1,0:T(8,128)}, bf16[4,2,128,1024]{3,2,1,0:T(8,128)(2,1)}, bf16[4,2,128,1024]{3,2,1,0:T(8,128)(2,1)}) custom-call(bf16[8,32,1024]{2,1,0:T(8,128)(2,1)} %bitcast.137, bf16[4,32,1024]{2,1,0:T(8,128)(2,1)} %collective-permute-done.refs_1_, ...), custom_call_target="tpu_custom_call" | custom-call | flops 15032385536 | bytes 18481152 | tf_op jit(solution)/shard_map/pallas_call | solution.py:355
  74.4 20.9 %shard_map.213 = (bf16[4,256,3072]{2,1,0:T(8,128)(2,1)}, bf16[4,256,1024]{2,1,0:T(8,128)(2,1)}, f32[4,16,256]{2,1,0:T(8,128)}, bf16[4,2,128,1024]{3,2,1,0:T(8,128)(2,1)}, bf16[4,2,128,1024]{3,2,1,0:T(8,128)(2,1)}) custom-call(bf16[8,32,1024]{2,1,0:T(8,128)(2,1)} %bitcast.138, bf16[4,32,1024]{2,1,0:T(8,128)(2,1)} %collective-permute-done.7.refs_1_, ...), custom_call_target="tpu_custom_call" | custom-call | flops 15032385536 | bytes 18481152 | tf_op jit(solution)/shard_map/pallas_call | solution.py:355
  95.9 1.6 collective-permute-start.14
  97.4 1.5 collective-permute-start.15
  100.0 45.7 %shard_map.214 = (f32[2048,1024]{1,0:T(8,128)}, f32[2048,1024]{1,0:T(8,128)}, bf16[2048,1024]{1,0:T(8,128)(2,1)}, bf16[2048,3072]{1,0:T(8,128)(2,1)}, bf16[2048,1024]{1,0:T(8,128)(2,1)}, /*index=5*/f32[16,2048]{1,0:T(8,128)}) custom-call(bf16[4,2,128,1024]{3,2,1,0:T(8,128)(2,1)} %get-tuple-element.253.refs_0_.refs_4_, ...), custom_call_target="tpu_custom_call" | custom-call | flops 30064771072 | bytes 55115776 | tf_op jit(solution)/shard_map/pallas_call | solution.py:355
  145.8 100.1 %shard_map.215 = (bf16[512,1024]{1,0:T(8,128)(2,1)}, bf16[512,1024]{1,0:T(8,128)(2,1)}, bf16[512,1024]{1,0:T(8,128)(2,1)}, bf16[512,1024]{1,0:T(8,128)(2,1)}, bf...) custom-call(f32[2048,1024]{1,0:T(8,128)} %get-tuple-element.265.refs, ...), custom_call_target="tpu_custom_call" | custom-call | flops 68719476736 | bytes 58818560 | tf_op jit(solution)/shard_map/pallas_call | solution.py:355
  245.9 1.7 collective-permute-start.17
  247.5 1.5 collective-permute-start.18
  249.0 25.4 %shard_map.216 = (bf16[16,64,2048]{2,1,0:T(8,128)(2,1)}, bf16[8,64,2048]{2,1,0:T(8,128)(2,1)}, bf16[8,64,2048]{2,1,0:T(8,128)(2,1)}) custom-call(s32[17]{0:T(128)} %concatenate.60.refs_0_, bf16[2048,1024]{1,0:T(8,128)(2,1)} %get-tuple-element.275.refs_1_, bf16[2048,4096]{1,0:T(8,128)(2,1)} %get-tuple-element.276.refs_2_), custom_call_target="tpu_custom_call" | custom-call | flops 17179869184 | bytes 41943040 | tf_op jit(solution)/shard_map/pallas_call | solution.py:355
  275.8 24.9 %shard_map.217 = (bf16[16,256,512]{2,1,0:T(8,128)(2,1)}, bf16[16,256,512]{2,1,0:T(8,128)(2,1)}) custom-call(s32[17]{0:T(128)} %concatenate.57.refs_0_, bf16[2048,4096]{1,0:T(8,128)(2,1)} %get-tuple-element.272.refs_1_.refs_2_, bf16[2048,4096]{1,0:T(8,128)(2,1)} %get-tuple-element.272.refs_1_.refs_2_, bf16[2048,1024]{1,0:T(8,128)(2,1)} %get-tuple-element.283.refs_3_), custom_call_target="tpu_custom_call" | custom-call | flops 17179869184 | bytes 75497472 | tf_op jit(solution)/shard_map/pallas_call | solution.py:355
  301.3 3.5 slice_add_fusion
  305.3 50.5 %shard_map.218 = (bf16[2048,3072]{1,0:T(8,128)(2,1)}, bf16[2048,1024]{1,0:T(8,128)(2,1)}, f32[8,1024]{1,0:T(8,128)}, bf16[8,128,1024]{2,1,0:T(8,128)(2,1)}, bf16[8,128,1024]{2,1,0:T(8,128)(2,1)}) custom-call(f32[2048,1024]{1,0:T(8,128)} %get-tuple-element.293.refs_0_, f32[2048,1024]{1,0:T(8,128)} %get-tuple-element.294.refs_1_, ...), custom_call_target="tpu_custom_call" | custom-call | flops 38654705664 | bytes 76218368 | tf_op jit(solution)/shard_map/pallas_call | solution.py:355
  356.0 1.3 copy-done.39
  357.3 30.5 %shard_map.219 = (bf16[16,64,2048]{2,1,0:T(8,128)(2,1)}, bf16[16,64,2048]{2,1,0:T(8,128)(2,1)}, bf16[16,256,512]{2,1,0:T(8,128)(2,1)}, bf16[8,64,2048]{2,1,0:T(8,128)(2,1)}) custom-call(s32[17]{0:T(128)} %concatenate.59.refs_0_, bf16[2048,1024]{1,0:T(8,128)(2,1)} %get-tuple-element.301.refs_1_, bf16[2048,3072]{1,0:T(8,128)(2,1)} %get-tuple-element.308.refs_2_, ...), custom_call_target="tpu_custom_call" | custom-call | flops 17179869184 | bytes 83886080 | tf_op jit(solution)/shard_map/pallas_call | solution.py:355
  387.8 2.4 slice.240
  393.4 33.6 %shard_map.220 = (bf16[4,256,3072]{2,1,0:T(8,128)(2,1)}, bf16[4,256,1024]{2,1,0:T(8,128)(2,1)}, bf16[4,256,1024]{2,1,0:T(8,128)(2,1)}, f32[16,1024]{1,0:T(8,128)...) custom-call(bf16[8,32,1024]{2,1,0:T(8,128)(2,1)} %bitcast.139, ...), custom_call_target="tpu_custom_call" | custom-call | flops 30064771072 | bytes 43909632 | tf_op jit(solution)/shard_map/pallas_call | solution.py:355
  427.9 1.6 collective-permute-start.29
  429.6 1.6 collective-permute-start.27
  431.2 1.8 collective-permute-start.28
  433.0 36.2 %shard_map.221 = (bf16[4,256,3072]{2,1,0:T(8,128)(2,1)}, bf16[4,256,1024]{2,1,0:T(8,128)(2,1)}, bf16[4,256,1024]{2,1,0:T(8,128)(2,1)}, f32[16,1024]{1,0:T(8,128)...) custom-call(bf16[8,32,1024]{2,1,0:T(8,128)(2,1)} %bitcast.140, ...), custom_call_target="tpu_custom_call" | custom-call | flops 30064771072 | bytes 60686848 | tf_op jit(solution)/shard_map/pallas_call | solution.py:355
  471.8 2.7 collective-permute-start.30
  474.7 1.6 collective-permute-start.33
  476.3 1.7 collective-permute-start.34
  478.0 29.2 %shard_map.222 = (bf16[16,64,1024]{2,1,0:T(8,128)(2,1)}, bf16[16,64,1024]{2,1,0:T(8,128)(2,1)}, bf16[8,64,1024]{2,1,0:T(8,128)(2,1)}, bf16[8,64,1024]{2,1,0:T(8,...) custom-call(s32[33]{0:T(128)} %concatenate.58.refs_0_, bf16[1024,1024]{1,0:T(8,128)(2,1)} %bitcast.147, ...), custom_call_target="tpu_custom_call" | custom-call | flops 17179869184 | bytes 50331648 | tf_op jit(solution)/shard_map/pallas_call | solution.py:355
  514.2 5.3 shard_map.223
  519.5 2.7 slice_add_fusion.1
  522.2 1.6 collective-permute-start.39
  523.8 2.6 slice_add_fusion.2
  528.4 1.5 collective-permute-start.40
  530.0 24.7 %collective-permute-done.40 = f32[36,1024]{1,0:T(8,128)S(1)} collective-permute-done((f32[36,1024]{1,0:T(8,128)S(1)}, f32[36,1024]{1,0:T(8,128)S(1)}, u32[]{:S(2)}, u32[]{:S(2)}) %collective-permute-start.40) | collective-permute-done | bytes 147488 | tf_op jit(solution)/shard_map/ppermute | solution.py:591
  554.7 3.3 add_convert_fusion
  558.7 3.3 add_convert_fusion.2
  565.0 9.1 %shard_map.224 = bf16[32,64,1024]{2,1,0:T(8,128)(2,1)} custom-call(s32[4]{0:T(128)} %iota_xor_fusion.meta.refs_0_, bf16[2,4,32,1024]{3,2,1,0:T(8,128)(2,1)} %get-tuple-element.433.refs_1_, bf16[2,4,32,1024]{3,2,1,0:T(8,128)(2,1)} %get-tuple-element.434.refs_2_, bf16[4,4,32,1024]{3,2,1,0:T(8,128)(2,1)} %copy-done.2, bf16[4,4,32,1024]{3,2,1,0:T(8,128)(2,1)} %copy-done.3, ...), custom_call_target="tpu_custom_call" | custom-call | bytes 25427968 | tf_op jit(solution)/shard_map/pallas_call | solution.py:355
  574.1 3.9 collective-permute-done.46
  579.9 1.3 fusion.20
  583.7 3.3 collective-permute-start.49
  588.5 14.6 %collective-permute-done.50 = f32[36,1024]{1,0:T(8,128)S(1)} collective-permute-done((f32[36,1024]{1,0:T(8,128)S(1)}, f32[36,1024]{1,0:T(8,128)S(1)}, u32[]{:S(2)}, u32[]{:S(2)}) %collective-permute-start.50) | collective-permute-done | bytes 147488 | tf_op jit(solution)/shard_map/ppermute | solution.py:591
  605.7 2.2 collective-permute-start.52
  609.4 7.0 %collective-permute-done.52 = f32[36,1024]{1,0:T(8,128)S(1)} collective-permute-done((f32[36,1024]{1,0:T(8,128)S(1)}, f32[36,1024]{1,0:T(8,128)S(1)}, u32[]{:S(2)}, u32[]{:S(2)}) %collective-permute-start.52) | collective-permute-done | bytes 147488 | tf_op jit(solution)/shard_map/ppermute | solution.py:591
  (278 shorter events, 59.5 us)
Async XLA Ops:
  7.2 500.8 %reduce-scatter.3.cloned.1.call-start = ((), (), s32[]{:S(2)}) async-start(), calls=%async_computation.2 | async-start | bytes 5242880 | tf_op jit(solution)/shard_map/reduce_scatter | solution.py:681
  12.8 19.4 %collective-permute-start.4 = (bf16[4,32,1024]{2,1,0:T(8,128)(2,1)}, bf16[4,32,1024]{2,1,0:T(8,128)(2,1)}, u32[]{:S(2)}, u32[]{:S(2)}) collective-permute-start(bf16[4,32,1024]{2,1,0:T(8,128)(2,1)} %get-tuple-element.507), channel_id=1, source_target_pairs={{0,3},{1,2},{2,1},{3,0},{4,7},{5,6},{6,5},{7,4},{8,11},{9,10},{10,... | collective-permute-start | bytes 786440 | tf_op jit(solution)/shard_map/ppermute | solution.py:591
  16.0 17.6 %collective-permute-start.5 = (bf16[4,32,1024]{2,1,0:T(8,128)(2,1)}, bf16[4,32,1024]{2,1,0:T(8,128)(2,1)}, u32[]{:S(2)}, u32[]{:S(2)}) collective-permute-start(bf16[4,32,1024]{2,1,0:T(8,128)(2,1)} %get-tuple-element.505), channel_id=1, source_target_pairs={{0,5},{1,4},{2,7},{3,6},{4,1},{5,0},{6,3},{7,2},{8,13},{9,12},{10,... | collective-permute-start | bytes 786440 | tf_op jit(solution)/shard_map/ppermute | solution.py:591
  19.2 28.2 %collective-permute-start.1 = (bf16[4,32,1024]{2,1,0:T(8,128)(2,1)}, bf16[4,32,1024]{2,1,0:T(8,128)(2,1)}, u32[]{:S(2)}, u32[]{:S(2)}) collective-permute-start(bf16[4,32,1024]{2,1,0:T(8,128)(2,1)} %get-tuple-element.511), channel_id=1, source_target_pairs={{0,4},{1,5},{2,6},{3,7},{4,0},{5,1},{6,2},{7,3},{8,12},{9,13},{10,... | collective-permute-start | bytes 786440 | tf_op jit(solution)/shard_map/ppermute | solution.py:591
  20.8 27.9 %collective-permute-start.3 = (bf16[8,32,1024]{2,1,0:T(8,128)(2,1)}, bf16[8,32,1024]{2,1,0:T(8,128)(2,1)}, u32[]{:S(2)}, u32[]{:S(2)}) collective-permute-start(bf16[8,32,1024]{2,1,0:T(8,128)(2,1)} %bitcast.122), channel_id=1, source_target_pairs={{0,1},{1,0},{2,3},{3,2},{4,5},{5,4},{6,7},{7,6},{8,9},{9,8},{10,11... | collective-permute-start | bytes 1572872 | tf_op jit(solution)/shard_map/ppermute | solution.py:591
  21.9 26.8 %collective-permute-start.6 = (bf16[8,32,1024]{2,1,0:T(8,128)(2,1)}, bf16[8,32,1024]{2,1,0:T(8,128)(2,1)}, u32[]{:S(2)}, u32[]{:S(2)}) collective-permute-start(bf16[8,32,1024]{2,1,0:T(8,128)(2,1)} %bitcast.121), channel_id=1, source_target_pairs={{0,7},{1,6},{2,5},{3,4},{4,3},{5,2},{6,1},{7,0},{8,15},{9,14},{10,... | collective-permute-start | bytes 1572872 | tf_op jit(solution)/shard_map/ppermute | solution.py:591
  32.1 15.4 %collective-permute-start.2 = (bf16[4,32,1024]{2,1,0:T(8,128)(2,1)S(1)}, bf16[4,32,1024]{2,1,0:T(8,128)(2,1)}, u32[]{:S(2)}, u32[]{:S(2)}) collective-permute-start(bf16[4,32,1024]{2,1,0:T(8,128)(2,1)S(1)} %copy-done.25), channel_id=1, source_target_pairs={{0,6},{1,7},{2,4},{3,5},{4,2},{5,3},{6,0},{7,1},{8,14},{9,15},{10,... | collective-permute-start | bytes 786440 | tf_op jit(solution)/shard_map/ppermute | solution.py:591
  33.6 15.1 %collective-permute-start = (bf16[4,32,1024]{2,1,0:T(8,128)(2,1)S(1)}, bf16[4,32,1024]{2,1,0:T(8,128)(2,1)}, u32[]{:S(2)}, u32[]{:S(2)}) collective-permute-start(bf16[4,32,1024]{2,1,0:T(8,128)(2,1)S(1)} %get-tuple-element.513), channel_id=1, source_target_pairs={{0,2},{1,3},{2,0},{3,1},{4,6},{5,7},{6,4},{7,5},{8,10},{9,11},{10,... | collective-permute-start | bytes 786440 | tf_op jit(solution)/shard_map/ppermute | solution.py:591
  48.7 24.9 %collective-permute-start.10 = (bf16[4,32,1024]{2,1,0:T(8,128)(2,1)S(1)}, bf16[4,32,1024]{2,1,0:T(8,128)(2,1)S(1)}, u32[]{:S(2)}, u32[]{:S(2)}) collective-permute-start(bf16[4,32,1024]{2,1,0:T(8,128)(2,1)S(1)} %get-tuple-element.257), channel_id=1, source_target_pairs={{0,3},{1,2},{2,1},{3,0},{4,7},{5,6},{6,5},{7,4},{8,11},{9,10},{10,... | collective-permute-start | bytes 786440 | tf_op jit(solution)/shard_map/ppermute | solution.py:591
  48.7 25.0 %collective-permute-start.11 = (bf16[4,32,1024]{2,1,0:T(8,128)(2,1)}, bf16[4,32,1024]{2,1,0:T(8,128)(2,1)S(1)}, u32[]{:S(2)}, u32[]{:S(2)}) collective-permute-start(bf16[4,32,1024]{2,1,0:T(8,128)(2,1)} %get-tuple-element.258), channel_id=1, source_target_pairs={{0,5},{1,4},{2,7},{3,6},{4,1},{5,0},{6,3},{7,2},{8,13},{9,12},{10,... | collective-permute-start | bytes 786440 | tf_op jit(solution)/shard_map/ppermute | solution.py:591
  49.4 24.3 %collective-permute-start.7 = (bf16[4,32,1024]{2,1,0:T(8,128)(2,1)}, bf16[4,32,1024]{2,1,0:T(8,128)(2,1)}, u32[]{:S(2)}, u32[]{:S(2)}) collective-permute-start(bf16[4,32,1024]{2,1,0:T(8,128)(2,1)} %get-tuple-element.254), channel_id=1, source_target_pairs={{0,2},{1,3},{2,0},{3,1},{4,6},{5,7},{6,4},{7,5},{8,10},{9,11},{10,... | collective-permute-start | bytes 786440 | tf_op jit(solution)/shard_map/ppermute | solution.py:591
  51.0 22.7 %collective-permute-start.8 = (bf16[4,32,1024]{2,1,0:T(8,128)(2,1)}, bf16[4,32,1024]{2,1,0:T(8,128)(2,1)}, u32[]{:S(2)}, u32[]{:S(2)}) collective-permute-start(bf16[4,32,1024]{2,1,0:T(8,128)(2,1)} %get-tuple-element.255), channel_id=1, source_target_pairs={{0,4},{1,5},{2,6},{3,7},{4,0},{5,1},{6,2},{7,3},{8,12},{9,13},{10,... | collective-permute-start | bytes 786440 | tf_op jit(solution)/shard_map/ppermute | solution.py:591
  52.5 21.2 %collective-permute-start.9 = (bf16[4,32,1024]{2,1,0:T(8,128)(2,1)}, bf16[4,32,1024]{2,1,0:T(8,128)(2,1)}, u32[]{:S(2)}, u32[]{:S(2)}) collective-permute-start(bf16[4,32,1024]{2,1,0:T(8,128)(2,1)} %get-tuple-element.256), channel_id=1, source_target_pairs={{0,6},{1,7},{2,4},{3,5},{4,2},{5,3},{6,0},{7,1},{8,14},{9,15},{10,... | collective-permute-start | bytes 786440 | tf_op jit(solution)/shard_map/ppermute | solution.py:591
  73.6 25.8 %collective-permute-start.12 = (bf16[4,2,128,1024]{3,2,1,0:T(8,128)(2,1)}, bf16[4,2,128,1024]{3,2,1,0:T(8,128)(2,1)}, u32[]{:S(2)}, u32[]{:S(2)}) collective-permute-start(bf16[4,2,128,1024]{3,2,1,0:T(8,128)(2,1)} %get-tuple-element.260), channel_id=1, source_target_pairs={{0,1},{1,0},{2,3},{3,2},{4,5},{5,4},{6,7},{7,6},{8,9},{9,8},{10,11... | collective-permute-start | bytes 6291464 | tf_op jit(solution)/shard_map/ppermute | solution.py:591
  95.9 49.9 %collective-permute-start.14 = (bf16[512,1024]{1,0:T(8,128)(2,1)S(1)}, bf16[512,1024]{1,0:T(8,128)(2,1)}, u32[]{:S(2)}, u32[]{:S(2)}) collective-permute-start(bf16[512,1024]{1,0:T(8,128)(2,1)S(1)} %bitcast.136), channel_id=1, source_target_pairs={{0,2},{1,3},{2,0},{3,1},{4,6},{5,7},{6,4},{7,5},{8,10},{9,11},{10,... | collective-permute-start | bytes 3145736 | tf_op jit(solution)/shard_map/ppermute | solution.py:591
  97.4 48.3 %collective-permute-start.15 = (bf16[512,1024]{1,0:T(8,128)(2,1)S(1)}, bf16[512,1024]{1,0:T(8,128)(2,1)}, u32[]{:S(2)}, u32[]{:S(2)}) collective-permute-start(bf16[512,1024]{1,0:T(8,128)(2,1)S(1)} %bitcast.135), channel_id=1, source_target_pairs={{0,4},{1,5},{2,6},{3,7},{4,0},{5,1},{6,2},{7,3},{8,12},{9,13},{10,... | collective-permute-start | bytes 3145736 | tf_op jit(solution)/shard_map/ppermute | solution.py:591
  99.0 46.8 %collective-permute-start.16 = (bf16[512,1024]{1,0:T(8,128)(2,1)S(1)}, bf16[512,1024]{1,0:T(8,128)(2,1)}, u32[]{:S(2)}, u32[]{:S(2)}) collective-permute-start(bf16[512,1024]{1,0:T(8,128)(2,1)S(1)} %bitcast.133), channel_id=1, source_target_pairs={{0,6},{1,7},{2,4},{3,5},{4,2},{5,3},{6,0},{7,1},{8,14},{9,15},{10,... | collective-permute-start | bytes 3145736 | tf_op jit(solution)/shard_map/ppermute | solution.py:591
  245.9 28.6 %collective-permute-start.17 = (bf16[512,1024]{1,0:T(8,128)(2,1)}, bf16[512,1024]{1,0:T(8,128)(2,1)S(1)}, u32[]{:S(2)}, u32[]{:S(2)}) collective-permute-start(bf16[512,1024]{1,0:T(8,128)(2,1)} %get-tuple-element.281), channel_id=1, source_target_pairs={{0,2},{1,3},{2,0},{3,1},{4,6},{5,7},{6,4},{7,5},{8,10},{9,11},{10,... | collective-permute-start | bytes 3145736 | tf_op jit(solution)/shard_map/ppermute | solution.py:591
  247.5 27.0 %collective-permute-start.18 = (bf16[512,1024]{1,0:T(8,128)(2,1)}, bf16[512,1024]{1,0:T(8,128)(2,1)S(1)}, u32[]{:S(2)}, u32[]{:S(2)}) collective-permute-start(bf16[512,1024]{1,0:T(8,128)(2,1)} %get-tuple-element.282), channel_id=1, source_target_pairs={{0,4},{1,5},{2,6},{3,7},{4,0},{5,1},{6,2},{7,3},{8,12},{9,13},{10,... | collective-permute-start | bytes 3145736 | tf_op jit(solution)/shard_map/ppermute | solution.py:591
  274.5 26.8 %collective-permute-start.19 = (bf16[16,64,2048]{2,1,0:T(8,128)(2,1)}, bf16[16,64,2048]{2,1,0:T(8,128)(2,1)}, u32[]{:S(2)}, u32[]{:S(2)}) collective-permute-start(bf16[16,64,2048]{2,1,0:T(8,128)(2,1)} %get-tuple-element.288), channel_id=1, source_target_pairs={{0,1},{1,0},{2,3},{3,2},{4,5},{5,4},{6,7},{7,6},{8,9},{9,8},{10,11... | collective-permute-start | bytes 12582920 | tf_op jit(solution)/shard_map/ppermute | solution.py:591
  274.6 26.7 %collective-permute-start.20 = (bf16[512,1024]{1,0:T(8,128)(2,1)}, bf16[512,1024]{1,0:T(8,128)(2,1)S(1)}, u32[]{:S(2)}, u32[]{:S(2)}) collective-permute-start(bf16[512,1024]{1,0:T(8,128)(2,1)} %get-tuple-element.292), channel_id=1, source_target_pairs={{0,6},{1,7},{2,4},{3,5},{4,2},{5,3},{6,0},{7,1},{8,14},{9,15},{10,... | collective-permute-start | bytes 3145736 | tf_op jit(solution)/shard_map/ppermute | solution.py:591
  301.3 54.7 %collective-permute-start.23 = (bf16[16,256,512]{2,1,0:T(8,128)(2,1)}, bf16[16,256,512]{2,1,0:T(8,128)(2,1)}, u32[]{:S(2)}, u32[]{:S(2)}) collective-permute-start(bf16[16,256,512]{2,1,0:T(8,128)(2,1)} %get-tuple-element.307), channel_id=1, source_target_pairs={{0,1},{1,0},{2,3},{3,2},{4,5},{5,4},{6,7},{7,6},{8,9},{9,8},{10,11... | collective-permute-start | bytes 12582920 | tf_op jit(solution)/shard_map/ppermute | solution.py:591
  304.8 51.1 %collective-permute-start.22 = (bf16[8,64,2048]{2,1,0:T(8,128)(2,1)}, bf16[8,64,2048]{2,1,0:T(8,128)(2,1)S(1)}, u32[]{:S(2)}, u32[]{:S(2)}) collective-permute-start(bf16[8,64,2048]{2,1,0:T(8,128)(2,1)} %slice_add_fusion), channel_id=1, source_target_pairs={{0,2},{1,3},{2,0},{3,1},{4,6},{5,7},{6,4},{7,5},{8,10},{9,11},{10,... | collective-permute-start | bytes 6291464 | tf_op jit(solution)/shard_map/ppermute | solution.py:591
  355.8 34.3 %collective-permute-start.21 = (bf16[8,128,1024]{2,1,0:T(8,128)(2,1)}, bf16[8,128,1024]{2,1,0:T(8,128)(2,1)}, u32[]{:S(2)}, u32[]{:S(2)}) collective-permute-start(bf16[8,128,1024]{2,1,0:T(8,128)(2,1)} %get-tuple-element.299), channel_id=1, source_target_pairs={{0,1},{1,0},{2,3},{3,2},{4,5},{5,4},{6,7},{7,6},{8,9},{9,8},{10,11... | collective-permute-start | bytes 6291464 | tf_op jit(solution)/shard_map/ppermute | solution.py:591
  390.2 189.8 %reduce-scatter.5.cloned.1.call-start = ((), (), s32[]{:S(2)}) async-start(), calls=%async_computation.3 | async-start | bytes 5242880 | tf_op jit(solution)/shard_map/reduce_scatter | solution.py:681
  390.2 36.8 %collective-permute-start.24 = (bf16[16,64,2048]{2,1,0:T(8,128)(2,1)}, bf16[16,64,2048]{2,1,0:T(8,128)(2,1)}, u32[]{:S(2)}, u32[]{:S(2)}) collective-permute-start(bf16[16,64,2048]{2,1,0:T(8,128)(2,1)} %get-tuple-element.334), channel_id=1, source_target_pairs={{0,1},{1,0},{2,3},{3,2},{4,5},{5,4},{6,7},{7,6},{8,9},{9,8},{10,11... | collective-permute-start | bytes 12582920 | tf_op jit(solution)/shard_map/ppermute | solution.py:591
  391.5 35.5 %collective-permute-start.25 = (bf16[4,64,2048]{2,1,0:T(8,128)(2,1)}, bf16[4,64,2048]{2,1,0:T(8,128)(2,1)S(1)}, u32[]{:S(2)}, u32[]{:S(2)}) collective-permute-start(bf16[4,64,2048]{2,1,0:T(8,128)(2,1)} %slice.240), channel_id=1, source_target_pairs={{0,4},{1,5},{2,6},{3,7},{4,0},{5,1},{6,2},{7,3},{8,12},{9,13},{10,... | collective-permute-start | bytes 3145736 | tf_op jit(solution)/shard_map/ppermute | solution.py:591
  427.9 41.2 %collective-permute-start.29 = (bf16[2,64,2048]{2,1,0:T(8,128)(2,1)}, bf16[2,64,2048]{2,1,0:T(8,128)(2,1)S(1)}, u32[]{:S(2)}, u32[]{:S(2)}) collective-permute-start(bf16[2,64,2048]{2,1,0:T(8,128)(2,1)} %get-tuple-element.489), channel_id=1, source_target_pairs={{0,8},{8,0},{16,24},{24,16},{1,9},{9,1},{17,25},{25,17},{2,10},{10... | collective-permute-start | bytes 1572872 | tf_op jit(solution)/shard_map/ppermute | solution.py:591
  429.5 39.7 %collective-permute-start.26 = (bf16[2,4,32,1024]{3,2,1,0:T(8,128)(2,1)}, bf16[2,4,32,1024]{3,2,1,0:T(8,128)(2,1)S(1)}, u32[]{:S(2)}, u32[]{:S(2)}) collective-permute-start(bf16[2,4,32,1024]{3,2,1,0:T(8,128)(2,1)} %get-tuple-element.341), channel_id=1, source_target_pairs={{0,2},{1,3},{2,0},{3,1},{4,6},{5,7},{6,4},{7,5},{8,10},{9,11},{10,... | collective-permute-start | bytes 1572872 | tf_op jit(solution)/shard_map/ppermute | solution.py:591
  429.6 39.6 %collective-permute-start.27 = (bf16[2,4,32,1024]{3,2,1,0:T(8,128)(2,1)}, bf16[2,4,32,1024]{3,2,1,0:T(8,128)(2,1)S(1)}, u32[]{:S(2)}, u32[]{:S(2)}) collective-permute-start(bf16[2,4,32,1024]{3,2,1,0:T(8,128)(2,1)} %get-tuple-element.342), channel_id=1, source_target_pairs={{0,4},{1,5},{2,6},{3,7},{4,0},{5,1},{6,2},{7,3},{8,12},{9,13},{10,... | collective-permute-start | bytes 1572872 | tf_op jit(solution)/shard_map/ppermute | solution.py:591
  431.2 38.0 %collective-permute-start.28 = (bf16[2,4,32,1024]{3,2,1,0:T(8,128)(2,1)}, bf16[2,4,32,1024]{3,2,1,0:T(8,128)(2,1)S(1)}, u32[]{:S(2)}, u32[]{:S(2)}) collective-permute-start(bf16[2,4,32,1024]{3,2,1,0:T(8,128)(2,1)} %get-tuple-element.343), channel_id=1, source_target_pairs={{0,6},{1,7},{2,4},{3,5},{4,2},{5,3},{6,0},{7,1},{8,14},{9,15},{10,... | collective-permute-start | bytes 1572872 | tf_op jit(solution)/shard_map/ppermute | solution.py:591
  471.7 36.3 %collective-permute-start.31 = (bf16[4,4,32,1024]{3,2,1,0:T(8,128)(2,1)}, bf16[4,4,32,1024]{3,2,1,0:T(8,128)(2,1)S(1)}, u32[]{:S(2)}, u32[]{:S(2)}) collective-permute-start(bf16[4,4,32,1024]{3,2,1,0:T(8,128)(2,1)} %pad_maximum_fusion.1), channel_id=1, source_target_pairs={{0,1},{1,0},{2,3},{3,2},{4,5},{5,4},{6,7},{7,6},{8,9},{9,8},{10,11... | collective-permute-start | bytes 3145736 | tf_op jit(solution)/shard_map/ppermute | solution.py:591
  471.8 35.5 %collective-permute-start.30 = (bf16[1,64,2048]{2,1,0:T(8,128)(2,1)S(1)}, bf16[1,64,2048]{2,1,0:T(8,128)(2,1)S(1)}, u32[]{:S(2)}, u32[]{:S(2)}) collective-permute-start(bf16[1,64,2048]{2,1,0:T(8,128)(2,1)S(1)} %get-tuple-element.502), channel_id=1, source_target_pairs={{0,16},{8,24},{16,0},{24,8},{1,17},{9,25},{17,1},{25,9},{2,18},{10... | collective-permute-start | bytes 786440 | tf_op jit(solution)/shard_map/ppermute | solution.py:591
  474.5 32.8 %collective-permute-start.32 = (bf16[2,4,32,1024]{3,2,1,0:T(8,128)(2,1)}, bf16[2,4,32,1024]{3,2,1,0:T(8,128)(2,1)S(1)}, u32[]{:S(2)}, u32[]{:S(2)}) collective-permute-start(bf16[2,4,32,1024]{3,2,1,0:T(8,128)(2,1)} %get-tuple-element.384), channel_id=1, source_target_pairs={{0,2},{1,3},{2,0},{3,1},{4,6},{5,7},{6,4},{7,5},{8,10},{9,11},{10,... | collective-permute-start | bytes 1572872 | tf_op jit(solution)/shard_map/ppermute | solution.py:591
  474.7 32.6 %collective-permute-start.33 = (bf16[2,4,32,1024]{3,2,1,0:T(8,128)(2,1)}, bf16[2,4,32,1024]{3,2,1,0:T(8,128)(2,1)S(1)}, u32[]{:S(2)}, u32[]{:S(2)}) collective-permute-start(bf16[2,4,32,1024]{3,2,1,0:T(8,128)(2,1)} %get-tuple-element.385), channel_id=1, source_target_pairs={{0,4},{1,5},{2,6},{3,7},{4,0},{5,1},{6,2},{7,3},{8,12},{9,13},{10,... | collective-permute-start | bytes 1572872 | tf_op jit(solution)/shard_map/ppermute | solution.py:591
  476.3 31.0 %collective-permute-start.34 = (bf16[2,4,32,1024]{3,2,1,0:T(8,128)(2,1)}, bf16[2,4,32,1024]{3,2,1,0:T(8,128)(2,1)S(1)}, u32[]{:S(2)}, u32[]{:S(2)}) collective-permute-start(bf16[2,4,32,1024]{3,2,1,0:T(8,128)(2,1)} %get-tuple-element.386), channel_id=1, source_target_pairs={{0,6},{1,7},{2,4},{3,5},{4,2},{5,3},{6,0},{7,1},{8,14},{9,15},{10,... | collective-permute-start | bytes 1572872 | tf_op jit(solution)/shard_map/ppermute | solution.py:591
  512.1 17.9 %collective-permute-start.42 = (bf16[4,4,32,1024]{3,2,1,0:T(8,128)(2,1)}, bf16[4,4,32,1024]{3,2,1,0:T(8,128)(2,1)S(1)}, u32[]{:S(2)}, u32[]{:S(2)}) collective-permute-start(bf16[4,4,32,1024]{3,2,1,0:T(8,128)(2,1)} %pad_maximum_fusion.2), channel_id=1, source_target_pairs={{0,1},{1,0},{2,3},{3,2},{4,5},{5,4},{6,7},{7,6},{8,9},{9,8},{10,11... | collective-permute-start | bytes 3145736 | tf_op jit(solution)/shard_map/ppermute | solution.py:591
  513.4 16.5 %collective-permute-start.41 = (bf16[2,256,512]{2,1,0:T(8,128)(2,1)}, bf16[2,256,512]{2,1,0:T(8,128)(2,1)}, u32[]{:S(2)}, u32[]{:S(2)}) collective-permute-start(bf16[2,256,512]{2,1,0:T(8,128)(2,1)} %get-tuple-element.500), channel_id=1, source_target_pairs={{0,2},{1,3},{2,0},{3,1},{4,6},{5,7},{6,4},{7,5},{8,10},{9,11},{10,... | collective-permute-start | bytes 1572872 | tf_op jit(solution)/shard_map/ppermute | solution.py:591
  522.2 32.5 %collective-permute-start.39 = (bf16[8,64,1024]{2,1,0:T(8,128)(2,1)}, bf16[8,64,1024]{2,1,0:T(8,128)(2,1)}, u32[]{:S(2)}, u32[]{:S(2)}) collective-permute-start(bf16[8,64,1024]{2,1,0:T(8,128)(2,1)} %slice_add_fusion.1), channel_id=1, source_target_pairs={{0,4},{1,5},{2,6},{3,7},{4,0},{5,1},{6,2},{7,3},{8,12},{9,13},{10,... | collective-permute-start | bytes 3145736 | tf_op jit(solution)/shard_map/ppermute | solution.py:591
  526.4 28.3 %collective-permute-start.38 = (bf16[8,64,1024]{2,1,0:T(8,128)(2,1)}, bf16[8,64,1024]{2,1,0:T(8,128)(2,1)}, u32[]{:S(2)}, u32[]{:S(2)}) collective-permute-start(bf16[8,64,1024]{2,1,0:T(8,128)(2,1)} %slice_add_fusion.2), channel_id=1, source_target_pairs={{0,2},{1,3},{2,0},{3,1},{4,6},{5,7},{6,4},{7,5},{8,10},{9,11},{10,... | collective-permute-start | bytes 3145736 | tf_op jit(solution)/shard_map/ppermute | solution.py:591
  528.4 26.3 %collective-permute-start.40 = (f32[36,1024]{1,0:T(8,128)S(1)}, f32[36,1024]{1,0:T(8,128)S(1)}, u32[]{:S(2)}, u32[]{:S(2)}) collective-permute-start(f32[36,1024]{1,0:T(8,128)S(1)} %add.472), channel_id=1, source_target_pairs={{0,2},{1,3},{2,0},{3,1},{4,6},{5,7},{6,4},{7,5},{8,10},{9,11},{10,... | collective-permute-start | bytes 442376 | tf_op jit(solution)/shard_map/ppermute | solution.py:591
  558.1 19.9 %collective-permute-start.45 = (bf16[4,64,1024]{2,1,0:T(8,128)(2,1)}, bf16[4,64,1024]{2,1,0:T(8,128)(2,1)}, u32[]{:S(2)}, u32[]{:S(2)}) collective-permute-start(bf16[4,64,1024]{2,1,0:T(8,128)(2,1)} %get-tuple-element.473), channel_id=1, source_target_pairs={{0,2},{1,3},{2,0},{3,1},{4,6},{5,7},{6,4},{7,5},{8,10},{9,11},{10,... | collective-permute-start | bytes 1572872 | tf_op jit(solution)/shard_map/ppermute | solution.py:591
  562.0 16.0 %collective-permute-start.44 = (bf16[4,64,1024]{2,1,0:T(8,128)(2,1)}, bf16[4,64,1024]{2,1,0:T(8,128)(2,1)S(1)}, u32[]{:S(2)}, u32[]{:S(2)}) collective-permute-start(bf16[4,64,1024]{2,1,0:T(8,128)(2,1)} %get-tuple-element.475), channel_id=1, source_target_pairs={{0,4},{1,5},{2,6},{3,7},{4,0},{5,1},{6,2},{7,3},{8,12},{9,13},{10,... | collective-permute-start | bytes 1572872 | tf_op jit(solution)/shard_map/ppermute | solution.py:591
  581.3 22.7 %collective-permute-start.51 = (bf16[2,64,2048]{2,1,0:T(8,128)(2,1)S(1)}, bf16[2,64,2048]{2,1,0:T(8,128)(2,1)S(1)}, u32[]{:S(2)}, u32[]{:S(2)}) collective-permute-start(bf16[2,64,2048]{2,1,0:T(8,128)(2,1)S(1)} %get-tuple-element.495), channel_id=1, source_target_pairs={{0,4},{1,5},{2,6},{3,7},{4,0},{5,1},{6,2},{7,3},{8,12},{9,13},{10,... | collective-permute-start | bytes 1572872 | tf_op jit(solution)/shard_map/ppermute | solution.py:591
  582.6 21.3 %collective-permute-start.47 = (bf16[1,64,2048]{2,1,0:T(8,128)(2,1)S(1)}, bf16[1,64,2048]{2,1,0:T(8,128)(2,1)S(1)}, u32[]{:S(2)}, u32[]{:S(2)}) collective-permute-start(bf16[1,64,2048]{2,1,0:T(8,128)(2,1)S(1)} %get-tuple-element.498), channel_id=1, source_target_pairs={{0,8},{8,0},{16,24},{24,16},{1,9},{9,1},{17,25},{25,17},{2,10},{10... | collective-permute-start | bytes 786440 | tf_op jit(solution)/shard_map/ppermute | solution.py:591
  583.7 20.2 %collective-permute-start.48 = (bf16[1,64,2048]{2,1,0:T(8,128)(2,1)S(1)}, bf16[1,64,2048]{2,1,0:T(8,128)(2,1)S(1)}, u32[]{:S(2)}, u32[]{:S(2)}) collective-permute-start(bf16[1,64,2048]{2,1,0:T(8,128)(2,1)S(1)} %get-tuple-element.499), channel_id=1, source_target_pairs={{0,16},{8,24},{16,0},{24,8},{1,17},{9,25},{17,1},{25,9},{2,18},{10... | collective-permute-start | bytes 786440 | tf_op jit(solution)/shard_map/ppermute | solution.py:591
  583.7 20.2 %collective-permute-start.49 = (bf16[1,64,2048]{2,1,0:T(8,128)(2,1)S(1)}, bf16[1,64,2048]{2,1,0:T(8,128)(2,1)S(1)}, u32[]{:S(2)}, u32[]{:S(2)}) collective-permute-start(bf16[1,64,2048]{2,1,0:T(8,128)(2,1)S(1)} %get-tuple-element.497), channel_id=1, source_target_pairs={{0,24},{8,16},{16,8},{24,0},{1,25},{9,17},{17,9},{25,1},{2,26},{10... | collective-permute-start | bytes 786440 | tf_op jit(solution)/shard_map/ppermute | solution.py:591
  588.2 14.9 %collective-permute-start.50 = (f32[36,1024]{1,0:T(8,128)S(1)}, f32[36,1024]{1,0:T(8,128)S(1)}, u32[]{:S(2)}, u32[]{:S(2)}) collective-permute-start(f32[36,1024]{1,0:T(8,128)S(1)} %add.485), channel_id=1, source_target_pairs={{0,8},{8,0},{16,24},{24,16},{1,9},{9,1},{17,25},{25,17},{2,10},{10... | collective-permute-start | bytes 442376 | tf_op jit(solution)/shard_map/ppermute | solution.py:591
  (54 other events, 596.1 us)
Sparse Core Ops, SparseCore 0:
  390.3 88.7 reduce-scatter.2
  481.5 81.5 reduce-scatter.4

commit v4 on v3

--- a/solution.py
+++ b/solution.py
@@ -163,7 +163,7 @@
     unit, _ = normalise(embedded)
     normed = (unit * vectors[0:1, :] + vectors[1:2, :]).astype(BF16)
     packed[0] = dot(normed, w_qkv[...]).astype(BF16)
-    attend_forward_rows(packed.at[0], slice(0, count), width, out.at[0], total.at[0], 4)
+    attend_forward_rows(packed.at[0], slice(0, count), width, out.at[0], total.at[0], 8)
     share = count // group
     for j in range(group):
         parts[j][0, 0] = raw[j * share : (j + 1) * share]
@@ -290,7 +290,7 @@
     count, width = raw.shape
     grad_out[...] = dot(r1, w_out[...], NT).astype(BF16)
     attend_back(
-        packed.at[0], slice(0, count), width, grad_out, total.at[0], None, grad_packed.at[0], 4
+        packed.at[0], slice(0, count), width, grad_out, total.at[0], None, grad_packed.at[0], 8
     )
     grad_normed = dot(grad_packed[0], w_qkv[...], NT)
     embedded, masked = embed(raw, vectors, act[0])

time: 637 us -> 637 us (level)
  no operation moved by 1% of the time
where the time goes in v4:
time: 637 us; the launch traced here: 630 us
  Pallas kernels  433 us (68%)
  waiting for transfers between devices  60.8 us (10%)
  starting transfers between devices  53.3 us (8%)
  other arithmetic  34.8 us (5%)
  local copies, waits for them, and re-layouts  32 us (5%)
  between operations  15.4 us (2%)
    pallas_call x13, Pallas kernels, call(): pl.pallas_call(kernel, grid_spec=pltpu.PrefetchScalarGridSpec(num_scalar_...  433 us
    ppermute x58, waiting for transfers between devices, swap(): return lax.ppermute(value, axis, [(i, i ^ k) for i in range(size)])  60.8 us
    ppermute x58, starting transfers between devices, swap(): return lax.ppermute(value, axis, [(i, i ^ k) for i in range(size)])  53.2 us
  transfers between devices with their start and end apart: 60, of which 10 were waited for; matrix products, arithmetic and copies ran while one was open for 8% of the time, Pallas kernels for 53%

profile of v4, /device:TPU:0, one launch (start us, length us, event | category | flops | bytes accessed | tf_op | source)
XLA Modules:
  0.0 629.7 jit_solution(17430542863434300241)
XLA Ops:
  8.2 2.5 broadcast_select_fusion
  12.8 2.4 collective-permute-start.4
  16.0 1.8 collective-permute-start.5
  21.9 1.6 collective-permute-start.6
  27.9 4.2 constant_dynamic-slice_fusion.2
  39.5 8.0 %collective-permute-done.1.refs_2_ = bf16[4,32,1024]{2,1,0:T(8,128)(2,1)} collective-permute-done((bf16[4,32,1024]{2,1,0:T(8,128)(2,1)}, bf16[4,32,1024]{2,1,0:T(8,128)(2,1)}, u32[]{:S(2)}, u32[]{:S(2)}) %collective-permute-start.1) | collective-permute-done | bytes 262176 | tf_op jit(solution)/shard_map/ppermute | solution.py:591
  49.4 1.6 collective-permute-start.7
  51.0 1.5 collective-permute-start.8
  52.9 20.7 %shard_map.212 = (bf16[4,256,3072]{2,1,0:T(8,128)(2,1)}, bf16[4,256,1024]{2,1,0:T(8,128)(2,1)}, f32[4,16,256]{2,1,0:T(8,128)}, bf16[4,2,128,1024]{3,2,1,0:T(8,128)(2,1)}, bf16[4,2,128,1024]{3,2,1,0:T(8,128)(2,1)}) custom-call(bf16[8,32,1024]{2,1,0:T(8,128)(2,1)} %bitcast.137, bf16[4,32,1024]{2,1,0:T(8,128)(2,1)} %collective-permute-done.refs_1_, ...), custom_call_target="tpu_custom_call" | custom-call | flops 15032385536 | bytes 18481152 | tf_op jit(solution)/shard_map/pallas_call | solution.py:355
  74.4 21.0 %shard_map.213 = (bf16[4,256,3072]{2,1,0:T(8,128)(2,1)}, bf16[4,256,1024]{2,1,0:T(8,128)(2,1)}, f32[4,16,256]{2,1,0:T(8,128)}, bf16[4,2,128,1024]{3,2,1,0:T(8,128)(2,1)}, bf16[4,2,128,1024]{3,2,1,0:T(8,128)(2,1)}) custom-call(bf16[8,32,1024]{2,1,0:T(8,128)(2,1)} %bitcast.138, bf16[4,32,1024]{2,1,0:T(8,128)(2,1)} %collective-permute-done.7.refs_1_, ...), custom_call_target="tpu_custom_call" | custom-call | flops 15032385536 | bytes 18481152 | tf_op jit(solution)/shard_map/pallas_call | solution.py:355
  96.0 1.6 collective-permute-start.14
  97.6 1.5 collective-permute-start.15
  100.2 45.7 %shard_map.214 = (f32[2048,1024]{1,0:T(8,128)}, f32[2048,1024]{1,0:T(8,128)}, bf16[2048,1024]{1,0:T(8,128)(2,1)}, bf16[2048,3072]{1,0:T(8,128)(2,1)}, bf16[2048,1024]{1,0:T(8,128)(2,1)}, /*index=5*/f32[16,2048]{1,0:T(8,128)}) custom-call(bf16[4,2,128,1024]{3,2,1,0:T(8,128)(2,1)} %get-tuple-element.253.refs_0_.refs_4_, ...), custom_call_target="tpu_custom_call" | custom-call | flops 30064771072 | bytes 55115776 | tf_op jit(solution)/shard_map/pallas_call | solution.py:355
  145.9 100.4 %shard_map.215 = (bf16[512,1024]{1,0:T(8,128)(2,1)}, bf16[512,1024]{1,0:T(8,128)(2,1)}, bf16[512,1024]{1,0:T(8,128)(2,1)}, bf16[512,1024]{1,0:T(8,128)(2,1)}, bf...) custom-call(f32[2048,1024]{1,0:T(8,128)} %get-tuple-element.265.refs, ...), custom_call_target="tpu_custom_call" | custom-call | flops 68719476736 | bytes 58818560 | tf_op jit(solution)/shard_map/pallas_call | solution.py:355
  246.3 1.7 collective-permute-start.17
  248.0 1.5 collective-permute-start.18
  249.5 25.2 %shard_map.216 = (bf16[16,64,2048]{2,1,0:T(8,128)(2,1)}, bf16[8,64,2048]{2,1,0:T(8,128)(2,1)}, bf16[8,64,2048]{2,1,0:T(8,128)(2,1)}) custom-call(s32[17]{0:T(128)} %concatenate.60.refs_0_, bf16[2048,1024]{1,0:T(8,128)(2,1)} %get-tuple-element.275.refs_1_, bf16[2048,4096]{1,0:T(8,128)(2,1)} %get-tuple-element.276.refs_2_), custom_call_target="tpu_custom_call" | custom-call | flops 17179869184 | bytes 41943040 | tf_op jit(solution)/shard_map/pallas_call | solution.py:355
  276.0 24.9 %shard_map.217 = (bf16[16,256,512]{2,1,0:T(8,128)(2,1)}, bf16[16,256,512]{2,1,0:T(8,128)(2,1)}) custom-call(s32[17]{0:T(128)} %concatenate.57.refs_0_, bf16[2048,4096]{1,0:T(8,128)(2,1)} %get-tuple-element.272.refs_1_.refs_2_, bf16[2048,4096]{1,0:T(8,128)(2,1)} %get-tuple-element.272.refs_1_.refs_2_, bf16[2048,1024]{1,0:T(8,128)(2,1)} %get-tuple-element.283.refs_3_), custom_call_target="tpu_custom_call" | custom-call | flops 17179869184 | bytes 75497472 | tf_op jit(solution)/shard_map/pallas_call | solution.py:355
  301.5 3.5 slice_add_fusion
  305.5 50.5 %shard_map.218 = (bf16[2048,3072]{1,0:T(8,128)(2,1)}, bf16[2048,1024]{1,0:T(8,128)(2,1)}, f32[8,1024]{1,0:T(8,128)}, bf16[8,128,1024]{2,1,0:T(8,128)(2,1)}, bf16[8,128,1024]{2,1,0:T(8,128)(2,1)}) custom-call(f32[2048,1024]{1,0:T(8,128)} %get-tuple-element.293.refs_0_, f32[2048,1024]{1,0:T(8,128)} %get-tuple-element.294.refs_1_, ...), custom_call_target="tpu_custom_call" | custom-call | flops 38654705664 | bytes 76218368 | tf_op jit(solution)/shard_map/pallas_call | solution.py:355
  357.5 30.5 %shard_map.219 = (bf16[16,64,2048]{2,1,0:T(8,128)(2,1)}, bf16[16,64,2048]{2,1,0:T(8,128)(2,1)}, bf16[16,256,512]{2,1,0:T(8,128)(2,1)}, bf16[8,64,2048]{2,1,0:T(8,128)(2,1)}) custom-call(s32[17]{0:T(128)} %concatenate.59.refs_0_, bf16[2048,1024]{1,0:T(8,128)(2,1)} %get-tuple-element.301.refs_1_, bf16[2048,3072]{1,0:T(8,128)(2,1)} %get-tuple-element.308.refs_2_, ...), custom_call_target="tpu_custom_call" | custom-call | flops 17179869184 | bytes 83886080 | tf_op jit(solution)/shard_map/pallas_call | solution.py:355
  388.0 2.4 slice.240
  393.6 34.0 %shard_map.220 = (bf16[4,256,3072]{2,1,0:T(8,128)(2,1)}, bf16[4,256,1024]{2,1,0:T(8,128)(2,1)}, bf16[4,256,1024]{2,1,0:T(8,128)(2,1)}, f32[16,1024]{1,0:T(8,128)...) custom-call(bf16[8,32,1024]{2,1,0:T(8,128)(2,1)} %bitcast.139, ...), custom_call_target="tpu_custom_call" | custom-call | flops 30064771072 | bytes 43909632 | tf_op jit(solution)/shard_map/pallas_call | solution.py:355
  428.5 1.5 collective-permute-start.29
  430.2 1.6 collective-permute-start.27
  431.8 1.8 collective-permute-start.28
  433.6 36.7 %shard_map.221 = (bf16[4,256,3072]{2,1,0:T(8,128)(2,1)}, bf16[4,256,1024]{2,1,0:T(8,128)(2,1)}, bf16[4,256,1024]{2,1,0:T(8,128)(2,1)}, f32[16,1024]{1,0:T(8,128)...) custom-call(bf16[8,32,1024]{2,1,0:T(8,128)(2,1)} %bitcast.140, ...), custom_call_target="tpu_custom_call" | custom-call | flops 30064771072 | bytes 60686848 | tf_op jit(solution)/shard_map/pallas_call | solution.py:355
  472.9 2.8 collective-permute-start.30
  475.9 1.6 collective-permute-start.33
  477.5 1.6 collective-permute-start.34
  479.2 29.1 %shard_map.222 = (bf16[16,64,1024]{2,1,0:T(8,128)(2,1)}, bf16[16,64,1024]{2,1,0:T(8,128)(2,1)}, bf16[8,64,1024]{2,1,0:T(8,128)(2,1)}, bf16[8,64,1024]{2,1,0:T(8,...) custom-call(s32[33]{0:T(128)} %concatenate.58.refs_0_, bf16[1024,1024]{1,0:T(8,128)(2,1)} %bitcast.147, ...), custom_call_target="tpu_custom_call" | custom-call | flops 17179869184 | bytes 50331648 | tf_op jit(solution)/shard_map/pallas_call | solution.py:355
  514.8 5.3 shard_map.223
  520.2 2.7 slice_add_fusion.1
  522.9 1.5 collective-permute-start.39
  524.4 2.6 slice_add_fusion.2
  529.0 1.6 collective-permute-start.40
  530.6 24.7 %collective-permute-done.40 = f32[36,1024]{1,0:T(8,128)S(1)} collective-permute-done((f32[36,1024]{1,0:T(8,128)S(1)}, f32[36,1024]{1,0:T(8,128)S(1)}, u32[]{:S(2)}, u32[]{:S(2)}) %collective-permute-start.40) | collective-permute-done | bytes 147488 | tf_op jit(solution)/shard_map/ppermute | solution.py:591
  555.4 3.4 add_convert_fusion
  559.2 3.3 add_convert_fusion.2
  562.6 1.7 collective-permute-start.44
  565.6 9.1 %shard_map.224 = bf16[32,64,1024]{2,1,0:T(8,128)(2,1)} custom-call(s32[4]{0:T(128)} %iota_xor_fusion.meta.refs_0_, bf16[2,4,32,1024]{3,2,1,0:T(8,128)(2,1)} %get-tuple-element.433.refs_1_, bf16[2,4,32,1024]{3,2,1,0:T(8,128)(2,1)} %get-tuple-element.434.refs_2_, bf16[4,4,32,1024]{3,2,1,0:T(8,128)(2,1)} %copy-done.2, bf16[4,4,32,1024]{3,2,1,0:T(8,128)(2,1)} %copy-done.3, ...), custom_call_target="tpu_custom_call" | custom-call | bytes 25427968 | tf_op jit(solution)/shard_map/pallas_call | solution.py:355
  574.6 3.9 collective-permute-done.46
  581.8 1.8 collective-permute-start.51
  584.6 3.5 collective-permute-start.49
  589.4 14.3 %collective-permute-done.50 = f32[36,1024]{1,0:T(8,128)S(1)} collective-permute-done((f32[36,1024]{1,0:T(8,128)S(1)}, f32[36,1024]{1,0:T(8,128)S(1)}, u32[]{:S(2)}, u32[]{:S(2)}) %collective-permute-start.50) | collective-permute-done | bytes 147488 | tf_op jit(solution)/shard_map/ppermute | solution.py:591
  604.5 1.7 collective-permute-start.53
  606.2 3.2 collective-permute-start.52
  610.8 6.6 %collective-permute-done.52 = f32[36,1024]{1,0:T(8,128)S(1)} collective-permute-done((f32[36,1024]{1,0:T(8,128)S(1)}, f32[36,1024]{1,0:T(8,128)S(1)}, u32[]{:S(2)}, u32[]{:S(2)}) %collective-permute-start.52) | collective-permute-done | bytes 147488 | tf_op jit(solution)/shard_map/ppermute | solution.py:591
  (278 shorter events, 58.1 us)
Async XLA Ops:
  7.2 501.8 %reduce-scatter.3.cloned.1.call-start = ((), (), s32[]{:S(2)}) async-start(), calls=%async_computation.2 | async-start | bytes 5242880 | tf_op jit(solution)/shard_map/reduce_scatter | solution.py:681
  12.8 19.4 %collective-permute-start.4 = (bf16[4,32,1024]{2,1,0:T(8,128)(2,1)}, bf16[4,32,1024]{2,1,0:T(8,128)(2,1)}, u32[]{:S(2)}, u32[]{:S(2)}) collective-permute-start(bf16[4,32,1024]{2,1,0:T(8,128)(2,1)} %get-tuple-element.507), channel_id=1, source_target_pairs={{0,3},{1,2},{2,1},{3,0},{4,7},{5,6},{6,5},{7,4},{8,11},{9,10},{10,... | collective-permute-start | bytes 786440 | tf_op jit(solution)/shard_map/ppermute | solution.py:591
  16.0 17.6 %collective-permute-start.5 = (bf16[4,32,1024]{2,1,0:T(8,128)(2,1)}, bf16[4,32,1024]{2,1,0:T(8,128)(2,1)}, u32[]{:S(2)}, u32[]{:S(2)}) collective-permute-start(bf16[4,32,1024]{2,1,0:T(8,128)(2,1)} %get-tuple-element.505), channel_id=1, source_target_pairs={{0,5},{1,4},{2,7},{3,6},{4,1},{5,0},{6,3},{7,2},{8,13},{9,12},{10,... | collective-permute-start | bytes 786440 | tf_op jit(solution)/shard_map/ppermute | solution.py:591
  19.2 28.2 %collective-permute-start.1 = (bf16[4,32,1024]{2,1,0:T(8,128)(2,1)}, bf16[4,32,1024]{2,1,0:T(8,128)(2,1)}, u32[]{:S(2)}, u32[]{:S(2)}) collective-permute-start(bf16[4,32,1024]{2,1,0:T(8,128)(2,1)} %get-tuple-element.511), channel_id=1, source_target_pairs={{0,4},{1,5},{2,6},{3,7},{4,0},{5,1},{6,2},{7,3},{8,12},{9,13},{10,... | collective-permute-start | bytes 786440 | tf_op jit(solution)/shard_map/ppermute | solution.py:591
  20.8 27.9 %collective-permute-start.3 = (bf16[8,32,1024]{2,1,0:T(8,128)(2,1)}, bf16[8,32,1024]{2,1,0:T(8,128)(2,1)}, u32[]{:S(2)}, u32[]{:S(2)}) collective-permute-start(bf16[8,32,1024]{2,1,0:T(8,128)(2,1)} %bitcast.122), channel_id=1, source_target_pairs={{0,1},{1,0},{2,3},{3,2},{4,5},{5,4},{6,7},{7,6},{8,9},{9,8},{10,11... | collective-permute-start | bytes 1572872 | tf_op jit(solution)/shard_map/ppermute | solution.py:591
  21.9 26.8 %collective-permute-start.6 = (bf16[8,32,1024]{2,1,0:T(8,128)(2,1)}, bf16[8,32,1024]{2,1,0:T(8,128)(2,1)}, u32[]{:S(2)}, u32[]{:S(2)}) collective-permute-start(bf16[8,32,1024]{2,1,0:T(8,128)(2,1)} %bitcast.121), channel_id=1, source_target_pairs={{0,7},{1,6},{2,5},{3,4},{4,3},{5,2},{6,1},{7,0},{8,15},{9,14},{10,... | collective-permute-start | bytes 1572872 | tf_op jit(solution)/shard_map/ppermute | solution.py:591
  32.1 15.4 %collective-permute-start.2 = (bf16[4,32,1024]{2,1,0:T(8,128)(2,1)S(1)}, bf16[4,32,1024]{2,1,0:T(8,128)(2,1)}, u32[]{:S(2)}, u32[]{:S(2)}) collective-permute-start(bf16[4,32,1024]{2,1,0:T(8,128)(2,1)S(1)} %copy-done.25), channel_id=1, source_target_pairs={{0,6},{1,7},{2,4},{3,5},{4,2},{5,3},{6,0},{7,1},{8,14},{9,15},{10,... | collective-permute-start | bytes 786440 | tf_op jit(solution)/shard_map/ppermute | solution.py:591
  33.6 15.1 %collective-permute-start = (bf16[4,32,1024]{2,1,0:T(8,128)(2,1)S(1)}, bf16[4,32,1024]{2,1,0:T(8,128)(2,1)}, u32[]{:S(2)}, u32[]{:S(2)}) collective-permute-start(bf16[4,32,1024]{2,1,0:T(8,128)(2,1)S(1)} %get-tuple-element.513), channel_id=1, source_target_pairs={{0,2},{1,3},{2,0},{3,1},{4,6},{5,7},{6,4},{7,5},{8,10},{9,11},{10,... | collective-permute-start | bytes 786440 | tf_op jit(solution)/shard_map/ppermute | solution.py:591
  48.7 24.9 %collective-permute-start.10 = (bf16[4,32,1024]{2,1,0:T(8,128)(2,1)S(1)}, bf16[4,32,1024]{2,1,0:T(8,128)(2,1)S(1)}, u32[]{:S(2)}, u32[]{:S(2)}) collective-permute-start(bf16[4,32,1024]{2,1,0:T(8,128)(2,1)S(1)} %get-tuple-element.257), channel_id=1, source_target_pairs={{0,3},{1,2},{2,1},{3,0},{4,7},{5,6},{6,5},{7,4},{8,11},{9,10},{10,... | collective-permute-start | bytes 786440 | tf_op jit(solution)/shard_map/ppermute | solution.py:591
  48.7 25.0 %collective-permute-start.11 = (bf16[4,32,1024]{2,1,0:T(8,128)(2,1)}, bf16[4,32,1024]{2,1,0:T(8,128)(2,1)S(1)}, u32[]{:S(2)}, u32[]{:S(2)}) collective-permute-start(bf16[4,32,1024]{2,1,0:T(8,128)(2,1)} %get-tuple-element.258), channel_id=1, source_target_pairs={{0,5},{1,4},{2,7},{3,6},{4,1},{5,0},{6,3},{7,2},{8,13},{9,12},{10,... | collective-permute-start | bytes 786440 | tf_op jit(solution)/shard_map/ppermute | solution.py:591
  49.4 24.3 %collective-permute-start.7 = (bf16[4,32,1024]{2,1,0:T(8,128)(2,1)}, bf16[4,32,1024]{2,1,0:T(8,128)(2,1)}, u32[]{:S(2)}, u32[]{:S(2)}) collective-permute-start(bf16[4,32,1024]{2,1,0:T(8,128)(2,1)} %get-tuple-element.254), channel_id=1, source_target_pairs={{0,2},{1,3},{2,0},{3,1},{4,6},{5,7},{6,4},{7,5},{8,10},{9,11},{10,... | collective-permute-start | bytes 786440 | tf_op jit(solution)/shard_map/ppermute | solution.py:591
  51.0 22.8 %collective-permute-start.8 = (bf16[4,32,1024]{2,1,0:T(8,128)(2,1)}, bf16[4,32,1024]{2,1,0:T(8,128)(2,1)}, u32[]{:S(2)}, u32[]{:S(2)}) collective-permute-start(bf16[4,32,1024]{2,1,0:T(8,128)(2,1)} %get-tuple-element.255), channel_id=1, source_target_pairs={{0,4},{1,5},{2,6},{3,7},{4,0},{5,1},{6,2},{7,3},{8,12},{9,13},{10,... | collective-permute-start | bytes 786440 | tf_op jit(solution)/shard_map/ppermute | solution.py:591
  52.5 21.3 %collective-permute-start.9 = (bf16[4,32,1024]{2,1,0:T(8,128)(2,1)}, bf16[4,32,1024]{2,1,0:T(8,128)(2,1)}, u32[]{:S(2)}, u32[]{:S(2)}) collective-permute-start(bf16[4,32,1024]{2,1,0:T(8,128)(2,1)} %get-tuple-element.256), channel_id=1, source_target_pairs={{0,6},{1,7},{2,4},{3,5},{4,2},{5,3},{6,0},{7,1},{8,14},{9,15},{10,... | collective-permute-start | bytes 786440 | tf_op jit(solution)/shard_map/ppermute | solution.py:591
  73.6 25.9 %collective-permute-start.12 = (bf16[4,2,128,1024]{3,2,1,0:T(8,128)(2,1)}, bf16[4,2,128,1024]{3,2,1,0:T(8,128)(2,1)}, u32[]{:S(2)}, u32[]{:S(2)}) collective-permute-start(bf16[4,2,128,1024]{3,2,1,0:T(8,128)(2,1)} %get-tuple-element.260), channel_id=1, source_target_pairs={{0,1},{1,0},{2,3},{3,2},{4,5},{5,4},{6,7},{7,6},{8,9},{9,8},{10,11... | collective-permute-start | bytes 6291464 | tf_op jit(solution)/shard_map/ppermute | solution.py:591
  96.0 49.9 %collective-permute-start.14 = (bf16[512,1024]{1,0:T(8,128)(2,1)S(1)}, bf16[512,1024]{1,0:T(8,128)(2,1)}, u32[]{:S(2)}, u32[]{:S(2)}) collective-permute-start(bf16[512,1024]{1,0:T(8,128)(2,1)S(1)} %bitcast.136), channel_id=1, source_target_pairs={{0,2},{1,3},{2,0},{3,1},{4,6},{5,7},{6,4},{7,5},{8,10},{9,11},{10,... | collective-permute-start | bytes 3145736 | tf_op jit(solution)/shard_map/ppermute | solution.py:591
  97.6 48.3 %collective-permute-start.15 = (bf16[512,1024]{1,0:T(8,128)(2,1)S(1)}, bf16[512,1024]{1,0:T(8,128)(2,1)}, u32[]{:S(2)}, u32[]{:S(2)}) collective-permute-start(bf16[512,1024]{1,0:T(8,128)(2,1)S(1)} %bitcast.135), channel_id=1, source_target_pairs={{0,4},{1,5},{2,6},{3,7},{4,0},{5,1},{6,2},{7,3},{8,12},{9,13},{10,... | collective-permute-start | bytes 3145736 | tf_op jit(solution)/shard_map/ppermute | solution.py:591
  99.1 46.8 %collective-permute-start.16 = (bf16[512,1024]{1,0:T(8,128)(2,1)S(1)}, bf16[512,1024]{1,0:T(8,128)(2,1)}, u32[]{:S(2)}, u32[]{:S(2)}) collective-permute-start(bf16[512,1024]{1,0:T(8,128)(2,1)S(1)} %bitcast.133), channel_id=1, source_target_pairs={{0,6},{1,7},{2,4},{3,5},{4,2},{5,3},{6,0},{7,1},{8,14},{9,15},{10,... | collective-permute-start | bytes 3145736 | tf_op jit(solution)/shard_map/ppermute | solution.py:591
  246.3 28.4 %collective-permute-start.17 = (bf16[512,1024]{1,0:T(8,128)(2,1)}, bf16[512,1024]{1,0:T(8,128)(2,1)S(1)}, u32[]{:S(2)}, u32[]{:S(2)}) collective-permute-start(bf16[512,1024]{1,0:T(8,128)(2,1)} %get-tuple-element.281), channel_id=1, source_target_pairs={{0,2},{1,3},{2,0},{3,1},{4,6},{5,7},{6,4},{7,5},{8,10},{9,11},{10,... | collective-permute-start | bytes 3145736 | tf_op jit(solution)/shard_map/ppermute | solution.py:591
  248.0 26.7 %collective-permute-start.18 = (bf16[512,1024]{1,0:T(8,128)(2,1)}, bf16[512,1024]{1,0:T(8,128)(2,1)S(1)}, u32[]{:S(2)}, u32[]{:S(2)}) collective-permute-start(bf16[512,1024]{1,0:T(8,128)(2,1)} %get-tuple-element.282), channel_id=1, source_target_pairs={{0,4},{1,5},{2,6},{3,7},{4,0},{5,1},{6,2},{7,3},{8,12},{9,13},{10,... | collective-permute-start | bytes 3145736 | tf_op jit(solution)/shard_map/ppermute | solution.py:591
  274.7 26.8 %collective-permute-start.19 = (bf16[16,64,2048]{2,1,0:T(8,128)(2,1)}, bf16[16,64,2048]{2,1,0:T(8,128)(2,1)}, u32[]{:S(2)}, u32[]{:S(2)}) collective-permute-start(bf16[16,64,2048]{2,1,0:T(8,128)(2,1)} %get-tuple-element.288), channel_id=1, source_target_pairs={{0,1},{1,0},{2,3},{3,2},{4,5},{5,4},{6,7},{7,6},{8,9},{9,8},{10,11... | collective-permute-start | bytes 12582920 | tf_op jit(solution)/shard_map/ppermute | solution.py:591
  274.8 26.7 %collective-permute-start.20 = (bf16[512,1024]{1,0:T(8,128)(2,1)}, bf16[512,1024]{1,0:T(8,128)(2,1)S(1)}, u32[]{:S(2)}, u32[]{:S(2)}) collective-permute-start(bf16[512,1024]{1,0:T(8,128)(2,1)} %get-tuple-element.292), channel_id=1, source_target_pairs={{0,6},{1,7},{2,4},{3,5},{4,2},{5,3},{6,0},{7,1},{8,14},{9,15},{10,... | collective-permute-start | bytes 3145736 | tf_op jit(solution)/shard_map/ppermute | solution.py:591
  301.5 54.7 %collective-permute-start.23 = (bf16[16,256,512]{2,1,0:T(8,128)(2,1)}, bf16[16,256,512]{2,1,0:T(8,128)(2,1)}, u32[]{:S(2)}, u32[]{:S(2)}) collective-permute-start(bf16[16,256,512]{2,1,0:T(8,128)(2,1)} %get-tuple-element.307), channel_id=1, source_target_pairs={{0,1},{1,0},{2,3},{3,2},{4,5},{5,4},{6,7},{7,6},{8,9},{9,8},{10,11... | collective-permute-start | bytes 12582920 | tf_op jit(solution)/shard_map/ppermute | solution.py:591
  305.0 51.1 %collective-permute-start.22 = (bf16[8,64,2048]{2,1,0:T(8,128)(2,1)}, bf16[8,64,2048]{2,1,0:T(8,128)(2,1)S(1)}, u32[]{:S(2)}, u32[]{:S(2)}) collective-permute-start(bf16[8,64,2048]{2,1,0:T(8,128)(2,1)} %slice_add_fusion), channel_id=1, source_target_pairs={{0,2},{1,3},{2,0},{3,1},{4,6},{5,7},{6,4},{7,5},{8,10},{9,11},{10,... | collective-permute-start | bytes 6291464 | tf_op jit(solution)/shard_map/ppermute | solution.py:591
  356.0 34.3 %collective-permute-start.21 = (bf16[8,128,1024]{2,1,0:T(8,128)(2,1)}, bf16[8,128,1024]{2,1,0:T(8,128)(2,1)}, u32[]{:S(2)}, u32[]{:S(2)}) collective-permute-start(bf16[8,128,1024]{2,1,0:T(8,128)(2,1)} %get-tuple-element.299), channel_id=1, source_target_pairs={{0,1},{1,0},{2,3},{3,2},{4,5},{5,4},{6,7},{7,6},{8,9},{9,8},{10,11... | collective-permute-start | bytes 6291464 | tf_op jit(solution)/shard_map/ppermute | solution.py:591
  390.4 190.1 %reduce-scatter.5.cloned.1.call-start = ((), (), s32[]{:S(2)}) async-start(), calls=%async_computation.3 | async-start | bytes 5242880 | tf_op jit(solution)/shard_map/reduce_scatter | solution.py:681
  390.4 37.2 %collective-permute-start.24 = (bf16[16,64,2048]{2,1,0:T(8,128)(2,1)}, bf16[16,64,2048]{2,1,0:T(8,128)(2,1)}, u32[]{:S(2)}, u32[]{:S(2)}) collective-permute-start(bf16[16,64,2048]{2,1,0:T(8,128)(2,1)} %get-tuple-element.334), channel_id=1, source_target_pairs={{0,1},{1,0},{2,3},{3,2},{4,5},{5,4},{6,7},{7,6},{8,9},{9,8},{10,11... | collective-permute-start | bytes 12582920 | tf_op jit(solution)/shard_map/ppermute | solution.py:591
  391.7 35.9 %collective-permute-start.25 = (bf16[4,64,2048]{2,1,0:T(8,128)(2,1)}, bf16[4,64,2048]{2,1,0:T(8,128)(2,1)S(1)}, u32[]{:S(2)}, u32[]{:S(2)}) collective-permute-start(bf16[4,64,2048]{2,1,0:T(8,128)(2,1)} %slice.240), channel_id=1, source_target_pairs={{0,4},{1,5},{2,6},{3,7},{4,0},{5,1},{6,2},{7,3},{8,12},{9,13},{10,... | collective-permute-start | bytes 3145736 | tf_op jit(solution)/shard_map/ppermute | solution.py:591
  428.5 41.7 %collective-permute-start.29 = (bf16[2,64,2048]{2,1,0:T(8,128)(2,1)}, bf16[2,64,2048]{2,1,0:T(8,128)(2,1)S(1)}, u32[]{:S(2)}, u32[]{:S(2)}) collective-permute-start(bf16[2,64,2048]{2,1,0:T(8,128)(2,1)} %get-tuple-element.489), channel_id=1, source_target_pairs={{0,8},{8,0},{16,24},{24,16},{1,9},{9,1},{17,25},{25,17},{2,10},{10... | collective-permute-start | bytes 1572872 | tf_op jit(solution)/shard_map/ppermute | solution.py:591
  430.1 40.2 %collective-permute-start.26 = (bf16[2,4,32,1024]{3,2,1,0:T(8,128)(2,1)}, bf16[2,4,32,1024]{3,2,1,0:T(8,128)(2,1)S(1)}, u32[]{:S(2)}, u32[]{:S(2)}) collective-permute-start(bf16[2,4,32,1024]{3,2,1,0:T(8,128)(2,1)} %get-tuple-element.341), channel_id=1, source_target_pairs={{0,2},{1,3},{2,0},{3,1},{4,6},{5,7},{6,4},{7,5},{8,10},{9,11},{10,... | collective-permute-start | bytes 1572872 | tf_op jit(solution)/shard_map/ppermute | solution.py:591
  430.2 40.1 %collective-permute-start.27 = (bf16[2,4,32,1024]{3,2,1,0:T(8,128)(2,1)}, bf16[2,4,32,1024]{3,2,1,0:T(8,128)(2,1)S(1)}, u32[]{:S(2)}, u32[]{:S(2)}) collective-permute-start(bf16[2,4,32,1024]{3,2,1,0:T(8,128)(2,1)} %get-tuple-element.342), channel_id=1, source_target_pairs={{0,4},{1,5},{2,6},{3,7},{4,0},{5,1},{6,2},{7,3},{8,12},{9,13},{10,... | collective-permute-start | bytes 1572872 | tf_op jit(solution)/shard_map/ppermute | solution.py:591
  431.8 38.5 %collective-permute-start.28 = (bf16[2,4,32,1024]{3,2,1,0:T(8,128)(2,1)}, bf16[2,4,32,1024]{3,2,1,0:T(8,128)(2,1)S(1)}, u32[]{:S(2)}, u32[]{:S(2)}) collective-permute-start(bf16[2,4,32,1024]{3,2,1,0:T(8,128)(2,1)} %get-tuple-element.343), channel_id=1, source_target_pairs={{0,6},{1,7},{2,4},{3,5},{4,2},{5,3},{6,0},{7,1},{8,14},{9,15},{10,... | collective-permute-start | bytes 1572872 | tf_op jit(solution)/shard_map/ppermute | solution.py:591
  472.8 36.2 %collective-permute-start.31 = (bf16[4,4,32,1024]{3,2,1,0:T(8,128)(2,1)}, bf16[4,4,32,1024]{3,2,1,0:T(8,128)(2,1)S(1)}, u32[]{:S(2)}, u32[]{:S(2)}) collective-permute-start(bf16[4,4,32,1024]{3,2,1,0:T(8,128)(2,1)} %pad_maximum_fusion.1), channel_id=1, source_target_pairs={{0,1},{1,0},{2,3},{3,2},{4,5},{5,4},{6,7},{7,6},{8,9},{9,8},{10,11... | collective-permute-start | bytes 3145736 | tf_op jit(solution)/shard_map/ppermute | solution.py:591
  472.9 35.4 %collective-permute-start.30 = (bf16[1,64,2048]{2,1,0:T(8,128)(2,1)S(1)}, bf16[1,64,2048]{2,1,0:T(8,128)(2,1)S(1)}, u32[]{:S(2)}, u32[]{:S(2)}) collective-permute-start(bf16[1,64,2048]{2,1,0:T(8,128)(2,1)S(1)} %get-tuple-element.502), channel_id=1, source_target_pairs={{0,16},{8,24},{16,0},{24,8},{1,17},{9,25},{17,1},{25,9},{2,18},{10... | collective-permute-start | bytes 786440 | tf_op jit(solution)/shard_map/ppermute | solution.py:591
  475.7 32.6 %collective-permute-start.32 = (bf16[2,4,32,1024]{3,2,1,0:T(8,128)(2,1)}, bf16[2,4,32,1024]{3,2,1,0:T(8,128)(2,1)S(1)}, u32[]{:S(2)}, u32[]{:S(2)}) collective-permute-start(bf16[2,4,32,1024]{3,2,1,0:T(8,128)(2,1)} %get-tuple-element.384), channel_id=1, source_target_pairs={{0,2},{1,3},{2,0},{3,1},{4,6},{5,7},{6,4},{7,5},{8,10},{9,11},{10,... | collective-permute-start | bytes 1572872 | tf_op jit(solution)/shard_map/ppermute | solution.py:591
  475.9 32.4 %collective-permute-start.33 = (bf16[2,4,32,1024]{3,2,1,0:T(8,128)(2,1)}, bf16[2,4,32,1024]{3,2,1,0:T(8,128)(2,1)S(1)}, u32[]{:S(2)}, u32[]{:S(2)}) collective-permute-start(bf16[2,4,32,1024]{3,2,1,0:T(8,128)(2,1)} %get-tuple-element.385), channel_id=1, source_target_pairs={{0,4},{1,5},{2,6},{3,7},{4,0},{5,1},{6,2},{7,3},{8,12},{9,13},{10,... | collective-permute-start | bytes 1572872 | tf_op jit(solution)/shard_map/ppermute | solution.py:591
  477.5 30.8 %collective-permute-start.34 = (bf16[2,4,32,1024]{3,2,1,0:T(8,128)(2,1)}, bf16[2,4,32,1024]{3,2,1,0:T(8,128)(2,1)S(1)}, u32[]{:S(2)}, u32[]{:S(2)}) collective-permute-start(bf16[2,4,32,1024]{3,2,1,0:T(8,128)(2,1)} %get-tuple-element.386), channel_id=1, source_target_pairs={{0,6},{1,7},{2,4},{3,5},{4,2},{5,3},{6,0},{7,1},{8,14},{9,15},{10,... | collective-permute-start | bytes 1572872 | tf_op jit(solution)/shard_map/ppermute | solution.py:591
  513.1 17.5 %collective-permute-start.42 = (bf16[4,4,32,1024]{3,2,1,0:T(8,128)(2,1)}, bf16[4,4,32,1024]{3,2,1,0:T(8,128)(2,1)S(1)}, u32[]{:S(2)}, u32[]{:S(2)}) collective-permute-start(bf16[4,4,32,1024]{3,2,1,0:T(8,128)(2,1)} %pad_maximum_fusion.2), channel_id=1, source_target_pairs={{0,1},{1,0},{2,3},{3,2},{4,5},{5,4},{6,7},{7,6},{8,9},{9,8},{10,11... | collective-permute-start | bytes 3145736 | tf_op jit(solution)/shard_map/ppermute | solution.py:591
  514.4 16.2 %collective-permute-start.41 = (bf16[2,256,512]{2,1,0:T(8,128)(2,1)}, bf16[2,256,512]{2,1,0:T(8,128)(2,1)}, u32[]{:S(2)}, u32[]{:S(2)}) collective-permute-start(bf16[2,256,512]{2,1,0:T(8,128)(2,1)} %get-tuple-element.500), channel_id=1, source_target_pairs={{0,2},{1,3},{2,0},{3,1},{4,6},{5,7},{6,4},{7,5},{8,10},{9,11},{10,... | collective-permute-start | bytes 1572872 | tf_op jit(solution)/shard_map/ppermute | solution.py:591
  522.9 32.5 %collective-permute-start.39 = (bf16[8,64,1024]{2,1,0:T(8,128)(2,1)}, bf16[8,64,1024]{2,1,0:T(8,128)(2,1)}, u32[]{:S(2)}, u32[]{:S(2)}) collective-permute-start(bf16[8,64,1024]{2,1,0:T(8,128)(2,1)} %slice_add_fusion.1), channel_id=1, source_target_pairs={{0,4},{1,5},{2,6},{3,7},{4,0},{5,1},{6,2},{7,3},{8,12},{9,13},{10,... | collective-permute-start | bytes 3145736 | tf_op jit(solution)/shard_map/ppermute | solution.py:591
  527.0 28.3 %collective-permute-start.38 = (bf16[8,64,1024]{2,1,0:T(8,128)(2,1)}, bf16[8,64,1024]{2,1,0:T(8,128)(2,1)}, u32[]{:S(2)}, u32[]{:S(2)}) collective-permute-start(bf16[8,64,1024]{2,1,0:T(8,128)(2,1)} %slice_add_fusion.2), channel_id=1, source_target_pairs={{0,2},{1,3},{2,0},{3,1},{4,6},{5,7},{6,4},{7,5},{8,10},{9,11},{10,... | collective-permute-start | bytes 3145736 | tf_op jit(solution)/shard_map/ppermute | solution.py:591
  529.0 26.3 %collective-permute-start.40 = (f32[36,1024]{1,0:T(8,128)S(1)}, f32[36,1024]{1,0:T(8,128)S(1)}, u32[]{:S(2)}, u32[]{:S(2)}) collective-permute-start(f32[36,1024]{1,0:T(8,128)S(1)} %add.472), channel_id=1, source_target_pairs={{0,2},{1,3},{2,0},{3,1},{4,6},{5,7},{6,4},{7,5},{8,10},{9,11},{10,... | collective-permute-start | bytes 442376 | tf_op jit(solution)/shard_map/ppermute | solution.py:591
  558.7 19.8 %collective-permute-start.45 = (bf16[4,64,1024]{2,1,0:T(8,128)(2,1)}, bf16[4,64,1024]{2,1,0:T(8,128)(2,1)}, u32[]{:S(2)}, u32[]{:S(2)}) collective-permute-start(bf16[4,64,1024]{2,1,0:T(8,128)(2,1)} %get-tuple-element.473), channel_id=1, source_target_pairs={{0,2},{1,3},{2,0},{3,1},{4,6},{5,7},{6,4},{7,5},{8,10},{9,11},{10,... | collective-permute-start | bytes 1572872 | tf_op jit(solution)/shard_map/ppermute | solution.py:591
  562.6 16.0 %collective-permute-start.44 = (bf16[4,64,1024]{2,1,0:T(8,128)(2,1)}, bf16[4,64,1024]{2,1,0:T(8,128)(2,1)S(1)}, u32[]{:S(2)}, u32[]{:S(2)}) collective-permute-start(bf16[4,64,1024]{2,1,0:T(8,128)(2,1)} %get-tuple-element.475), channel_id=1, source_target_pairs={{0,4},{1,5},{2,6},{3,7},{4,0},{5,1},{6,2},{7,3},{8,12},{9,13},{10,... | collective-permute-start | bytes 1572872 | tf_op jit(solution)/shard_map/ppermute | solution.py:591
  581.8 22.3 %collective-permute-start.51 = (bf16[2,64,2048]{2,1,0:T(8,128)(2,1)S(1)}, bf16[2,64,2048]{2,1,0:T(8,128)(2,1)S(1)}, u32[]{:S(2)}, u32[]{:S(2)}) collective-permute-start(bf16[2,64,2048]{2,1,0:T(8,128)(2,1)S(1)} %get-tuple-element.495), channel_id=1, source_target_pairs={{0,4},{1,5},{2,6},{3,7},{4,0},{5,1},{6,2},{7,3},{8,12},{9,13},{10,... | collective-permute-start | bytes 1572872 | tf_op jit(solution)/shard_map/ppermute | solution.py:591
  583.7 20.1 %collective-permute-start.47 = (bf16[1,64,2048]{2,1,0:T(8,128)(2,1)S(1)}, bf16[1,64,2048]{2,1,0:T(8,128)(2,1)S(1)}, u32[]{:S(2)}, u32[]{:S(2)}) collective-permute-start(bf16[1,64,2048]{2,1,0:T(8,128)(2,1)S(1)} %get-tuple-element.498), channel_id=1, source_target_pairs={{0,8},{8,0},{16,24},{24,16},{1,9},{9,1},{17,25},{25,17},{2,10},{10... | collective-permute-start | bytes 786440 | tf_op jit(solution)/shard_map/ppermute | solution.py:591
  584.1 20.0 %collective-permute-start.48 = (bf16[1,64,2048]{2,1,0:T(8,128)(2,1)S(1)}, bf16[1,64,2048]{2,1,0:T(8,128)(2,1)S(1)}, u32[]{:S(2)}, u32[]{:S(2)}) collective-permute-start(bf16[1,64,2048]{2,1,0:T(8,128)(2,1)S(1)} %get-tuple-element.499), channel_id=1, source_target_pairs={{0,16},{8,24},{16,0},{24,8},{1,17},{9,25},{17,1},{25,9},{2,18},{10... | collective-permute-start | bytes 786440 | tf_op jit(solution)/shard_map/ppermute | solution.py:591
  584.6 19.4 %collective-permute-start.49 = (bf16[1,64,2048]{2,1,0:T(8,128)(2,1)S(1)}, bf16[1,64,2048]{2,1,0:T(8,128)(2,1)S(1)}, u32[]{:S(2)}, u32[]{:S(2)}) collective-permute-start(bf16[1,64,2048]{2,1,0:T(8,128)(2,1)S(1)} %get-tuple-element.497), channel_id=1, source_target_pairs={{0,24},{8,16},{16,8},{24,0},{1,25},{9,17},{17,9},{25,1},{2,26},{10... | collective-permute-start | bytes 786440 | tf_op jit(solution)/shard_map/ppermute | solution.py:591
  589.2 14.5 %collective-permute-start.50 = (f32[36,1024]{1,0:T(8,128)S(1)}, f32[36,1024]{1,0:T(8,128)S(1)}, u32[]{:S(2)}, u32[]{:S(2)}) collective-permute-start(f32[36,1024]{1,0:T(8,128)S(1)} %add.485), channel_id=1, source_target_pairs={{0,8},{8,0},{16,24},{24,16},{1,9},{9,1},{17,25},{25,17},{2,10},{10... | collective-permute-start | bytes 442376 | tf_op jit(solution)/shard_map/ppermute | solution.py:591
  (54 other events, 597.9 us)
Sparse Core Ops, SparseCore 0:
  390.5 89.0 reduce-scatter.2
  482.0 80.4 reduce-scatter.4
